TPU v7x, 256 devices: a whole 4x4x8 slice. The times are simulated.
256 devices in a mesh: lat: 32 (over z, y_hi, core), lon: 8 (over y_lo, x).
Axes of the slice: x: 4, y: 4 (y_hi: 2, y_lo: 2; y = y_hi * 2 + y_lo), z: 8, core: 2. Of those that a mesh axis runs over, the one named last changes fastest.
Arguments:
- u_wind: float32 [24, 1024, 3072], P(None, 'lat', 'lon'), may hold values from -4 to 4
- v_wind: float32 [24, 1024, 3072], P(None, 'lat', 'lon'), may hold values from -4 to 4
- thickness: float32 [24, 1024, 3072], P(None, 'lat', 'lon'), may hold values from 0.5 to 1.5
- theta: float32 [24, 1024, 3072], P(None, 'lat', 'lon'), may hold values from 0.5 to 1.5
- polar_rows: int32 [32, 16], replicated, may hold values from 0 to 1023, as said below
- cutoffs: int32 [1024], replicated, may hold values from 1 to 768, as said below
Outputs:
- u_next: float32 [24, 1024, 3072], P(None, 'lat', 'lon')
- v_next: float32 [24, 1024, 3072], P(None, 'lat', 'lon')
- thickness_next: float32 [24, 1024, 3072], P(None, 'lat', 'lon')
- heat_next: float32 [24, 1024, 3072], P(None, 'lat', 'lon')
Inputs may be any that keep to these rules, and one draw needn't show every extreme that they name: `polar_rows`: each helper lists exactly 16 distinct rows, no row is listed twice, and no helper lists more than 1 row of one index of lat. The listed rows are all rows below a southern edge s and all rows from 1024 - (512 - s) up, with s within 16 of 256. `cutoffs`: the cutoff of row j lies between half of and all of (2 d + 1) * 3072 // 4096 + 1, d = min(j, 1023 - j).
All inputs are finite; a program needn't handle non-finite values.
Results may differ from a plain program's by a relative error of at most 0.0002.
Values sent between devices are 32-bit elements; how exact they have to be, the bound alone decides.
No kernel may reach another device: no remote copies, remote signals or barrier semaphores. Data moves between devices by JAX's collectives and lax.ppermute only.
A program may use at most 128 MiB of HBM per device.

v0:
```python
import math

import jax
import jax.numpy as jnp
from jax import lax
from jax.sharding import PartitionSpec as P

KMAX = 512


OMEGA = 30.0


def extended(block, sides, width, periodic):
    for axis, dim in sides:
        count = lax.axis_size(axis)
        forward = [(i, i + 1) for i in range(count - 1)]
        if periodic:
            forward.append((count - 1, 0))
        backward = [(target, source) for source, target in forward]
        low = lax.ppermute(
            lax.slice_in_dim(block, block.shape[dim] - width, None, axis=dim), axis, forward
        )
        high = lax.ppermute(lax.slice_in_dim(block, 0, width, axis=dim), axis, backward)
        block = jnp.concatenate([low, block, high], axis=dim)
    return block


def passed_along(value, axis, steps):
    count = lax.axis_size(axis)
    pairs = [(source, (source + steps) % count) for source in range(count)]
    return lax.ppermute(value, axis, pairs)


def row_cos(index, total):
    dist = jnp.maximum(jnp.minimum(index, total - 1 - index), 0)
    return jnp.sin(math.pi * (dist.astype(jnp.float32) + 0.5) / total)


def face_cos(face, total):
    dist = jnp.minimum(face, total - face)
    return jnp.sin(math.pi * dist.astype(jnp.float32) / total)


def spin_rate(index, total):
    return -2.0 * OMEGA * jnp.cos(math.pi * (index.astype(jnp.float32) + 0.5) / total)


def tendencies(xpad, ypad, cos_ext, cos_faces, coriolis, dlon, dlat):
    ux, vx, px, hx = (xpad[0], xpad[1], xpad[2], xpad[3])
    uy, vy, py, hy = (ypad[0], ypad[1], ypad[2], ypad[3])
    cos_mid = cos_ext[1:-1][:, None]
    heat_xp = px * hx
    heat_yp = py * hy
    east = 0.5 * (ux[..., :-1] + ux[..., 1:])
    mass_x = jnp.maximum(east, 0.0) * px[..., :-1] + jnp.minimum(east, 0.0) * px[..., 1:]
    heat_x = jnp.maximum(east, 0.0) * heat_xp[..., :-1] + jnp.minimum(east, 0.0) * heat_xp[..., 1:]
    north = 0.5 * (vy[..., :-1, :] + vy[..., 1:, :])
    faces = cos_faces[:, None]
    mass_y = faces * (
        jnp.maximum(north, 0.0) * py[..., :-1, :] + jnp.minimum(north, 0.0) * py[..., 1:, :]
    )
    heat_y = faces * (
        jnp.maximum(north, 0.0) * heat_yp[..., :-1, :]
        + jnp.minimum(north, 0.0) * heat_yp[..., 1:, :]
    )
    mass_t = (
        -(
            (mass_x[..., 1:] - mass_x[..., :-1]) / dlon
            + (mass_y[..., 1:, :] - mass_y[..., :-1, :]) / dlat
        )
        / cos_mid
    )
    heat_t = (
        -(
            (heat_x[..., 1:] - heat_x[..., :-1]) / dlon
            + (heat_y[..., 1:, :] - heat_y[..., :-1, :]) / dlat
        )
        / cos_mid
    )
    energy_x = 0.5 * (ux * ux + vx * vx) + heat_xp
    energy_y = 0.5 * (uy * uy + vy * vy) + heat_yp
    weighted = uy * cos_ext[:, None]
    spin = (
        (vx[..., 2:] - vx[..., :-2]) / (2.0 * dlon)
        - (weighted[..., 2:, :] - weighted[..., :-2, :]) / (2.0 * dlat)
    ) / cos_mid
    absolute = coriolis[:, None] + spin
    u_mid = ux[..., 1:-1]
    v_mid = vx[..., 1:-1]
    u_t = absolute * v_mid - (energy_x[..., 2:] - energy_x[..., :-2]) / (2.0 * dlon * cos_mid)
    v_t = -absolute * u_mid - (energy_y[..., 2:, :] - energy_y[..., :-2, :]) / (2.0 * dlat)
    return jnp.stack([u_t, v_t, mass_t, heat_t])


def fourier_table(start, count, total):
    column = start + jnp.arange(count)
    phase = column[:, None] * jnp.arange(KMAX)[None, :] % total
    angle = phase.astype(jnp.float32) * (2.0 * math.pi / total)
    return jnp.concatenate([jnp.cos(angle), jnp.sin(angle)], axis=1)


def per_device(u_wind, v_wind, thickness, theta, polar_rows, cutoffs):
    levels, rows, cols = u_wind.shape
    lat_count = lax.axis_size("lat")
    lon_count = lax.axis_size("lon")
    lat_place = lax.axis_index("lat")
    lon_place = lax.axis_index("lon")
    total_rows = rows * lat_count
    total_cols = cols * lon_count
    dlon = 2.0 * math.pi / total_cols
    dlat = math.pi / total_rows
    step_size = 0.25 * dlon
    highest = lax.Precision.HIGHEST
    fields = jnp.stack([u_wind, v_wind, thickness, theta])
    lat_padded = extended(fields, (("lat", 2),), 1, False)
    edges = jnp.stack([fields[:, :, 0, :], fields[:, :, rows - 1, :]], axis=2)
    opposite = passed_along(edges, "lon", lon_count // 2)
    opposite = opposite * jnp.array([-1.0, -1.0, 1.0, 1.0], jnp.float32)[:, None, None, None]
    south = jnp.where(lat_place == 0, opposite[:, :, 0, :], lat_padded[:, :, 0, :])
    north = jnp.where(
        lat_place == lat_count - 1, opposite[:, :, 1, :], lat_padded[:, :, rows + 1, :]
    )
    lat_padded = jnp.concatenate(
        [south[:, :, None, :], lat_padded[:, :, 1 : rows + 1, :], north[:, :, None, :]], axis=2
    )
    lon_padded = extended(fields, (("lon", 3),), 1, True)
    first_row = lat_place * rows
    cos_ext = row_cos(first_row - 1 + jnp.arange(rows + 2), total_rows)
    cos_faces = face_cos(first_row + jnp.arange(rows + 1), total_rows)
    coriolis = spin_rate(first_row + jnp.arange(rows), total_rows)
    tend = tendencies(lon_padded, lat_padded, cos_ext, cos_faces, coriolis, dlon, dlat)
    channels = 4 * levels
    slots = polar_rows.shape[1]
    cap = -(-rows // lat_count)
    queue = lat_count * cap
    source = polar_rows // rows
    local = polar_rows - source * rows
    order = jnp.arange(slots)
    earlier = (source[:, :, None] == source[:, None, :]) & (
        order[None, None, :] < order[None, :, None]
    )
    rank = jnp.sum(earlier.astype(jnp.int32), axis=2)
    target = (jnp.arange(lat_count)[:, None] * cap + rank).reshape(-1)
    owned = (source == lat_place).reshape(-1)
    picker = ((target[None, :] == jnp.arange(queue)[:, None]) & owned[None, :]).astype(jnp.float32)
    placer = (local.reshape(-1)[:, None] == jnp.arange(rows)[None, :]).astype(jnp.float32)
    sender = jnp.dot(picker, placer, preferred_element_type=jnp.float32)
    flat_tend = tend.reshape(channels, rows, cols)
    outgoing = jnp.einsum("qr,hrx->qhx", sender, flat_tend, precision=highest)
    incoming = lax.all_to_all(
        outgoing.reshape(lat_count, cap, channels, cols),
        "lat",
        split_axis=0,
        concat_axis=0,
        tiled=True,
    )
    own_rows = lax.dynamic_slice_in_dim(polar_rows, lat_place, 1, 0)[0]
    own_source = lax.dynamic_slice_in_dim(source, lat_place, 1, 0)[0]
    own_rank = lax.dynamic_slice_in_dim(rank, lat_place, 1, 0)[0]
    taker = ((own_source * cap + own_rank)[:, None] == jnp.arange(queue)[None, :]).astype(
        jnp.float32
    )
    compact = jnp.einsum(
        "sq,qhx->shx", taker, incoming.reshape(queue, channels, cols), precision=highest
    )
    limit = jnp.sum(
        jnp.where(own_rows[:, None] == jnp.arange(total_rows)[None, :], cutoffs[None, :], 0), axis=1
    )
    wave = jnp.arange(KMAX)
    weight = (
        jnp.where(wave[None, :] == 0, 1.0, jnp.where(wave[None, :] <= limit[:, None], 2.0, 0.0))
        / total_cols
    )
    weight = jnp.concatenate([weight, weight], axis=1)
    table = fourier_table(lon_place * cols, cols, total_cols)
    partial_sums = jnp.dot(
        compact.reshape(slots * channels, cols),
        table,
        precision=highest,
        preferred_element_type=jnp.float32,
    )
    summed = lax.psum(partial_sums, "lon")
    scaled = (summed.reshape(slots, channels, 2 * KMAX) * weight[:, None, :]).reshape(
        slots * channels, 2 * KMAX
    )
    filtered = jnp.dot(
        scaled, table.T, precision=highest, preferred_element_type=jnp.float32
    ).reshape(slots, channels, cols)
    returning = jnp.einsum("sq,shx->qhx", taker, filtered, precision=highest)
    arrived = lax.all_to_all(
        returning.reshape(lat_count, cap, channels, cols),
        "lat",
        split_axis=0,
        concat_axis=0,
        tiled=True,
    )
    restored = jnp.einsum(
        "qr,qhx->hrx", sender, arrived.reshape(queue, channels, cols), precision=highest
    )
    covered = jnp.sum(sender, axis=0)
    final = (flat_tend * (1.0 - covered)[None, :, None] + restored).reshape(4, levels, rows, cols)
    u_next = u_wind + step_size * final[0]
    v_next = v_wind + step_size * final[1]
    thickness_next = thickness + step_size * final[2]
    heat_next = thickness * theta + step_size * final[3]
    return (u_next, v_next, thickness_next, heat_next)


def solution(mesh):
    placed = (
        P(None, "lat", "lon"),
        P(None, "lat", "lon"),
        P(None, "lat", "lon"),
        P(None, "lat", "lon"),
        P(),
        P(),
    )
    return jax.shard_map(
        per_device,
        mesh=mesh,
        in_specs=placed,
        out_specs=(
            P(None, "lat", "lon"),
            P(None, "lat", "lon"),
            P(None, "lat", "lon"),
            P(None, "lat", "lon"),
        ),
        check_vma=False,
    )
```

profile of v0, /device:TPU:16, one launch (start us, length us, event | category | flops | bytes accessed | tf_op | source)
XLA Modules:
  0.0 526.0 jit_solution(14470549080982667643)
XLA Ops:
  12.4 5.1 collective-permute-start.4
  21.0 2.2 fusion.89
  23.2 2.7 copy.81
  27.3 2.7 copy.82
  30.0 2.8 collective-permute-start.1
  48.6 2.6 copy.63
  51.2 2.6 copy.64
  53.8 6.2 %pad_maximum_fusion = f32[4,24,32,386]{3,2,1,0:T(8,128)S(1)} fusion(f32[4,24,32,1]{3,2,1,0:T(8,128)} %copy.64, f32[1,24,32,384]{3,2,1,0:T(8,128)S(1)} %bitcast.89, f32[1,24,32,384]{3,2,1,0:T(8,128)S(1)} %bitcast.93, f32[1,24,32,384]{3,2,1,0:T(8,128)S(1)} %bitcast.97, f32[1,24,32,384]{3,2,1,0:T(8,128)} %bitcast.100, f32[4,24,32,1]{3,2,1,0:T(8,128)} %copy.63), kind=kLoop, calls=%fused_computation | loop fusion | flops 5928960 | bytes 9486336 | tf_op jit(solution)/shard_map/concatenate | solution.py:25
  71.4 4.1 convolution_bitcast_fusion
  75.5 4.9 copy.72
  80.4 11.6 %all-to-all-start = ((f32[32,1,96,384]{3,2,1,0:T(8,128)}), f32[32,1,96,384]{3,2,1,0:T(8,128)}, u32[]{:S(2)}, u32[]{:S(2)}) async-start(f32[32,1,96,384]{3,2,1,0:T(8,128)} %copy.72), calls=%async_computation | async-start | bytes 9437184 | tf_op jit(solution)/shard_map/all_to_all | solution.py:151
  93.5 5.0 fusion.59
  98.5 101.2 %all-to-all-done = f32[32,1,96,384]{3,2,1,0:T(8,128)} async-done(((f32[32,1,96,384]{3,2,1,0:T(8,128)}), f32[32,1,96,384]{3,2,1,0:T(8,128)}, u32[]{:S(2)}, u32[]{:S(2)}) %all-to-all-start) | async-done | bytes 4718624 | tf_op jit(solution)/shard_map/all_to_all | solution.py:151
  199.8 6.7 %fusion.2 = f32[16,96,384]{2,0,1:T(8,128)S(1)} fusion(f32[32,1,96,384]{3,2,1,0:T(8,128)} %all-to-all-done, s32[16]{0:T(128)S(1)} %copy-done.15), kind=kOutput, calls=%fused_computation.8 | convolution fusion | flops 226492928 | bytes 7077952 | tf_op jit(solution)/shard_map/sq,qhx->shx/dot_general | solution.py:164
  207.8 12.0 %fusion.26 = f32[1536,1024]{1,0:T(8,128)} fusion(f32[1536,384]{1,0:T(8,128)S(1)} %bitcast.104, f32[384,512]{1,0:T(8,128)S(1)} %copy-done.9, f32[384,512]{1,0:T(8,128)S(1)} %copy-done.7), kind=kOutput, calls=%fused_computation.50 | convolution fusion | flops 7248150528 | bytes 10223616 | tf_op jit(solution)/shard_map/dot_general | solution.py:177
  221.5 142.4 %all-reduce.2.cloned.1.call-done = f32[1536,1024]{1,0:T(8,128)} async-done(((f32[1536,1024]{1,0:T(8,128)}), f32[1536,1024]{1,0:T(8,128)}) %all-reduce.2.cloned.1.call-update) | async-done | bytes 6291472 | tf_op jit(solution)/shard_map/psum | solution.py:183
  363.8 3.7 bitcast_multiply_fusion
  367.6 10.4 %fusion.17 = f32[16,96,384]{2,1,0:T(8,128)S(1)} fusion(f32[16,96,1024]{2,1,0:T(8,128)S(1)} %bitcast.103, f32[384,512]{1,0:T(8,128)S(1)} %copy-done.10, f32[384,512]{1,0:T(8,128)S(1)} %copy-done.8), kind=kOutput, calls=%fused_computation.30 | convolution fusion | flops 7248150528 | bytes 10223616 | tf_op jit(solution)/shard_map/dot_general | solution.py:187
  378.0 3.5 fusion.8
  381.5 4.9 copy.76
  386.4 10.3 %all-to-all-start.1 = ((f32[32,1,96,384]{3,2,1,0:T(8,128)}), f32[32,1,96,384]{3,2,1,0:T(8,128)}, u32[]{:S(2)}, u32[]{:S(2)}) async-start(f32[32,1,96,384]{3,2,1,0:T(8,128)} %copy.76), calls=%async_computation.1 | async-start | bytes 9437184 | tf_op jit(solution)/shard_map/all_to_all | solution.py:191
  397.9 106.6 %all-to-all-done.1 = f32[32,1,96,384]{3,2,1,0:T(8,128)} async-done(((f32[32,1,96,384]{3,2,1,0:T(8,128)}), f32[32,1,96,384]{3,2,1,0:T(8,128)}, u32[]{:S(2)}, u32[]{:S(2)}) %all-to-all-start.1) | async-done | bytes 4718624 | tf_op jit(solution)/shard_map/all_to_all | solution.py:191
  504.4 11.5 %bitcast_add_fusion = f32[96,32,384]{2,1,0:T(8,128)S(1)} fusion(f32[96,32,384]{2,1,0:T(8,128)} %bitcast.86, f32[32]{0:T(128)} %broadcast_subtract_fusion, f32[32,1,96,384]{3,2,1,0:T(8,128)} %all-to-all-done.1, f32[32,32]{1,0:T(8,128)S(1)} %copy-done.14), kind=kOutput, calls=%fused_computation.5 | convolution fusion | flops 455344128 | bytes 14160000 | tf_op jit(solution)/shard_map/qr,qhx->hrx/dot_general | solution.py:198
  516.0 3.0 fusion.27
  (101 shorter events, 42.6 us)
Async XLA Ops:
  7.2 13.4 %copy-start.2 = (f32[24,32,384]{2,1,0:T(8,128)S(1)}, f32[24,32,384]{2,1,0:T(8,128)}, u32[]{:S(2)}) copy-start(f32[24,32,384]{2,1,0:T(8,128)} %param.9) | copy-start | bytes 3538948
  7.2 13.4 %copy-start.3 = (f32[24,32,384]{2,1,0:T(8,128)S(1)}, f32[24,32,384]{2,1,0:T(8,128)}, u32[]{:S(2)}) copy-start(f32[24,32,384]{2,1,0:T(8,128)} %param.8) | copy-start | bytes 3538948
  7.2 13.4 %copy-start.4 = (f32[24,32,384]{2,1,0:T(8,128)S(1)}, f32[24,32,384]{2,1,0:T(8,128)}, u32[]{:S(2)}) copy-start(f32[24,32,384]{2,1,0:T(8,128)} %param.7) | copy-start | bytes 3538948
  9.2 11.4 %copy-start.1 = (f32[24,32,384]{2,1,0:T(8,128)S(1)}, f32[24,32,384]{2,1,0:T(8,128)}, u32[]{:S(2)}) copy-start(f32[24,32,384]{2,1,0:T(8,128)} %param.10) | copy-start | bytes 3538948
  9.8 53.9 %collective-permute-start.3 = (f32[4,24,1,384]{3,1,2,0:T(8,128)}, f32[4,24,1,384]{3,1,2,0:T(8,128)}, u32[]{:S(2)}, u32[]{:S(2)}) collective-permute-start(f32[4,24,1,384]{3,1,2,0:T(8,128)} %copy.84), channel_id=1, source_target_pairs={{0,8},{8,16},{16,24},{24,32},{32,40},{40,48},{48,56},{56,64},{64,7... | collective-permute-start | bytes 442376 | tf_op jit(solution)/shard_map/ppermute | solution.py:21
  12.4 51.3 %collective-permute-start.4 = (f32[4,24,1,384]{3,1,2,0:T(8,128)}, f32[4,24,1,384]{3,1,2,0:T(8,128)}, u32[]{:S(2)}, u32[]{:S(2)}) collective-permute-start(f32[4,24,1,384]{3,1,2,0:T(8,128)} %copy.83), channel_id=1, source_target_pairs={{8,0},{16,8},{24,16},{32,24},{40,32},{48,40},{56,48},{64,56},{72,6... | collective-permute-start | bytes 442376 | tf_op jit(solution)/shard_map/ppermute | solution.py:24
  19.3 43.3 %collective-permute-start.2 = (f32[4,24,2,384]{3,1,2,0:T(8,128)}, f32[4,24,2,384]{3,1,2,0:T(8,128)}, u32[]{:S(2)}, u32[]{:S(2)}) collective-permute-start(f32[4,24,2,384]{3,1,2,0:T(8,128)} %pad_maximum_fusion.7), channel_id=1, source_target_pairs={{0,4},{1,5},{2,6},{3,7},{4,0},{5,1},{6,2},{7,3},{8,12},{9,13},{10,... | collective-permute-start | bytes 884744 | tf_op jit(solution)/shard_map/ppermute | solution.py:32
  23.2 10.2 %copy-start.11 = (s32[32,16]{0,1:T(8,128)S(1)}, s32[32,16]{0,1:T(8,128)}, u32[]{:S(2)}) copy-start(s32[32,16]{0,1:T(8,128)} %param.11) | copy-start | bytes 6148
  25.8 22.8 %collective-permute-start = (f32[4,24,32,1]{2,1,3,0:T(8,128)}, f32[4,24,32,1]{2,1,3,0:T(8,128)}, u32[]{:S(2)}, u32[]{:S(2)}) collective-permute-start(f32[4,24,32,1]{2,1,3,0:T(8,128)} %copy.81), channel_id=1, source_target_pairs={{0,1},{1,2},{2,3},{3,4},{4,5},{5,6},{6,7},{7,0},{8,9},{9,10},{10,1... | collective-permute-start | bytes 36872 | tf_op jit(solution)/shard_map/ppermute | solution.py:21
  30.0 21.2 %collective-permute-start.1 = (f32[4,24,32,1]{2,1,3,0:T(8,128)}, f32[4,24,32,1]{2,1,3,0:T(8,128)}, u32[]{:S(2)}, u32[]{:S(2)}) collective-permute-start(f32[4,24,32,1]{2,1,3,0:T(8,128)} %copy.82), channel_id=1, source_target_pairs={{1,0},{2,1},{3,2},{4,3},{5,4},{6,5},{7,6},{0,7},{9,8},{10,9},{11,1... | collective-permute-start | bytes 36872 | tf_op jit(solution)/shard_map/ppermute | solution.py:24
  61.3 1.3 copy-start.23
  62.6 2.6 copy-start.5
  65.1 1.2 copy-start.21
  71.0 4.5 copy-start
  80.4 119.3 %all-to-all-start = ((f32[32,1,96,384]{3,2,1,0:T(8,128)}), f32[32,1,96,384]{3,2,1,0:T(8,128)}, u32[]{:S(2)}, u32[]{:S(2)}) async-start(f32[32,1,96,384]{3,2,1,0:T(8,128)} %copy.72), calls=%async_computation | async-start | bytes 9437184 | tf_op jit(solution)/shard_map/all_to_all | solution.py:151
  92.1 271.8 %all-reduce.2.cloned.1.call-start = ((), (), s32[]{:S(2)}) async-start(), calls=%async_computation.2 | async-start | bytes 12582912 | tf_op jit(solution)/shard_map/psum | solution.py:183
  93.5 106.2 %copy-start.15 = (s32[16]{0:T(128)S(1)}, s32[16]{0:T(128)}, u32[]{:S(2)}) copy-start(s32[16]{0:T(128)} %add_reduce_fusion) | copy-start | bytes 196
  206.5 1.1 copy-start.7
  206.5 1.4 copy-start.9
  363.8 3.8 copy-start.8
  363.8 3.8 copy-start.10
  386.4 118.0 %copy-start.14 = (f32[32,32]{1,0:T(8,128)S(1)}, f32[32,32]{1,0:T(8,128)}, u32[]{:S(2)}) copy-start(f32[32,32]{1,0:T(8,128)} %get-tuple-element.39) | copy-start | bytes 12292
  386.4 118.0 %all-to-all-start.1 = ((f32[32,1,96,384]{3,2,1,0:T(8,128)}), f32[32,1,96,384]{3,2,1,0:T(8,128)}, u32[]{:S(2)}, u32[]{:S(2)}) async-start(f32[32,1,96,384]{3,2,1,0:T(8,128)} %copy.76), calls=%async_computation.1 | async-start | bytes 9437184 | tf_op jit(solution)/shard_map/all_to_all | solution.py:191
  504.4 11.5 %copy-start.6 = (f32[24,32,384]{2,1,0:T(8,128)S(1)}, f32[24,32,384]{2,1,0:T(8,128)}, u32[]{:S(2)}) copy-start(f32[24,32,384]{2,1,0:T(8,128)} %param.7) | copy-start | bytes 3538948
  (8 other events, 5.8 us)
Sparse Core Ops, SparseCore 0:
  220.0 143.7 all-reduce.1
where the time goes:
time: 530 us; the launch traced here: 526 us
  waiting for transfers between devices  350 us (66%)
  matrix products  50.3 us (9%)
  other arithmetic  39.2 us (7%)
  local copies, waits for them, and re-layouts  37 us (7%)
  starting transfers between devices  34.6 us (7%)
  between operations  14.7 us (3%)
    psum x1, waiting for transfers between devices, per_device(): summed = lax.psum(partial_sums, 'lon')  142 us
    all_to_all x1, waiting for transfers between devices, per_device(): lax.all_to_all(returning.reshape(lat_count, cap, channels, cols), 'lat',...  107 us
    all_to_all x1, waiting for transfers between devices, per_device(): lax.all_to_all(outgoing.reshape(lat_count, cap, channels, cols), 'lat', s...  101 us
    dot_general x1, matrix products, per_device(): jnp.dot(compact.reshape(slots * channels, cols), table, precision=highest...  12 us
    all_to_all x1, starting transfers between devices, per_device(): lax.all_to_all(outgoing.reshape(lat_count, cap, channels, cols), 'lat', s...  11.6 us
    dot_general x1, matrix products, per_device(): jnp.einsum('qr,qhx->hrx', sender, arrived.reshape(queue, channels, cols),...  11.5 us
  transfers between devices with their start and end apart: 8, of which 3 were waited for; matrix products, arithmetic and copies ran while one was open for 9% of the time, Pallas kernels for 0%

commit v1 on v0

v1 whole, which is shorter than its diff:
```python
import functools
import math

import jax
import jax.numpy as jnp
import numpy as np
from jax import lax
from jax.experimental import pallas as pl
from jax.experimental.pallas import tpu as pltpu
from jax.sharding import PartitionSpec as P

OMEGA = 30.0
KHALF = 208


def geometry(total_rows):
    row = np.arange(-1, total_rows + 1)
    dist = np.maximum(np.minimum(row, total_rows - 1 - row), 0)
    cos_row = np.sin(np.pi * (dist + 0.5) / total_rows)
    face = np.arange(total_rows + 1)
    cos_face = np.sin(np.pi * np.minimum(face, total_rows - face) / total_rows)
    spin = -2.0 * OMEGA * np.cos(np.pi * (np.arange(total_rows) + 0.5) / total_rows)
    table = np.zeros((total_rows, 8))
    table[:, 0] = cos_row[1:-1]
    table[:, 1] = cos_row[:-2]
    table[:, 2] = cos_row[2:]
    table[:, 3] = cos_face[:-1]
    table[:, 4] = cos_face[1:]
    table[:, 5] = spin
    table[:, 6] = 1.0 / cos_row[1:-1]
    return table.astype(np.float32)


def fourier_tables(total):
    column = np.arange(total // 2)
    tables = []
    for odd in (0, 1):
        wave = 2 * np.arange(KHALF) + odd
        angle = (column[:, None] * wave[None, :] % total) * (2.0 * np.pi / total)
        tables.append(np.concatenate([np.cos(angle), np.sin(angle)], axis=1))
    return [table.astype(np.float32) for table in tables]


def shifted(x, amount, axis, edge):
    size = x.shape[axis]
    place = lax.broadcasted_iota(jnp.int32, x.shape, axis)
    at = size - 1 if amount < 0 else 0
    return jnp.where(place == at, edge, pltpu.roll(x, amount % size, axis))


def tend_body(part, dlon, dlat, geo_ref, u_ref, v_ref, p_ref, h_ref, s_ref, n_ref, w_ref, e_ref, out_ref):
    geo = geo_ref[...]
    c0, cs, cn = geo[:, 0:1], geo[:, 1:2], geo[:, 2:3]
    fs, fn, spin0, inv = geo[:, 3:4], geo[:, 4:5], geo[:, 5:6], geo[:, 6:7]
    for k in range(u_ref.shape[0]):
        u, v, p, h = u_ref[k], v_ref[k], p_ref[k], h_ref[k]
        south = [s_ref[k, f : f + 1, :] for f in range(4)]
        north = [n_ref[k, f : f + 1, :] for f in range(4)]
        west = [w_ref[k, :, f : f + 1] for f in range(4)]
        east = [e_ref[k, :, f : f + 1] for f in range(4)]
        heat = p * h
        if part == 0:
            energy = 0.5 * (u * u + v * v) + heat
            edge = [0.5 * (q[0] * q[0] + q[1] * q[1]) + q[2] * q[3] for q in (south, north, west, east)]
            zeta = (shifted(v, -1, 1, east[1]) - shifted(v, 1, 1, west[1])) * (0.5 / dlon)
            zeta -= (cn * shifted(u, -1, 0, north[0]) - cs * shifted(u, 1, 0, south[0])) * (0.5 / dlat)
            absolute = spin0 + zeta * inv
            de_x = shifted(energy, -1, 1, edge[3]) - shifted(energy, 1, 1, edge[2])
            de_y = shifted(energy, -1, 0, edge[1]) - shifted(energy, 1, 0, edge[0])
            out_ref[0, 0, k] = absolute * v - de_x * ((0.5 / dlon) * inv)
            out_ref[0, 1, k] = -absolute * u - de_y * (0.5 / dlat)
        else:
            a = 0.5 * (u + shifted(u, -1, 1, east[0]))
            ap, am = jnp.maximum(a, 0.0), jnp.minimum(a, 0.0)
            mx = ap * p + am * shifted(p, -1, 1, east[2])
            hx = ap * heat + am * shifted(heat, -1, 1, east[2] * east[3])
            a0 = 0.5 * (west[0] + u[:, 0:1])
            ap0, am0 = jnp.maximum(a0, 0.0), jnp.minimum(a0, 0.0)
            mx0 = ap0 * west[2] + am0 * p[:, 0:1]
            hx0 = ap0 * (west[2] * west[3]) + am0 * heat[:, 0:1]
            b = 0.5 * (v + shifted(v, -1, 0, north[1]))
            bp, bm = fn * jnp.maximum(b, 0.0), fn * jnp.minimum(b, 0.0)
            my = bp * p + bm * shifted(p, -1, 0, north[2])
            hy = bp * heat + bm * shifted(heat, -1, 0, north[2] * north[3])
            b0 = 0.5 * (south[1] + v[0:1, :])
            bp0, bm0 = fs[0:1] * jnp.maximum(b0, 0.0), fs[0:1] * jnp.minimum(b0, 0.0)
            my0 = bp0 * south[2] + bm0 * p[0:1, :]
            hy0 = bp0 * (south[2] * south[3]) + bm0 * heat[0:1, :]
            out_ref[0, 0, k] = -inv * (
                (mx - shifted(mx, 1, 1, mx0)) * (1.0 / dlon) + (my - shifted(my, 1, 0, my0)) * (1.0 / dlat)
            )
            out_ref[0, 1, k] = -inv * (
                (hx - shifted(hx, 1, 1, hx0)) * (1.0 / dlon) + (hy - shifted(hy, 1, 0, hy0)) * (1.0 / dlat)
            )


def tendencies(part, groups, dlon, dlat, geo, fields, south, north, west, east):
    levels, rows, cols = fields[0].shape
    per = levels // groups
    field = pl.BlockSpec((per, rows, cols), lambda g: (g, 0, 0))
    lat_halo = pl.BlockSpec((per, 4, cols), lambda g: (g, 0, 0))
    lon_halo = pl.BlockSpec((per, rows, 4), lambda g: (g, 0, 0))
    return pl.pallas_call(
        functools.partial(tend_body, part, dlon, dlat),
        grid=(groups,),
        in_specs=[pl.BlockSpec((rows, 8), lambda g: (0, 0))] + [field] * 4 + [lat_halo] * 2 + [lon_halo] * 2,
        out_specs=pl.BlockSpec((1, 2, per, rows, cols), lambda g: (g, 0, 0, 0, 0)),
        out_shape=jax.ShapeDtypeStruct((groups, 2, per, rows, cols), jnp.float32),
        cost_estimate=pl.CostEstimate(flops=40 * levels * rows * cols, bytes_accessed=24 * levels * rows * cols, transcendentals=0),
    )(geo, *fields, south, north, west, east)


def per_device(u_wind, v_wind, thickness, theta, polar_rows, cutoffs):
    levels, rows, cols = u_wind.shape
    lat_count = lax.axis_size("lat")
    lon_count = lax.axis_size("lon")
    lat_place = lax.axis_index("lat")
    total_rows = rows * lat_count
    total_cols = cols * lon_count
    dlon = 2.0 * math.pi / total_cols
    dlat = math.pi / total_rows
    step_size = 0.25 * dlon
    high = lax.Precision.HIGH
    first_row = lat_place * rows
    fields = (u_wind, v_wind, thickness, theta)

    low_rows = jnp.stack([f[:, 0, :] for f in fields], axis=1)
    high_rows = jnp.stack([f[:, rows - 1, :] for f in fields], axis=1)
    south = lax.ppermute(high_rows, "lat", [(i, i + 1) for i in range(lat_count - 1)])
    north = lax.ppermute(low_rows, "lat", [(i + 1, i) for i in range(lat_count - 1)])
    polar = jnp.where(lat_place == 0, low_rows, high_rows)
    half = lon_count // 2
    pairs = [
        (band * lon_count + i, band * lon_count + (i + half) % lon_count)
        for band in (0, lat_count - 1)
        for i in range(lon_count)
    ]
    signs = jnp.array([-1.0, -1.0, 1.0, 1.0], jnp.float32)[None, :, None]
    polar = lax.ppermute(polar, ("lat", "lon"), pairs) * signs
    south = jnp.where(lat_place == 0, polar, south)
    north = jnp.where(lat_place == lat_count - 1, polar, north)
    ring = [(i, (i + 1) % lon_count) for i in range(lon_count)]
    west = lax.ppermute(jnp.stack([f[:, :, cols - 1] for f in fields]), "lon", ring)
    east = lax.ppermute(jnp.stack([f[:, :, 0] for f in fields]), "lon", [(j, i) for i, j in ring])
    west = jnp.transpose(west, (1, 2, 0))
    east = jnp.transpose(east, (1, 2, 0))
    geo = lax.dynamic_slice_in_dim(jnp.asarray(geometry(total_rows)), first_row, rows, 0)

    own = first_row + jnp.arange(rows)
    listed = jnp.any(polar_rows.reshape(-1)[None, :] == own[:, None], axis=1)[:, None]
    limit = lax.dynamic_slice_in_dim(cutoffs, first_row, rows, 0)
    tables = [jnp.asarray(t).reshape(lon_count // 2, cols, 2 * KHALF) for t in fourier_tables(total_cols)]
    weights = []
    for odd in (0, 1):
        wave = 2 * jnp.arange(KHALF) + odd
        w = jnp.where(wave[None, :] == 0, 1.0, jnp.where(wave[None, :] <= limit[:, None], 2.0, 0.0)) / total_cols
        weights.append(jnp.concatenate([w, w], axis=1))

    def filtered(tend):
        per = levels // lon_count
        got = lax.all_to_all(tend, "lon", 0, 0, tiled=True)
        front, back = got[:half], got[half:]
        sides = []
        for x, table, weight in ((front + back, tables[0], weights[0]), (front - back, tables[1], weights[1])):
            spectrum = jnp.einsum("bflrc,bck->flrk", x, table, precision=high, preferred_element_type=jnp.float32)
            spectrum = spectrum * weight
            sides.append(
                jnp.einsum("flrk,bck->bflrc", spectrum, table, precision=high, preferred_element_type=jnp.float32)
            )
        out = jnp.concatenate([sides[0] + sides[1], sides[0] - sides[1]], axis=0)
        return lax.all_to_all(out, "lon", 0, 0, tiled=True)

    final = []
    for part in (0, 1):
        tend = tendencies(part, lon_count, dlon, dlat, geo, fields, south, north, west, east)
        chosen = jnp.where(listed, filtered(tend), tend)
        final += [chosen[:, q].reshape(levels, rows, cols) for q in (0, 1)]
    return (
        u_wind + step_size * final[0],
        v_wind + step_size * final[1],
        thickness + step_size * final[2],
        thickness * theta + step_size * final[3],
    )


def solution(mesh):
    field = P(None, "lat", "lon")
    return jax.shard_map(
        per_device,
        mesh=mesh,
        in_specs=(field, field, field, field, P(), P()),
        out_specs=(field, field, field, field),
        check_vma=False,
    )
```

time: 530 us -> 203 us (0.38)
  waiting for transfers between devices: 350 us -> 98.2 us
  matrix products: 50.3 us -> 10.8 us
  other arithmetic: 39.2 us -> 17.6 us
  local copies, waits for them, and re-layouts: 37 us -> 16.7 us
  Pallas kernels: 0 us -> 18.3 us
  between operations: 14.7 us -> 0.92 us
    psum x1 -> x0, waiting for transfers between devices: 142 us -> none  [per_device(): summed = lax.psum(partial_sums, 'lon')]
    all_to_all x2 -> x4, waiting for transfers between devices: 208 us -> 89.5 us  [the longest x2 47.7 us: filtered(): return lax.all_to_all(out, 'lon', 0, 0, tiled=True)]
    dot_general x7 -> x8, matrix products: 50.3 us -> 10.8 us  [the longest x4 5.62 us: filtered(): jnp.einsum('bflrc,bck->flrk', x, table, precision=high, preferred_element...]
    pallas_call x0 -> x2, Pallas kernels: none -> 18.3 us  [tendencies(): pl.pallas_call(functools.partial(tend_body, part, dlon, dlat), grid=(grou...]
    reshape x2 -> x0, local copies, waits for them, and re-layouts: 9.83 us -> none  [the longest x1 4.92 us: per_device(): outgoing.reshape(lat_count, cap, channels, cols)]
    ppermute x5, waiting for transfers between devices: 0.01 us -> 8.72 us  [the longest x1 6.04 us: per_device(): lax.ppermute(jnp.stack([f[:, :, cols - 1] for f in fields]), 'lon', ring)]
    all_to_all x2 -> x4, starting transfers between devices: 21.9 us -> 29.5 us  [the longest x2 17.2 us: filtered(): return lax.all_to_all(out, 'lon', 0, 0, tiled=True)]
    mul x4 -> x3, other arithmetic: 6.42 us -> 0.51 us  [the longest x1 0.28 us: per_device(): step_size * final[3]]
  transfers between devices with their start and end apart: 8 -> 9, of which waited for: 3 -> 6; matrix products, arithmetic and copies ran while one was open for 9% -> 12% of each run, Pallas kernels for 0% -> 4%
where the time goes in v1:
time: 203 us; the launch traced here: 202 us
  waiting for transfers between devices  98.2 us (48%)
  starting transfers between devices  39 us (19%)
  Pallas kernels  18.3 us (9%)
  other arithmetic  17.6 us (9%)
  local copies, waits for them, and re-layouts  16.7 us (8%)
  matrix products  10.8 us (5%)
    all_to_all x2, waiting for transfers between devices, filtered(): return lax.all_to_all(out, 'lon', 0, 0, tiled=True)  47.7 us
    all_to_all x2, waiting for transfers between devices, filtered(): got = lax.all_to_all(tend, 'lon', 0, 0, tiled=True)  41.9 us
    pallas_call x2, Pallas kernels, tendencies(): pl.pallas_call(functools.partial(tend_body, part, dlon, dlat), grid=(grou...  18.3 us
    all_to_all x2, starting transfers between devices, filtered(): return lax.all_to_all(out, 'lon', 0, 0, tiled=True)  17.2 us
    all_to_all x2, starting transfers between devices, filtered(): got = lax.all_to_all(tend, 'lon', 0, 0, tiled=True)  12.4 us
    unnamed x49, local copies, waits for them, and re-layouts  10.7 us
    ppermute x1, waiting for transfers between devices, per_device(): lax.ppermute(jnp.stack([f[:, :, cols - 1] for f in fields]), 'lon', ring)  6.04 us
    dot_general x4, matrix products, filtered(): jnp.einsum('bflrc,bck->flrk', x, table, precision=high, preferred_element...  5.62 us
  transfers between devices with their start and end apart: 9, of which 6 were waited for; matrix products, arithmetic and copies ran while one was open for 12% of the time, Pallas kernels for 4%

profile of v1, /device:TPU:16, one launch (start us, length us, event | category | flops | bytes accessed | tf_op | source)
XLA Modules:
  0.0 201.6 jit_solution(10743262000811213549)
XLA Ops:
  0.6 1.4 fusion.30
  4.4 1.9 collective-permute-start.2
  7.6 2.4 %collective-permute-start.1 = (f32[24,4,384]{2,1,0:T(4,128)S(1)}, f32[24,4,384]{2,1,0:T(4,128)}, u32[]{:S(2)}, u32[]{:S(2)}) collective-permute-start(f32[24,4,384]{2,1,0:T(4,128)S(1)} %get-tuple-element.38), channel_id=1, source_target_pairs={{0,8},{8,16},{16,24},{24,32},{32,40},{40,48},{48,56},{56,64},{64,7... | collective-permute-start | bytes 442376 | tf_op jit(solution)/shard_map/ppermute | solution.py:129
  14.0 3.7 %collective-permute-start.4 = (f32[4,24,32]{0,2,1:T(8,128)S(1)}, f32[4,24,32]{0,2,1:T(8,128)S(1)}, u32[]{:S(2)}, u32[]{:S(2)}) collective-permute-start(f32[4,24,32]{0,2,1:T(8,128)S(1)} %copy.92), channel_id=1, source_target_pairs={{1,0},{2,1},{3,2},{4,3},{5,4},{6,5},{7,6},{0,7},{9,8},{10,9},{11,1... | collective-permute-start | bytes 36872 | tf_op jit(solution)/shard_map/ppermute | solution.py:144
  20.3 1.9 multiply_select_fusion
  22.2 2.7 %collective-permute-done.4 = f32[4,24,32]{0,2,1:T(8,128)S(1)} collective-permute-done((f32[4,24,32]{0,2,1:T(8,128)S(1)}, f32[4,24,32]{0,2,1:T(8,128)S(1)}, u32[]{:S(2)}, u32[]{:S(2)}) %collective-permute-start.4) | collective-permute-done | bytes 12320 | tf_op jit(solution)/shard_map/ppermute | solution.py:144
  24.9 6.0 %collective-permute-done.3 = f32[4,24,32]{0,2,1:T(8,128)S(1)} collective-permute-done((f32[4,24,32]{0,2,1:T(8,128)S(1)}, f32[4,24,32]{0,2,1:T(8,128)S(1)}, u32[]{:S(2)}, u32[]{:S(2)}) %collective-permute-start.3) | collective-permute-done | bytes 12320 | tf_op jit(solution)/shard_map/ppermute | solution.py:143
  31.7 9.4 %shard_map.130 = f32[8,2,3,32,384]{4,3,2,1,0:T(8,128)} custom-call(f32[32,8]{1,0:T(8,128)} %constant_dynamic-slice_fusion.geo_ref, f32[24,32,384]{2,1,0:T(8,128)} %u_ref.3, f32[24,32,384]{2,1,0:T(8,128)} %v_ref.3, f32[24,32,384]{2,1,0:T(8,128)} %p_ref.3, f32[24,32,384]{2,1,0:T(8,128)} %h_ref.3, f32[24,4,384]{2,1,0:T(4,128)} %get-tuple-element.35.s_ref, ...), custom_call_target="tpu_custom_call" | custom-call | flops 11796480 | bytes 7077888 | tf_op jit(solution)/shard_map/pallas_call | solution.py:103
  41.0 3.6 %all-to-all-start.2 = ((f32[8,2,3,32,384]{4,3,2,1,0:T(8,128)}), f32[8,2,3,32,384]{4,3,2,1,0:T(8,128)S(1)}, u32[]{:S(2)}, u32[]{:S(2)}) async-start(f32[8,2,3,32,384]{4,3,2,1,0:T(8,128)} %shard_map.130), calls=%async_computation.2 | async-start | bytes 4718592 | tf_op jit(solution)/shard_map/all_to_all | solution.py:161
  45.5 8.9 %shard_map.129 = f32[8,2,3,32,384]{4,3,2,1,0:T(8,128)} custom-call(f32[32,8]{1,0:T(8,128)} %constant_dynamic-slice_fusion.geo_ref, f32[24,32,384]{2,1,0:T(8,128)} %u_ref.3, f32[24,32,384]{2,1,0:T(8,128)} %v_ref.3, f32[24,32,384]{2,1,0:T(8,128)} %p_ref.3, f32[24,32,384]{2,1,0:T(8,128)} %h_ref.3, f32[24,4,384]{2,1,0:T(4,128)} %get-tuple-element.35.s_ref, ...), custom_call_target="tpu_custom_call" | custom-call | flops 11796480 | bytes 7077888 | tf_op jit(solution)/shard_map/pallas_call | solution.py:103
  54.4 21.0 %all-to-all-done.2 = f32[8,2,3,32,384]{4,3,2,1,0:T(8,128)S(1)} async-done(((f32[8,2,3,32,384]{4,3,2,1,0:T(8,128)}), f32[8,2,3,32,384]{4,3,2,1,0:T(8,128)S(1)}, u32[]{:S(2)}, u32[]{:S(2)}) %all-to-all-start.2) | async-done | bytes 2359328 | tf_op jit(solution)/shard_map/all_to_all | solution.py:161
  75.4 8.7 %all-to-all-start = ((f32[8,2,3,32,384]{4,3,2,1,0:T(8,128)}), f32[8,2,3,32,384]{4,3,2,1,0:T(8,128)}, u32[]{:S(2)}, u32[]{:S(2)}) async-start(f32[8,2,3,32,384]{4,3,2,1,0:T(8,128)} %shard_map.129), calls=%async_computation | async-start | bytes 4718592 | tf_op jit(solution)/shard_map/all_to_all | solution.py:161
  84.6 1.5 copy-done.14
  92.4 1.6 pad_maximum_fusion.1
  94.1 20.9 %all-to-all-done = f32[8,2,3,32,384]{4,3,2,1,0:T(8,128)} async-done(((f32[8,2,3,32,384]{4,3,2,1,0:T(8,128)}), f32[8,2,3,32,384]{4,3,2,1,0:T(8,128)}, u32[]{:S(2)}, u32[]{:S(2)}) %all-to-all-start) | async-done | bytes 2359328 | tf_op jit(solution)/shard_map/all_to_all | solution.py:161
  114.9 10.3 %all-to-all-start.3 = ((f32[8,2,3,32,384]{4,3,2,1,0:T(8,128)}), f32[8,2,3,32,384]{4,3,2,1,0:T(8,128)}, u32[]{:S(2)}, u32[]{:S(2)}) async-start(f32[8,2,3,32,384]{4,3,2,1,0:T(8,128)} %pad_maximum_fusion.1), calls=%async_computation.3 | async-start | bytes 4718592 | tf_op jit(solution)/shard_map/all_to_all | solution.py:171
  125.3 2.0 slice_subtract_fusion.1
  127.7 1.4 fusion.4
  133.7 1.6 pad_maximum_fusion
  135.4 19.6 %all-to-all-done.3 = f32[8,2,3,32,384]{4,3,2,1,0:T(8,128)} async-done(((f32[8,2,3,32,384]{4,3,2,1,0:T(8,128)}), f32[8,2,3,32,384]{4,3,2,1,0:T(8,128)}, u32[]{:S(2)}, u32[]{:S(2)}) %all-to-all-start.3) | async-done | bytes 2359328 | tf_op jit(solution)/shard_map/all_to_all | solution.py:171
  154.9 6.9 %all-to-all-start.1 = ((f32[8,2,3,32,384]{4,3,2,1,0:T(8,128)}), f32[8,2,3,32,384]{4,3,2,1,0:T(8,128)}, u32[]{:S(2)}, u32[]{:S(2)}) async-start(f32[8,2,3,32,384]{4,3,2,1,0:T(8,128)} %pad_maximum_fusion), calls=%async_computation.1 | async-start | bytes 4718592 | tf_op jit(solution)/shard_map/all_to_all | solution.py:171
  162.2 28.1 %all-to-all-done.1 = f32[8,2,3,32,384]{4,3,2,1,0:T(8,128)} async-done(((f32[8,2,3,32,384]{4,3,2,1,0:T(8,128)}), f32[8,2,3,32,384]{4,3,2,1,0:T(8,128)}, u32[]{:S(2)}, u32[]{:S(2)}) %all-to-all-start.1) | async-done | bytes 2359328 | tf_op jit(solution)/shard_map/all_to_all | solution.py:171
  190.2 4.2 %broadcast_select_fusion = (f32[8,2,3,32,384]{4,3,2,1,0:T(8,128)S(1)}, f32[8,2,3,32,384]{4,3,2,1,0:T(8,128)S(1)}) fusion(f32[8,2,3,32,384]{4,3,2,1,0:T(8,128)} %all-to-all-done.3, f32[8,2,3,32,384]{4,3,2,1,0:T(8,128)S(1)} %copy-done, pred[32]{0:T(512)(128)(4,1)S(1)} %compare_reduce_fusion, f32[8,2,3,32,384]{4,3,2,1,0:T(8,128)} %all-to-all-done.1, ...), kind=kLoop, calls=%fused_computation.22 | loop fusion | flops 1179648 | bytes 14155808 | tf_op jit(solution)/shard_map/jit(_where)/select_n | solution.py:176
  199.7 1.9 bitcast_add_fusion
  (86 shorter events, 29.1 us)
Async XLA Ops:
  0.6 9.4 %copy-start.3 = (f32[24,32,384]{2,1,0:T(8,128)S(1)}, f32[24,32,384]{2,1,0:T(8,128)}, u32[]{:S(2)}) copy-start(f32[24,32,384]{2,1,0:T(8,128)} %u_ref.3) | copy-start | bytes 3538948
  3.4 6.8 %copy-start.1 = (f32[24,32,384]{2,1,0:T(8,128)S(1)}, f32[24,32,384]{2,1,0:T(8,128)}, u32[]{:S(2)}) copy-start(f32[24,32,384]{2,1,0:T(8,128)} %v_ref.3) | copy-start | bytes 3538948
  4.4 15.9 %collective-permute-start.2 = (f32[24,4,384]{2,1,0:T(4,128)}, f32[24,4,384]{2,1,0:T(4,128)}, u32[]{:S(2)}, u32[]{:S(2)}) collective-permute-start(f32[24,4,384]{2,1,0:T(4,128)} %get-tuple-element.36), channel_id=1, source_target_pairs={{8,0},{16,8},{24,16},{32,24},{40,32},{48,40},{56,48},{64,56},{72,6... | collective-permute-start | bytes 442376 | tf_op jit(solution)/shard_map/ppermute | solution.py:130
  6.3 14.0 %collective-permute-start = (f32[24,4,384]{2,1,0:T(4,128)S(1)}, f32[24,4,384]{2,1,0:T(4,128)}, u32[]{:S(2)}, u32[]{:S(2)}) collective-permute-start(f32[24,4,384]{2,1,0:T(4,128)S(1)} %get-tuple-element.37), channel_id=1, source_target_pairs={{0,4},{1,5},{2,6},{3,7},{4,0},{5,1},{6,2},{7,3},{248,252},{249,253... | collective-permute-start | bytes 442376 | tf_op jit(solution)/shard_map/ppermute | solution.py:139
  7.6 12.7 %collective-permute-start.1 = (f32[24,4,384]{2,1,0:T(4,128)S(1)}, f32[24,4,384]{2,1,0:T(4,128)}, u32[]{:S(2)}, u32[]{:S(2)}) collective-permute-start(f32[24,4,384]{2,1,0:T(4,128)S(1)} %get-tuple-element.38), channel_id=1, source_target_pairs={{0,8},{8,16},{16,24},{24,32},{32,40},{40,48},{48,56},{56,64},{64,7... | collective-permute-start | bytes 442376 | tf_op jit(solution)/shard_map/ppermute | solution.py:129
  14.0 6.3 %copy-start.19 = (f32[4]{0:T(128)S(1)}, f32[4]{0:T(128)}, u32[]{:S(2)}) copy-start(f32[4]{0:T(128)} %constant.41.clone) | copy-start | bytes 52
  14.0 10.8 %collective-permute-start.4 = (f32[4,24,32]{0,2,1:T(8,128)S(1)}, f32[4,24,32]{0,2,1:T(8,128)S(1)}, u32[]{:S(2)}, u32[]{:S(2)}) collective-permute-start(f32[4,24,32]{0,2,1:T(8,128)S(1)} %copy.92), channel_id=1, source_target_pairs={{1,0},{2,1},{3,2},{4,3},{5,4},{6,5},{7,6},{0,7},{9,8},{10,9},{11,1... | collective-permute-start | bytes 36872 | tf_op jit(solution)/shard_map/ppermute | solution.py:144
  18.9 12.1 %collective-permute-start.3 = (f32[4,24,32]{0,2,1:T(8,128)S(1)}, f32[4,24,32]{0,2,1:T(8,128)S(1)}, u32[]{:S(2)}, u32[]{:S(2)}) collective-permute-start(f32[4,24,32]{0,2,1:T(8,128)S(1)} %copy.87), channel_id=1, source_target_pairs={{0,1},{1,2},{2,3},{3,4},{4,5},{5,6},{6,7},{7,0},{8,9},{9,10},{10,1... | collective-permute-start | bytes 36872 | tf_op jit(solution)/shard_map/ppermute | solution.py:143
  24.9 6.0 %copy-start.16 = (f32[4,24,32]{0,2,1:T(8,128)}, f32[4,24,32]{0,2,1:T(8,128)S(1)}, u32[]{:S(2)}) copy-start(f32[4,24,32]{0,2,1:T(8,128)S(1)} %collective-permute-done.4) | copy-start | bytes 36868
  41.0 34.3 %all-to-all-start.2 = ((f32[8,2,3,32,384]{4,3,2,1,0:T(8,128)}), f32[8,2,3,32,384]{4,3,2,1,0:T(8,128)S(1)}, u32[]{:S(2)}, u32[]{:S(2)}) async-start(f32[8,2,3,32,384]{4,3,2,1,0:T(8,128)} %shard_map.130), calls=%async_computation.2 | async-start | bytes 4718592 | tf_op jit(solution)/shard_map/all_to_all | solution.py:161
  75.4 39.5 %all-to-all-start = ((f32[8,2,3,32,384]{4,3,2,1,0:T(8,128)}), f32[8,2,3,32,384]{4,3,2,1,0:T(8,128)}, u32[]{:S(2)}, u32[]{:S(2)}) async-start(f32[8,2,3,32,384]{4,3,2,1,0:T(8,128)} %shard_map.129), calls=%async_computation | async-start | bytes 4718592 | tf_op jit(solution)/shard_map/all_to_all | solution.py:161
  84.3 1.7 copy-start.14
  86.0 1.7 copy-start.12
  87.7 1.7 copy-start.10
  89.5 1.7 copy-start.9
  114.9 40.0 %all-to-all-start.3 = ((f32[8,2,3,32,384]{4,3,2,1,0:T(8,128)}), f32[8,2,3,32,384]{4,3,2,1,0:T(8,128)}, u32[]{:S(2)}, u32[]{:S(2)}) async-start(f32[8,2,3,32,384]{4,3,2,1,0:T(8,128)} %pad_maximum_fusion.1), calls=%async_computation.3 | async-start | bytes 4718592 | tf_op jit(solution)/shard_map/all_to_all | solution.py:171
  125.3 2.4 %copy-start.15 = (f32[4,384,416,1,1]{1,2,3,4,0:T(8,128)S(1)}, f32[4,384,416,1,1]{1,2,3,4,0:T(8,128)}, u32[]{:S(2)}) copy-start(f32[4,384,416,1,1]{1,2,3,4,0:T(8,128)} %constant.49) | copy-start | bytes 7667716
  127.7 1.7 copy-start.13
  129.4 1.7 copy-start.11
  135.4 26.5 %copy-start.18 = (s32[32,16]{0,1:T(8,128)S(1)}, s32[32,16]{0,1:T(8,128)}, u32[]{:S(2)}) copy-start(s32[32,16]{0,1:T(8,128)} %param.14) | copy-start | bytes 6148
  154.9 35.3 %copy-start = (f32[8,2,3,32,384]{4,3,2,1,0:T(8,128)S(1)}, f32[8,2,3,32,384]{4,3,2,1,0:T(8,128)}, u32[]{:S(2)}) copy-start(f32[8,2,3,32,384]{4,3,2,1,0:T(8,128)} %shard_map.130) | copy-start | bytes 7077892
  154.9 35.3 %all-to-all-start.1 = ((f32[8,2,3,32,384]{4,3,2,1,0:T(8,128)}), f32[8,2,3,32,384]{4,3,2,1,0:T(8,128)}, u32[]{:S(2)}, u32[]{:S(2)}) async-start(f32[8,2,3,32,384]{4,3,2,1,0:T(8,128)} %pad_maximum_fusion), calls=%async_computation.1 | async-start | bytes 4718592 | tf_op jit(solution)/shard_map/all_to_all | solution.py:171
  196.0 1.7 copy-start.4
  197.7 2.0 %copy-start.8 = (f32[24,32,384]{2,1,0:T(8,128)S(1)}, f32[24,32,384]{2,1,0:T(8,128)}, u32[]{:S(2)}) copy-start(f32[24,32,384]{2,1,0:T(8,128)} %h_ref.3) | copy-start | bytes 3538948
  (5 other events, 6.3 us)

commit v2 on v1

v2 whole, which is shorter than its diff:
```python
import functools
import math

import jax
import jax.numpy as jnp
import numpy as np
from jax import lax
from jax.experimental import pallas as pl
from jax.experimental.pallas import tpu as pltpu
from jax.sharding import PartitionSpec as P

OMEGA = 30.0
KHALF = 208
LANES = 128


def geometry(total_rows):
    row = np.arange(-1, total_rows + 1)
    dist = np.maximum(np.minimum(row, total_rows - 1 - row), 0)
    cos_row = np.sin(np.pi * (dist + 0.5) / total_rows)
    face = np.arange(total_rows + 1)
    cos_face = np.sin(np.pi * np.minimum(face, total_rows - face) / total_rows)
    spin = -2.0 * OMEGA * np.cos(np.pi * (np.arange(total_rows) + 0.5) / total_rows)
    table = np.zeros((total_rows, 8))
    table[:, 0] = cos_row[1:-1]
    table[:, 1] = cos_row[:-2]
    table[:, 2] = cos_row[2:]
    table[:, 3] = cos_face[:-1]
    table[:, 4] = cos_face[1:]
    table[:, 5] = spin
    table[:, 6] = 1.0 / cos_row[1:-1]
    return table.astype(np.float32)


def fourier_tables(total):
    column = np.arange(total // 2)
    tables = []
    for odd in (0, 1):
        wave = 2 * np.arange(KHALF) + odd
        angle = (column[:, None] * wave[None, :] % total) * (2.0 * np.pi / total)
        tables.append(np.concatenate([np.cos(angle), np.sin(angle)], axis=1))
    return [table.astype(np.float32) for table in tables]


def copy_all(pairs, sems):
    copies = [pltpu.make_async_copy(src, dst, sems.at[i]) for i, (src, dst) in enumerate(pairs)]
    for copy in copies:
        copy.start()
    for copy in copies:
        copy.wait()


def pack_body(count, chunk, halo_chunks, rows, me_ref, *refs):
    fields = refs[:4]
    halo = refs[4] if halo_chunks else None
    outs, sems = refs[-count - 1 : -1], refs[-1]
    me = me_ref[0]
    pairs = []
    for step in range(count):
        level = lax.rem(me + step, count)
        for f in range(4):
            pairs.append((fields[f].at[chunk * count + level], outs[step].at[pl.ds(f * rows, rows)]))
        for k, c in enumerate(halo_chunks):
            pairs.append((halo.at[c * count + level], outs[step].at[pl.ds(4 * rows + 8 * k, 8)]))
    copy_all(pairs, sems)


def pack(count, chunk, halo_chunks, me, fields, halo):
    _, rows, cols = fields[0].shape
    height = 4 * rows + 8 * len(halo_chunks)
    anywhere = pl.BlockSpec(memory_space=pl.ANY)
    operands = list(fields) + ([halo] if halo_chunks else [])
    return pl.pallas_call(
        functools.partial(pack_body, count, chunk, halo_chunks, rows),
        in_specs=[pl.BlockSpec(memory_space=pltpu.SMEM)] + [anywhere] * len(operands),
        out_specs=[anywhere] * count,
        out_shape=[jax.ShapeDtypeStruct((height, cols), jnp.float32)] * count,
        scratch_shapes=[pltpu.SemaphoreType.DMA((count * (4 + len(halo_chunks)),))],
        cost_estimate=pl.CostEstimate(flops=0, bytes_accessed=8 * count * height * cols, transcendentals=0),
    )(me, *operands)


def place_body(count, chunk, rows, me_ref, *refs):
    blocks, outs, sems = refs[:count], refs[-5:-1], refs[-1]
    me = me_ref[0]
    pairs = []
    for step in range(count):
        level = chunk * count + lax.rem(me + count - step, count)
        for f in range(4):
            pairs.append((blocks[step].at[pl.ds(f * rows, rows)], outs[f].at[level]))
    copy_all(pairs, sems)


def place(chunk, me, blocks, earlier, shape):
    count = len(blocks)
    anywhere = pl.BlockSpec(memory_space=pl.ANY)
    operands = list(blocks) + list(earlier)
    return pl.pallas_call(
        functools.partial(place_body, count, chunk, shape[1]),
        in_specs=[pl.BlockSpec(memory_space=pltpu.SMEM)] + [anywhere] * len(operands),
        out_specs=[anywhere] * 4,
        out_shape=[jax.ShapeDtypeStruct(shape, jnp.float32)] * 4,
        scratch_shapes=[pltpu.SemaphoreType.DMA((4 * count,))],
        input_output_aliases={1 + count + f: f for f in range(4)} if earlier else {},
        cost_estimate=pl.CostEstimate(flops=0, bytes_accessed=32 * count * shape[1] * shape[2], transcendentals=0),
    )(me, *operands)


def lat_shift(x, amount, edge):
    size = x.shape[0]
    place = lax.broadcasted_iota(jnp.int32, x.shape, 0)
    at = size - 1 if amount < 0 else 0
    return jnp.where(place == at, edge, pltpu.roll(x, amount % size, 0))


def tend_body(count, rows, cols, dlon, dlat, where_ref, geo_ref, *refs):
    blocks, halos = refs[:count], refs[count : 2 * count]
    tend_ref, even_ref, odd_ref = refs[2 * count :]
    is_first, is_last = where_ref[0] == 1, where_ref[1] == 1
    geo = geo_ref[...]
    cs, cn = geo[:, 1:2], geo[:, 2:3]
    fs, fn, spin0, inv = geo[0:1, 3:4], geo[:, 4:5], geo[:, 5:6], geo[:, 6:7]
    wide = cols + 2 * LANES
    signs = (-1.0, -1.0, 1.0, 1.0)

    def mid(x):
        return x[:, LANES : LANES + cols]

    def east_of(x):
        return pltpu.roll(x, wide - 1, 1)

    def west_of(x):
        return pltpu.roll(x, 1, 1)

    for r in range(count):
        prev, here, nxt = blocks[r - 1], blocks[r], blocks[(r + 1) % count]
        across = blocks[(r + count // 2) % count]
        ext = []
        south, north = [], []
        for f in range(4):
            part = slice(f * rows, (f + 1) * rows)
            ext.append(jnp.concatenate([prev[part, cols - LANES :], here[part, :], nxt[part, :LANES]], axis=1))
            low, high = f * rows, (f + 1) * rows - 1
            south.append(jnp.where(is_first, signs[f] * across[low : low + 1, :], halos[r][f : f + 1, :]))
            north.append(jnp.where(is_last, signs[f] * across[high : high + 1, :], halos[r][4 + f : 5 + f, :]))
        ux, vx, px, hx = ext
        heat_x = px * hx
        energy_x = 0.5 * (ux * ux + vx * vx) + heat_x
        u, v, p, heat, energy = mid(ux), mid(vx), mid(px), mid(heat_x), mid(energy_x)
        out = slice(r * cols, (r + 1) * cols)

        zeta = (mid(east_of(vx)) - mid(west_of(vx))) * (0.5 / dlon)
        zeta -= (cn * lat_shift(u, -1, north[0]) - cs * lat_shift(u, 1, south[0])) * (0.5 / dlat)
        absolute = spin0 + zeta * inv
        edges = [0.5 * (q[0] * q[0] + q[1] * q[1]) + q[2] * q[3] for q in (south, north)]
        de_x = mid(east_of(energy_x)) - mid(west_of(energy_x))
        de_y = lat_shift(energy, -1, edges[1]) - lat_shift(energy, 1, edges[0])
        tend_ref[0:rows, out] = absolute * v - de_x * ((0.5 / dlon) * inv)
        tend_ref[rows : 2 * rows, out] = -absolute * u - de_y * (0.5 / dlat)

        a = 0.5 * (ux + east_of(ux))
        ap, am = jnp.maximum(a, 0.0), jnp.minimum(a, 0.0)
        flow_x = ap * px + am * east_of(px)
        hot_x = ap * heat_x + am * east_of(heat_x)
        b = 0.5 * (v + lat_shift(v, -1, north[1]))
        bp, bm = fn * jnp.maximum(b, 0.0), fn * jnp.minimum(b, 0.0)
        flow_y = bp * p + bm * lat_shift(p, -1, north[2])
        hot_y = bp * heat + bm * lat_shift(heat, -1, north[2] * north[3])
        b0 = 0.5 * (south[1] + v[0:1, :])
        bp0, bm0 = fs * jnp.maximum(b0, 0.0), fs * jnp.minimum(b0, 0.0)
        flow_y0 = bp0 * south[2] + bm0 * p[0:1, :]
        hot_y0 = bp0 * (south[2] * south[3]) + bm0 * heat[0:1, :]
        tend_ref[2 * rows : 3 * rows, out] = -inv * (
            (mid(flow_x) - mid(west_of(flow_x))) * (1.0 / dlon) + (flow_y - lat_shift(flow_y, 1, flow_y0)) * (1.0 / dlat)
        )
        tend_ref[3 * rows : 4 * rows, out] = -inv * (
            (mid(hot_x) - mid(west_of(hot_x))) * (1.0 / dlon) + (hot_y - lat_shift(hot_y, 1, hot_y0)) * (1.0 / dlat)
        )
    half = count * cols // 2
    for r in range(count // 2):
        near = tend_ref[:, r * cols : (r + 1) * cols]
        far = tend_ref[:, half + r * cols : half + (r + 1) * cols]
        even_ref[:, r * cols : (r + 1) * cols] = near + far
        odd_ref[:, r * cols : (r + 1) * cols] = near - far


def tendencies(rows, dlon, dlat, ends, geo, blocks, halo_blocks, halo_slot):
    count = len(blocks)
    cols = blocks[0].shape[1]
    full = count * cols
    high = 4 * rows
    return pl.pallas_call(
        functools.partial(tend_body, count, rows, cols, dlon, dlat),
        grid=(1,),
        in_specs=[pl.BlockSpec(memory_space=pltpu.SMEM), pl.BlockSpec((rows, 8), lambda g: (0, 0))]
        + [pl.BlockSpec((high, cols), lambda g: (0, 0))] * count
        + [pl.BlockSpec((8, cols), lambda g: (high // 8 + halo_slot, 0))] * count,
        out_specs=[
            pl.BlockSpec((high, full), lambda g: (0, 0)),
            pl.BlockSpec((high, full // 2), lambda g: (0, 0)),
            pl.BlockSpec((high, full // 2), lambda g: (0, 0)),
        ],
        out_shape=[
            jax.ShapeDtypeStruct((high, full), jnp.float32),
            jax.ShapeDtypeStruct((high, full // 2), jnp.float32),
            jax.ShapeDtypeStruct((high, full // 2), jnp.float32),
        ],
        compiler_params=pltpu.CompilerParams(vmem_limit_bytes=32 * 1024 * 1024),
        cost_estimate=pl.CostEstimate(flops=40 * high * full, bytes_accessed=12 * high * full, transcendentals=0),
    )(ends, geo, *blocks, *halo_blocks)


def update_body(count, rows, cols, step_size, listed_ref, tend_ref, even_ref, odd_ref, *refs):
    blocks, outs = refs[:count], refs[count:]
    listed = listed_ref[...] > 0
    half = count // 2
    for r in range(count):
        src = slice((r % half) * cols, (r % half + 1) * cols)
        for f in range(4):
            part = slice(f * rows, (f + 1) * rows)
            if r < half:
                smooth = even_ref[part, src] + odd_ref[part, src]
            else:
                smooth = even_ref[part, src] - odd_ref[part, src]
            chosen = jnp.where(listed, smooth, tend_ref[part, r * cols : (r + 1) * cols])
            base = blocks[r][part, :]
            if f == 3:
                base = base * blocks[r][2 * rows : 3 * rows, :]
            outs[r][part, :] = base + step_size * chosen


def updated(rows, step_size, listed, tend, even, odd, blocks):
    count = len(blocks)
    cols = blocks[0].shape[1]
    high = 4 * rows
    whole = lambda shape: pl.BlockSpec(shape, lambda g: (0, 0))
    return pl.pallas_call(
        functools.partial(update_body, count, rows, cols, step_size),
        grid=(1,),
        in_specs=[whole((rows, 1)), whole(tend.shape), whole(even.shape), whole(odd.shape)] + [whole((high, cols))] * count,
        out_specs=[whole((high, cols))] * count,
        out_shape=[jax.ShapeDtypeStruct((high, cols), jnp.float32)] * count,
        compiler_params=pltpu.CompilerParams(vmem_limit_bytes=32 * 1024 * 1024),
        cost_estimate=pl.CostEstimate(flops=4 * high * count * cols, bytes_accessed=16 * high * count * cols, transcendentals=0),
    )(listed, tend, even, odd, *blocks)


def per_device(u_wind, v_wind, thickness, theta, polar_rows, cutoffs):
    levels, rows, cols = u_wind.shape
    lat_count = lax.axis_size("lat")
    count = lax.axis_size("lon")
    lat_place = lax.axis_index("lat")
    total_rows = rows * lat_count
    total_cols = cols * count
    dlon = 2.0 * math.pi / total_cols
    dlat = math.pi / total_rows
    step_size = 0.25 * dlon
    first_row = lat_place * rows
    fields = (u_wind, v_wind, thickness, theta)
    me = lax.axis_index("lon").astype(jnp.int32).reshape(1)
    chunks = levels // count

    def exchanged(blocks):
        return [blocks[0]] + [
            lax.ppermute(blocks[step], "lon", [(i, (i + step) % count) for i in range(count)])
            for step in range(1, count)
        ]

    def circle(received):
        return [received[(count - r) % count] for r in range(count)]

    first = circle(exchanged(pack(count, 0, (), me, fields, None)))
    low_rows = jnp.stack([f[:, 0, :] for f in fields], axis=1)
    high_rows = jnp.stack([f[:, rows - 1, :] for f in fields], axis=1)
    south = lax.ppermute(high_rows, "lat", [(i, i + 1) for i in range(lat_count - 1)])
    north = lax.ppermute(low_rows, "lat", [(i + 1, i) for i in range(lat_count - 1)])
    halo = jnp.concatenate([south, north], axis=1)
    circles = [first]
    for c in range(1, chunks):
        carried = (0, 1) if c == 1 else (c,)
        circles.append(circle(exchanged(pack(count, c, carried, me, fields, halo))))
    halo_at = [(1, 0), (1, 1)] + [(c, 0) for c in range(2, chunks)]

    geo = lax.dynamic_slice_in_dim(jnp.asarray(geometry(total_rows)), first_row, rows, 0)
    own = first_row + jnp.arange(rows)
    listed = jnp.any(polar_rows.reshape(-1)[None, :] == own[:, None], axis=1)[:, None].astype(jnp.int32)
    limit = jnp.tile(lax.dynamic_slice_in_dim(cutoffs, first_row, rows, 0), 4)
    ends = jnp.stack([lat_place == 0, lat_place == lat_count - 1]).astype(jnp.int32)
    tables = [jnp.asarray(t) for t in fourier_tables(total_cols)]
    weights = []
    for odd in (0, 1):
        wave = 2 * jnp.arange(KHALF) + odd
        w = jnp.where(wave[None, :] == 0, 1.0, jnp.where(wave[None, :] <= limit[:, None], 2.0, 0.0)) / total_cols
        weights.append(jnp.concatenate([w, w], axis=1))

    done = ()
    high = lax.Precision.HIGH
    for c in range(chunks):
        source, slot = halo_at[c]
        tend, *sides = tendencies(rows, dlon, dlat, ends, geo, circles[c], circles[source], slot)
        smooth = []
        for x, table, weight in zip(sides, tables, weights):
            spectrum = jnp.dot(x, table, precision=high, preferred_element_type=jnp.float32) * weight
            smooth.append(jnp.dot(spectrum, table.T, precision=high, preferred_element_type=jnp.float32))
        fresh = updated(rows, step_size, listed, tend, *smooth, circles[c])
        done = place(c, me, exchanged(fresh), done, (levels, rows, cols))
    return tuple(done)


def solution(mesh):
    field = P(None, "lat", "lon")
    return jax.shard_map(
        per_device,
        mesh=mesh,
        in_specs=(field, field, field, field, P(), P()),
        out_specs=(field, field, field, field),
        check_vma=False,
    )
```

time: 203 us -> 483 us (2.38); the launches traced: 202 us -> 475 us
  Pallas kernels: 18.3 us -> 312 us
  waiting for transfers between devices: 98.2 us -> 28.1 us
  starting transfers between devices: 39 us -> 97.7 us
  other arithmetic: 17.6 us -> 1.52 us
  matrix products: 10.8 us -> 26.7 us
  local copies, waits for them, and re-layouts: 16.7 us -> 7.52 us
    pallas_call x2 -> x12, Pallas kernels: 18.3 us -> 312 us  [the longest x3 156 us: pack(): pl.pallas_call(functools.partial(pack_body, count, chunk, halo_chunks, ro...]
    all_to_all x4 -> x0, waiting for transfers between devices: 89.5 us -> none  [the longest x2 47.7 us: filtered(): return lax.all_to_all(out, 'lon', 0, 0, tiled=True)]
    ppermute x3 -> x42, starting transfers between devices: 5.14 us -> 90.7 us  [exchanged(): lax.ppermute(blocks[step], 'lon', [(i, (i + step) % count) for i in range...]
    all_to_all x4 -> x0, starting transfers between devices: 29.5 us -> none  [the longest x2 17.2 us: filtered(): return lax.all_to_all(out, 'lon', 0, 0, tiled=True)]
    ppermute x3 -> x42, waiting for transfers between devices: 8.71 us -> 28.1 us  [exchanged(): lax.ppermute(blocks[step], 'lon', [(i, (i + step) % count) for i in range...]
    dot_general x8 -> x12, matrix products: 10.8 us -> 26.7 us  [the longest x6 15.8 us: per_device(): jnp.dot(x, table, precision=high, preferred_element_type=jnp.float32)]
    unnamed x49 -> x83, local copies, waits for them, and re-layouts: 10.7 us -> 3.1 us
    select_n x2 -> x0, other arithmetic: 6.06 us -> none  [the longest x1 4.16 us: per_device(): chosen = jnp.where(listed, filtered(tend), tend)]
  transfers between devices with their start and end apart: 9 -> 44, of which waited for: 6 -> 10; matrix products, arithmetic and copies ran while one was open for 12% -> 6% of each run, Pallas kernels for 4% -> 44%
where the time goes in v2:
time: 483 us; the launch traced here: 475 us
  Pallas kernels  312 us (65%)
  starting transfers between devices  97.7 us (20%)
  waiting for transfers between devices  28.1 us (6%)
  matrix products  26.7 us (6%)
  local copies, waits for them, and re-layouts  7.52 us (2%)
    pallas_call x3, Pallas kernels, pack(): pl.pallas_call(functools.partial(pack_body, count, chunk, halo_chunks, ro...  156 us
    pallas_call x3, Pallas kernels, place(): pl.pallas_call(functools.partial(place_body, count, chunk, shape[1]), in_...  147 us
    ppermute x42, starting transfers between devices, exchanged(): lax.ppermute(blocks[step], 'lon', [(i, (i + step) % count) for i in range...  90.7 us
    ppermute x42, waiting for transfers between devices, exchanged(): lax.ppermute(blocks[step], 'lon', [(i, (i + step) % count) for i in range...  28.1 us
    dot_general x6, matrix products, per_device(): jnp.dot(x, table, precision=high, preferred_element_type=jnp.float32)  15.8 us
    dot_general x6, matrix products, per_device(): jnp.dot(spectrum, table.T, precision=high, preferred_element_type=jnp.flo...  10.9 us
  transfers between devices with their start and end apart: 44, of which 10 were waited for; matrix products, arithmetic and copies ran while one was open for 6% of the time, Pallas kernels for 44%

profile of v2, /device:TPU:16, one launch (start us, length us, event | category | flops | bytes accessed | tf_op | source)
XLA Modules:
  0.0 475.4 jit_solution(11964189923681825817)
XLA Ops:
  5.6 5.1 %collective-permute-start.1 = (f32[24,4,384]{2,1,0:T(4,128)S(1)}, f32[24,4,384]{2,1,0:T(4,128)S(1)}, u32[]{:S(2)}, u32[]{:S(2)}) collective-permute-start(f32[24,4,384]{2,1,0:T(4,128)S(1)} %pad_maximum_fusion.4), channel_id=1, source_target_pairs={{8,0},{16,8},{24,16},{32,24},{40,32},{48,40},{56,48},{64,56},{72,6... | collective-permute-start | bytes 442376 | tf_op jit(solution)/shard_map/ppermute | solution.py:276
  11.8 49.0 %shard_map.126 = (f32[128,384]{1,0:T(8,128)}, f32[128,384]{1,0:T(8,128)}, f32[128,384]{1,0:T(8,128)}, f32[128,384]{1,0:T(8,128)}, f32[128,384]{1,0:T(8,128)}, /*...) custom-call(s32[1]{0:T(128)} %bitcast.me_ref, f32[24,32,384]{2,1,0:T(8,128)} %refs_0_.5, ...), custom_call_target="tpu_custom_call" | custom-call | bytes 3145728 | tf_op jit(solution)/shard_map/pallas_call | solution.py:73
  62.6 52.1 %shard_map.120 = (f32[136,384]{1,0:T(8,128)}, f32[136,384]{1,0:T(8,128)}, f32[136,384]{1,0:T(8,128)}, f32[136,384]{1,0:T(8,128)}, f32[136,384]{1,0:T(8,128)}, /*...) custom-call(s32[1]{0:T(128)} %bitcast.me_ref, f32[24,32,384]{2,1,0:T(8,128)} %refs_0_.5, ...), custom_call_target="tpu_custom_call" | custom-call | bytes 3342336 | tf_op jit(solution)/shard_map/pallas_call | solution.py:73
  114.7 3.6 collective-permute-start.2
  123.9 7.9 %collective-permute-done.2.refs_1_.refs_9_ = f32[136,384]{1,0:T(8,128)S(1)} collective-permute-done((f32[136,384]{1,0:T(8,128)}, f32[136,384]{1,0:T(8,128)S(1)}, u32[]{:S(2)}, u32[]{:S(2)}) %collective-permute-start.2) | collective-permute-done | bytes 208928 | tf_op jit(solution)/shard_map/ppermute | solution.py:265
  131.7 3.5 collective-permute-start.8
  135.4 55.1 %shard_map.123 = (f32[144,384]{1,0:T(8,128)}, f32[144,384]{1,0:T(8,128)}, f32[144,384]{1,0:T(8,128)}, f32[144,384]{1,0:T(8,128)}, f32[144,384]{1,0:T(8,128)}, /*...) custom-call(s32[1]{0:T(128)} %bitcast.me_ref, f32[24,32,384]{2,1,0:T(8,128)} %refs_0_.5, ...), custom_call_target="tpu_custom_call" | custom-call | bytes 3538944 | tf_op jit(solution)/shard_map/pallas_call | solution.py:73
  191.8 2.9 collective-permute-start.31
  200.9 2.6 convolution_multiply_fusion.4
  223.2 4.8 %collective-permute-start.22 = (f32[144,384]{1,0:T(8,128)S(1)}, f32[144,384]{1,0:T(8,128)S(1)}, u32[]{:S(2)}, u32[]{:S(2)}) collective-permute-start(f32[144,384]{1,0:T(8,128)S(1)} %copy-done.28), channel_id=1, source_target_pairs={{0,1},{1,2},{2,3},{3,4},{4,5},{5,6},{6,7},{7,0},{8,9},{9,10},{10,1... | collective-permute-start | bytes 663560 | tf_op jit(solution)/shard_map/ppermute | solution.py:265
  231.0 3.0 collective-permute-start.10
  233.9 8.5 %collective-permute-done.19.refs_4_.refs_12_ = f32[144,384]{1,0:T(8,128)S(1)} collective-permute-done((f32[144,384]{1,0:T(8,128)S(1)}, f32[144,384]{1,0:T(8,128)S(1)}, u32[]{:S(2)}, u32[]{:S(2)}) %collective-permute-start.19) | collective-permute-done | bytes 221216 | tf_op jit(solution)/shard_map/ppermute | solution.py:265
  242.4 8.2 %collective-permute-start.11 = (f32[128,384]{1,0:T(8,128)S(1)}, f32[128,384]{1,0:T(8,128)S(1)}, u32[]{:S(2)}, u32[]{:S(2)}) collective-permute-start(f32[128,384]{1,0:T(8,128)S(1)} %get-tuple-element.83), channel_id=1, source_target_pairs={{0,3},{1,4},{2,5},{3,6},{4,7},{5,0},{6,1},{7,2},{8,11},{9,12},{10,... | collective-permute-start | bytes 589832 | tf_op jit(solution)/shard_map/ppermute | solution.py:265
  253.1 2.6 convolution_multiply_fusion
  265.0 3.3 collective-permute-start.39
  281.9 4.3 collective-permute-start.42
  290.5 3.6 collective-permute-start.25
  299.8 3.0 collective-permute-start.28
  303.5 3.7 collective-permute-done.25.refs_3_
  308.3 4.3 collective-permute-start.13
  312.6 12.1 %collective-permute-start.14 = (f32[128,384]{1,0:T(8,128)S(1)}, f32[128,384]{1,0:T(8,128)S(1)}, u32[]{:S(2)}, u32[]{:S(2)}) collective-permute-start(f32[128,384]{1,0:T(8,128)S(1)} %get-tuple-element.86), channel_id=1, source_target_pairs={{0,6},{1,7},{2,0},{3,1},{4,2},{5,3},{6,4},{7,5},{8,14},{9,15},{10,... | collective-permute-start | bytes 589832 | tf_op jit(solution)/shard_map/ppermute | solution.py:265
  326.8 49.0 %shard_map.129 = (f32[24,32,384]{2,1,0:T(8,128)}, f32[24,32,384]{2,1,0:T(8,128)}, f32[24,32,384]{2,1,0:T(8,128)}, f32[24,32,384]{2,1,0:T(8,128)}) custom-call(s32[1]{0:T(128)} %bitcast.me_ref, f32[128,384]{1,0:T(8,128)} %copy-done.5, f32[128,384]{1,0:T(8,128)} %copy-done.21, f32[128,384]{1,0:T(8,128)} %copy-done.22, f32[128,384]{1,0:T(8,128)} %copy-done.23, ...), custom_call_target="tpu_custom_call" | custom-call | bytes 3145728 | tf_op jit(solution)/shard_map/pallas_call | solution.py:98
  375.9 49.0 %shard_map.130 = (f32[24,32,384]{2,1,0:T(8,128)}, f32[24,32,384]{2,1,0:T(8,128)}, f32[24,32,384]{2,1,0:T(8,128)}, f32[24,32,384]{2,1,0:T(8,128)}) custom-call(s32[1]{0:T(128)} %bitcast.me_ref, f32[128,384]{1,0:T(8,128)} %copy-done.4, f32[128,384]{1,0:T(8,128)} %copy-done.10, ...), custom_call_target="tpu_custom_call", output_to_operand_aliasing={{0}: (9, {}), {1}: (10, {}), {2}: (11, {}), {3}: (12, {})} | custom-call | bytes 3145728 | tf_op jit(solution)/shard_map/pallas_call | solution.py:98
  425.9 49.0 %shard_map.131 = (f32[24,32,384]{2,1,0:T(8,128)}, f32[24,32,384]{2,1,0:T(8,128)}, f32[24,32,384]{2,1,0:T(8,128)}, f32[24,32,384]{2,1,0:T(8,128)}) custom-call(s32[1]{0:T(128)} %bitcast.me_ref, f32[128,384]{1,0:T(8,128)} %copy-done.3, ...), custom_call_target="tpu_custom_call", output_to_operand_aliasing={{0}: (9, {}), {1}: (10, {}), {2}: (11, {}), {3}: (12, {})} | custom-call | bytes 3145728 | tf_op jit(solution)/shard_map/pallas_call | solution.py:98
  (189 shorter events, 83.0 us)
Async XLA Ops:
  3.5 58.3 %collective-permute-start = (f32[24,4,384]{2,1,0:T(4,128)S(1)}, f32[24,4,384]{2,1,0:T(4,128)S(1)}, u32[]{:S(2)}, u32[]{:S(2)}) collective-permute-start(f32[24,4,384]{2,1,0:T(4,128)S(1)} %pad_maximum_fusion.3), channel_id=1, source_target_pairs={{0,8},{8,16},{16,24},{24,32},{32,40},{40,48},{48,56},{56,64},{64,7... | collective-permute-start | bytes 442376 | tf_op jit(solution)/shard_map/ppermute | solution.py:275
  5.6 56.3 %collective-permute-start.1 = (f32[24,4,384]{2,1,0:T(4,128)S(1)}, f32[24,4,384]{2,1,0:T(4,128)S(1)}, u32[]{:S(2)}, u32[]{:S(2)}) collective-permute-start(f32[24,4,384]{2,1,0:T(4,128)S(1)} %pad_maximum_fusion.4), channel_id=1, source_target_pairs={{8,0},{16,8},{24,16},{32,24},{40,32},{48,40},{56,48},{64,56},{72,6... | collective-permute-start | bytes 442376 | tf_op jit(solution)/shard_map/ppermute | solution.py:276
  119.9 70.7 %collective-permute-start.4 = (f32[136,384]{1,0:T(8,128)}, f32[136,384]{1,0:T(8,128)S(1)}, u32[]{:S(2)}, u32[]{:S(2)}) collective-permute-start(f32[136,384]{1,0:T(8,128)} %get-tuple-element.72), channel_id=1, source_target_pairs={{0,5},{1,6},{2,7},{3,0},{4,1},{5,2},{6,3},{7,4},{8,13},{9,14},{10,... | collective-permute-start | bytes 626696 | tf_op jit(solution)/shard_map/ppermute | solution.py:265
  121.0 70.9 %collective-permute-start.5 = (f32[136,384]{1,0:T(8,128)}, f32[136,384]{1,0:T(8,128)S(1)}, u32[]{:S(2)}, u32[]{:S(2)}) collective-permute-start(f32[136,384]{1,0:T(8,128)} %get-tuple-element.73), channel_id=1, source_target_pairs={{0,4},{1,5},{2,6},{3,7},{4,0},{5,1},{6,2},{7,3},{8,12},{9,13},{10,... | collective-permute-start | bytes 626696 | tf_op jit(solution)/shard_map/ppermute | solution.py:265
  122.2 72.5 %collective-permute-start.6 = (f32[136,384]{1,0:T(8,128)}, f32[136,384]{1,0:T(8,128)S(1)}, u32[]{:S(2)}, u32[]{:S(2)}) collective-permute-start(f32[136,384]{1,0:T(8,128)} %get-tuple-element.74), channel_id=1, source_target_pairs={{0,3},{1,4},{2,5},{3,6},{4,7},{5,0},{6,1},{7,2},{8,11},{9,12},{10,... | collective-permute-start | bytes 626696 | tf_op jit(solution)/shard_map/ppermute | solution.py:265
  131.7 63.1 %collective-permute-start.7 = (f32[136,384]{1,0:T(8,128)}, f32[136,384]{1,0:T(8,128)S(1)}, u32[]{:S(2)}, u32[]{:S(2)}) collective-permute-start(f32[136,384]{1,0:T(8,128)} %get-tuple-element.75), channel_id=1, source_target_pairs={{0,2},{1,3},{2,4},{3,5},{4,6},{5,7},{6,0},{7,1},{8,10},{9,11},{10,... | collective-permute-start | bytes 626696 | tf_op jit(solution)/shard_map/ppermute | solution.py:265
  131.7 64.4 %collective-permute-start.8 = (f32[136,384]{1,0:T(8,128)}, f32[136,384]{1,0:T(8,128)S(1)}, u32[]{:S(2)}, u32[]{:S(2)}) collective-permute-start(f32[136,384]{1,0:T(8,128)} %get-tuple-element.76), channel_id=1, source_target_pairs={{0,1},{1,2},{2,3},{3,4},{4,5},{5,6},{6,7},{7,0},{8,9},{9,10},{10,1... | collective-permute-start | bytes 626696 | tf_op jit(solution)/shard_map/ppermute | solution.py:265
  196.2 18.9 %collective-permute-start.34 = (f32[128,384]{1,0:T(8,128)S(1)}, f32[128,384]{1,0:T(8,128)S(1)}, u32[]{:S(2)}, u32[]{:S(2)}) collective-permute-start(f32[128,384]{1,0:T(8,128)S(1)} %copy-done.37), channel_id=1, source_target_pairs={{0,3},{1,4},{2,5},{3,6},{4,7},{5,0},{6,1},{7,2},{8,11},{9,12},{10,... | collective-permute-start | bytes 589832 | tf_op jit(solution)/shard_map/ppermute | solution.py:265
  217.2 25.2 %collective-permute-start.19 = (f32[144,384]{1,0:T(8,128)S(1)}, f32[144,384]{1,0:T(8,128)S(1)}, u32[]{:S(2)}, u32[]{:S(2)}) collective-permute-start(f32[144,384]{1,0:T(8,128)S(1)} %copy-done.31), channel_id=1, source_target_pairs={{0,4},{1,5},{2,6},{3,7},{4,0},{5,1},{6,2},{7,3},{8,12},{9,13},{10,... | collective-permute-start | bytes 663560 | tf_op jit(solution)/shard_map/ppermute | solution.py:265
  218.6 32.0 %collective-permute-start.20 = (f32[144,384]{1,0:T(8,128)S(1)}, f32[144,384]{1,0:T(8,128)S(1)}, u32[]{:S(2)}, u32[]{:S(2)}) collective-permute-start(f32[144,384]{1,0:T(8,128)S(1)} %copy-done.30), channel_id=1, source_target_pairs={{0,3},{1,4},{2,5},{3,6},{4,7},{5,0},{6,1},{7,2},{8,11},{9,12},{10,... | collective-permute-start | bytes 663560 | tf_op jit(solution)/shard_map/ppermute | solution.py:265
  221.1 29.6 %collective-permute-start.21 = (f32[144,384]{1,0:T(8,128)S(1)}, f32[144,384]{1,0:T(8,128)S(1)}, u32[]{:S(2)}, u32[]{:S(2)}) collective-permute-start(f32[144,384]{1,0:T(8,128)S(1)} %copy-done.29), channel_id=1, source_target_pairs={{0,2},{1,3},{2,4},{3,5},{4,6},{5,7},{6,0},{7,1},{8,10},{9,11},{10,... | collective-permute-start | bytes 663560 | tf_op jit(solution)/shard_map/ppermute | solution.py:265
  223.2 27.5 %collective-permute-start.22 = (f32[144,384]{1,0:T(8,128)S(1)}, f32[144,384]{1,0:T(8,128)S(1)}, u32[]{:S(2)}, u32[]{:S(2)}) collective-permute-start(f32[144,384]{1,0:T(8,128)S(1)} %copy-done.28), channel_id=1, source_target_pairs={{0,1},{1,2},{2,3},{3,4},{4,5},{5,6},{6,7},{7,0},{8,9},{9,10},{10,1... | collective-permute-start | bytes 663560 | tf_op jit(solution)/shard_map/ppermute | solution.py:265
  231.0 47.0 %collective-permute-start.10 = (f32[128,384]{1,0:T(8,128)S(1)}, f32[128,384]{1,0:T(8,128)S(1)}, u32[]{:S(2)}, u32[]{:S(2)}) collective-permute-start(f32[128,384]{1,0:T(8,128)S(1)} %get-tuple-element.82), channel_id=1, source_target_pairs={{0,2},{1,3},{2,4},{3,5},{4,6},{5,7},{6,0},{7,1},{8,10},{9,11},{10,... | collective-permute-start | bytes 589832 | tf_op jit(solution)/shard_map/ppermute | solution.py:265
  242.4 39.4 %collective-permute-start.11 = (f32[128,384]{1,0:T(8,128)S(1)}, f32[128,384]{1,0:T(8,128)S(1)}, u32[]{:S(2)}, u32[]{:S(2)}) collective-permute-start(f32[128,384]{1,0:T(8,128)S(1)} %get-tuple-element.83), channel_id=1, source_target_pairs={{0,3},{1,4},{2,5},{3,6},{4,7},{5,0},{6,1},{7,2},{8,11},{9,12},{10,... | collective-permute-start | bytes 589832 | tf_op jit(solution)/shard_map/ppermute | solution.py:265
  262.4 19.4 %collective-permute-start.37 = (f32[128,384]{1,0:T(8,128)S(1)}, f32[128,384]{1,0:T(8,128)S(1)}, u32[]{:S(2)}, u32[]{:S(2)}) collective-permute-start(f32[128,384]{1,0:T(8,128)S(1)} %get-tuple-element.119), channel_id=1, source_target_pairs={{0,1},{1,2},{2,3},{3,4},{4,5},{5,6},{6,7},{7,0},{8,9},{9,10},{10,1... | collective-permute-start | bytes 589832 | tf_op jit(solution)/shard_map/ppermute | solution.py:265
  264.2 21.9 %collective-permute-start.38 = (f32[128,384]{1,0:T(8,128)S(1)}, f32[128,384]{1,0:T(8,128)S(1)}, u32[]{:S(2)}, u32[]{:S(2)}) collective-permute-start(f32[128,384]{1,0:T(8,128)S(1)} %get-tuple-element.120), channel_id=1, source_target_pairs={{0,2},{1,3},{2,4},{3,5},{4,6},{5,7},{6,0},{7,1},{8,10},{9,11},{10,... | collective-permute-start | bytes 589832 | tf_op jit(solution)/shard_map/ppermute | solution.py:265
  265.0 21.4 %collective-permute-start.39 = (f32[128,384]{1,0:T(8,128)S(1)}, f32[128,384]{1,0:T(8,128)S(1)}, u32[]{:S(2)}, u32[]{:S(2)}) collective-permute-start(f32[128,384]{1,0:T(8,128)S(1)} %get-tuple-element.121), channel_id=1, source_target_pairs={{0,3},{1,4},{2,5},{3,6},{4,7},{5,0},{6,1},{7,2},{8,11},{9,12},{10,... | collective-permute-start | bytes 589832 | tf_op jit(solution)/shard_map/ppermute | solution.py:265
  299.8 24.9 %collective-permute-start.28 = (f32[128,384]{1,0:T(8,128)S(1)}, f32[128,384]{1,0:T(8,128)S(1)}, u32[]{:S(2)}, u32[]{:S(2)}) collective-permute-start(f32[128,384]{1,0:T(8,128)S(1)} %get-tuple-element.105), channel_id=1, source_target_pairs={{0,6},{1,7},{2,0},{3,1},{4,2},{5,3},{6,4},{7,5},{8,14},{9,15},{10,... | collective-permute-start | bytes 589832 | tf_op jit(solution)/shard_map/ppermute | solution.py:265
  303.5 21.2 %collective-permute-start.29 = (f32[128,384]{1,0:T(8,128)S(1)}, f32[128,384]{1,0:T(8,128)S(1)}, u32[]{:S(2)}, u32[]{:S(2)}) collective-permute-start(f32[128,384]{1,0:T(8,128)S(1)} %get-tuple-element.106), channel_id=1, source_target_pairs={{0,7},{1,0},{2,1},{3,2},{4,3},{5,4},{6,5},{7,6},{8,15},{9,8},{10,9... | collective-permute-start | bytes 589832 | tf_op jit(solution)/shard_map/ppermute | solution.py:265
  307.3 117.7 %collective-permute-start.12 = (f32[128,384]{1,0:T(8,128)S(1)}, f32[128,384]{1,0:T(8,128)S(1)}, u32[]{:S(2)}, u32[]{:S(2)}) collective-permute-start(f32[128,384]{1,0:T(8,128)S(1)} %get-tuple-element.84), channel_id=1, source_target_pairs={{0,4},{1,5},{2,6},{3,7},{4,0},{5,1},{6,2},{7,3},{8,12},{9,13},{10,... | collective-permute-start | bytes 589832 | tf_op jit(solution)/shard_map/ppermute | solution.py:265
  308.3 116.7 %collective-permute-start.13 = (f32[128,384]{1,0:T(8,128)S(1)}, f32[128,384]{1,0:T(8,128)S(1)}, u32[]{:S(2)}, u32[]{:S(2)}) collective-permute-start(f32[128,384]{1,0:T(8,128)S(1)} %get-tuple-element.85), channel_id=1, source_target_pairs={{0,5},{1,6},{2,7},{3,0},{4,1},{5,2},{6,3},{7,4},{8,13},{9,14},{10,... | collective-permute-start | bytes 589832 | tf_op jit(solution)/shard_map/ppermute | solution.py:265
  312.6 112.4 %collective-permute-start.14 = (f32[128,384]{1,0:T(8,128)S(1)}, f32[128,384]{1,0:T(8,128)S(1)}, u32[]{:S(2)}, u32[]{:S(2)}) collective-permute-start(f32[128,384]{1,0:T(8,128)S(1)} %get-tuple-element.86), channel_id=1, source_target_pairs={{0,6},{1,7},{2,0},{3,1},{4,2},{5,3},{6,4},{7,5},{8,14},{9,15},{10,... | collective-permute-start | bytes 589832 | tf_op jit(solution)/shard_map/ppermute | solution.py:265
  324.7 100.3 %collective-permute-start.15 = (f32[128,384]{1,0:T(8,128)S(1)}, f32[128,384]{1,0:T(8,128)S(1)}, u32[]{:S(2)}, u32[]{:S(2)}) collective-permute-start(f32[128,384]{1,0:T(8,128)S(1)} %get-tuple-element.87), channel_id=1, source_target_pairs={{0,7},{1,0},{2,1},{3,2},{4,3},{5,4},{6,5},{7,6},{8,15},{9,8},{10,9... | collective-permute-start | bytes 589832 | tf_op jit(solution)/shard_map/ppermute | solution.py:265
  324.7 100.3 %collective-permute-start.9 = (f32[128,384]{1,0:T(8,128)S(1)}, f32[128,384]{1,0:T(8,128)}, u32[]{:S(2)}, u32[]{:S(2)}) collective-permute-start(f32[128,384]{1,0:T(8,128)S(1)} %get-tuple-element.81), channel_id=1, source_target_pairs={{0,1},{1,2},{2,3},{3,4},{4,5},{5,6},{6,7},{7,0},{8,9},{9,10},{10,1... | collective-permute-start | bytes 589832 | tf_op jit(solution)/shard_map/ppermute | solution.py:265
  (61 other events, 1668.7 us)

commit v3 on v2

v3 whole, which is shorter than its diff:
```python
import functools
import math

import jax
import jax.numpy as jnp
import numpy as np
from jax import lax
from jax.experimental import pallas as pl
from jax.experimental.pallas import tpu as pltpu
from jax.sharding import PartitionSpec as P

OMEGA = 30.0
KHALF = 208
LANES = 128


def geometry(total_rows):
    row = np.arange(-1, total_rows + 1)
    dist = np.maximum(np.minimum(row, total_rows - 1 - row), 0)
    cos_row = np.sin(np.pi * (dist + 0.5) / total_rows)
    face = np.arange(total_rows + 1)
    cos_face = np.sin(np.pi * np.minimum(face, total_rows - face) / total_rows)
    spin = -2.0 * OMEGA * np.cos(np.pi * (np.arange(total_rows) + 0.5) / total_rows)
    table = np.zeros((total_rows, 8))
    table[:, 0] = cos_row[1:-1]
    table[:, 1] = cos_row[:-2]
    table[:, 2] = cos_row[2:]
    table[:, 3] = cos_face[:-1]
    table[:, 4] = cos_face[1:]
    table[:, 5] = spin
    table[:, 6] = 1.0 / cos_row[1:-1]
    return table.astype(np.float32)


def fourier_tables(total):
    column = np.arange(total // 2)
    tables = []
    for odd in (0, 1):
        wave = 2 * np.arange(KHALF) + odd
        angle = (column[:, None] * wave[None, :] % total) * (2.0 * np.pi / total)
        tables.append(np.concatenate([np.cos(angle), np.sin(angle)], axis=1))
    return [table.astype(np.float32) for table in tables]


def copy_all(pairs, sems):
    copies = [pltpu.make_async_copy(src, dst, sems.at[i]) for i, (src, dst) in enumerate(pairs)]
    for copy in copies:
        copy.start()
    for copy in copies:
        copy.wait()


def pack_body(first, per, rows, *refs):
    fields, out, sems = refs[:4], refs[4], refs[5]
    count = out.shape[0]
    pairs = []
    for k in range(per):
        for f in range(4):
            src = fields[f].at[pl.ds(first + k * count, count)]
            pairs.append((src, out.at[:, pl.ds((4 * k + f) * rows, rows), :]))
    copy_all(pairs, sems)


def pack(count, first, per, fields):
    _, rows, cols = fields[0].shape
    shape = (count, 4 * per * rows, cols)
    return pl.pallas_call(
        functools.partial(pack_body, first, per, rows),
        in_specs=[pl.BlockSpec(memory_space=pl.ANY)] * 4,
        out_specs=pl.BlockSpec(memory_space=pltpu.VMEM),
        out_shape=jax.ShapeDtypeStruct(shape, jnp.float32),
        scratch_shapes=[pltpu.SemaphoreType.DMA((4 * per,))],
        compiler_params=pltpu.CompilerParams(vmem_limit_bytes=32 * 1024 * 1024),
        cost_estimate=pl.CostEstimate(flops=0, bytes_accessed=8 * math.prod(shape), transcendentals=0),
    )(*fields)


def place_body(first, per, rows, *refs):
    got, outs, sems = refs[0], refs[-5:-1], refs[-1]
    count = got.shape[0]
    pairs = []
    for k in range(per):
        for f in range(4):
            src = got.at[:, pl.ds((4 * k + f) * rows, rows), :]
            pairs.append((src, outs[f].at[pl.ds(first + k * count, count)]))
    copy_all(pairs, sems)


def place(first, per, got, earlier, shape):
    return pl.pallas_call(
        functools.partial(place_body, first, per, shape[1]),
        in_specs=[pl.BlockSpec(memory_space=pltpu.VMEM)] + [pl.BlockSpec(memory_space=pl.ANY)] * len(earlier),
        out_specs=[pl.BlockSpec(memory_space=pl.ANY)] * 4,
        out_shape=[jax.ShapeDtypeStruct(shape, jnp.float32)] * 4,
        scratch_shapes=[pltpu.SemaphoreType.DMA((4 * per,))],
        input_output_aliases={1 + f: f for f in range(4)} if earlier else {},
        compiler_params=pltpu.CompilerParams(vmem_limit_bytes=32 * 1024 * 1024),
        cost_estimate=pl.CostEstimate(flops=0, bytes_accessed=8 * got.size, transcendentals=0),
    )(got, *earlier)


def lat_shift(x, amount, edge):
    size = x.shape[0]
    place = lax.broadcasted_iota(jnp.int32, x.shape, 0)
    at = size - 1 if amount < 0 else 0
    return jnp.where(place == at, edge, pltpu.roll(x, amount % size, 0))


def tend_body(count, rows, cols, dlon, dlat, where_ref, geo_ref, got_ref, south_ref, north_ref, *refs):
    tend_ref, even_ref, odd_ref = refs
    blocks = [got_ref.at[r] for r in range(count)]
    is_first, is_last = where_ref[0] == 1, where_ref[1] == 1
    geo = geo_ref[...]
    cs, cn = geo[:, 1:2], geo[:, 2:3]
    fs, fn, spin0, inv = geo[0:1, 3:4], geo[:, 4:5], geo[:, 5:6], geo[:, 6:7]
    wide = cols + 2 * LANES
    signs = (-1.0, -1.0, 1.0, 1.0)

    def mid(x):
        return x[:, LANES : LANES + cols]

    def east_of(x):
        return pltpu.roll(x, wide - 1, 1)

    def west_of(x):
        return pltpu.roll(x, 1, 1)

    for r in range(count):
        prev, here, nxt = blocks[r - 1], blocks[r], blocks[(r + 1) % count]
        across = blocks[(r + count // 2) % count]
        ext = []
        south, north = [], []
        for f in range(4):
            part = slice(f * rows, (f + 1) * rows)
            ext.append(jnp.concatenate([prev[part, cols - LANES :], here[part, :], nxt[part, :LANES]], axis=1))
            low, high = f * rows, (f + 1) * rows - 1
            south.append(jnp.where(is_first, signs[f] * across[low : low + 1, :], south_ref[r, 0, f : f + 1, :]))
            north.append(jnp.where(is_last, signs[f] * across[high : high + 1, :], north_ref[r, 0, f : f + 1, :]))
        ux, vx, px, hx = ext
        heat_x = px * hx
        energy_x = 0.5 * (ux * ux + vx * vx) + heat_x
        u, v, p, heat, energy = mid(ux), mid(vx), mid(px), mid(heat_x), mid(energy_x)
        out = slice(r * cols, (r + 1) * cols)

        zeta = (mid(east_of(vx)) - mid(west_of(vx))) * (0.5 / dlon)
        zeta -= (cn * lat_shift(u, -1, north[0]) - cs * lat_shift(u, 1, south[0])) * (0.5 / dlat)
        absolute = spin0 + zeta * inv
        edges = [0.5 * (q[0] * q[0] + q[1] * q[1]) + q[2] * q[3] for q in (south, north)]
        de_x = mid(east_of(energy_x)) - mid(west_of(energy_x))
        de_y = lat_shift(energy, -1, edges[1]) - lat_shift(energy, 1, edges[0])
        tend_ref[0:rows, out] = absolute * v - de_x * ((0.5 / dlon) * inv)
        tend_ref[rows : 2 * rows, out] = -absolute * u - de_y * (0.5 / dlat)

        a = 0.5 * (ux + east_of(ux))
        ap, am = jnp.maximum(a, 0.0), jnp.minimum(a, 0.0)
        flow_x = ap * px + am * east_of(px)
        hot_x = ap * heat_x + am * east_of(heat_x)
        b = 0.5 * (v + lat_shift(v, -1, north[1]))
        bp, bm = fn * jnp.maximum(b, 0.0), fn * jnp.minimum(b, 0.0)
        flow_y = bp * p + bm * lat_shift(p, -1, north[2])
        hot_y = bp * heat + bm * lat_shift(heat, -1, north[2] * north[3])
        b0 = 0.5 * (south[1] + v[0:1, :])
        bp0, bm0 = fs * jnp.maximum(b0, 0.0), fs * jnp.minimum(b0, 0.0)
        flow_y0 = bp0 * south[2] + bm0 * p[0:1, :]
        hot_y0 = bp0 * (south[2] * south[3]) + bm0 * heat[0:1, :]
        tend_ref[2 * rows : 3 * rows, out] = -inv * (
            (mid(flow_x) - mid(west_of(flow_x))) * (1.0 / dlon) + (flow_y - lat_shift(flow_y, 1, flow_y0)) * (1.0 / dlat)
        )
        tend_ref[3 * rows : 4 * rows, out] = -inv * (
            (mid(hot_x) - mid(west_of(hot_x))) * (1.0 / dlon) + (hot_y - lat_shift(hot_y, 1, hot_y0)) * (1.0 / dlat)
        )
    half = count * cols // 2
    for r in range(count // 2):
        near = tend_ref[:, r * cols : (r + 1) * cols]
        far = tend_ref[:, half + r * cols : half + (r + 1) * cols]
        even_ref[:, r * cols : (r + 1) * cols] = near + far
        odd_ref[:, r * cols : (r + 1) * cols] = near - far


def tendencies(rows, dlon, dlat, ends, geo, got, south, north):
    count, height, cols = got.shape
    full = count * cols
    high = 4 * rows
    halo = pl.BlockSpec((count, 1, 4, cols), lambda k: (0, k, 0, 0))
    return pl.pallas_call(
        functools.partial(tend_body, count, rows, cols, dlon, dlat),
        grid=(height // high,),
        in_specs=[
            pl.BlockSpec(memory_space=pltpu.SMEM),
            pl.BlockSpec((rows, 8), lambda k: (0, 0)),
            pl.BlockSpec((count, high, cols), lambda k: (0, k, 0)),
            halo,
            halo,
        ],
        out_specs=[
            pl.BlockSpec((high, full), lambda k: (k, 0)),
            pl.BlockSpec((high, full // 2), lambda k: (k, 0)),
            pl.BlockSpec((high, full // 2), lambda k: (k, 0)),
        ],
        out_shape=[
            jax.ShapeDtypeStruct((height, full), jnp.float32),
            jax.ShapeDtypeStruct((height, full // 2), jnp.float32),
            jax.ShapeDtypeStruct((height, full // 2), jnp.float32),
        ],
        compiler_params=pltpu.CompilerParams(vmem_limit_bytes=32 * 1024 * 1024),
        cost_estimate=pl.CostEstimate(flops=40 * height * full, bytes_accessed=12 * height * full, transcendentals=0),
    )(ends, geo, got, south, north)


def update_body(count, rows, cols, step_size, listed_ref, tend_ref, even_ref, odd_ref, got_ref, out_ref):
    listed = listed_ref[...] > 0
    half = count // 2
    for r in range(count):
        src = slice((r % half) * cols, (r % half + 1) * cols)
        for f in range(4):
            part = slice(f * rows, (f + 1) * rows)
            if r < half:
                smooth = even_ref[part, src] + odd_ref[part, src]
            else:
                smooth = even_ref[part, src] - odd_ref[part, src]
            chosen = jnp.where(listed, smooth, tend_ref[part, r * cols : (r + 1) * cols])
            base = got_ref[r, part, :]
            if f == 3:
                base = base * got_ref[r, 2 * rows : 3 * rows, :]
            out_ref[r, part, :] = base + step_size * chosen


def updated(rows, step_size, listed, tend, even, odd, got):
    count, height, cols = got.shape
    high = 4 * rows
    circles = pl.BlockSpec((count, high, cols), lambda k: (0, k, 0))
    flat = lambda width: pl.BlockSpec((high, width), lambda k: (k, 0))
    return pl.pallas_call(
        functools.partial(update_body, count, rows, cols, step_size),
        grid=(height // high,),
        in_specs=[
            pl.BlockSpec((rows, 1), lambda k: (0, 0)),
            flat(count * cols),
            flat(count * cols // 2),
            flat(count * cols // 2),
            circles,
        ],
        out_specs=circles,
        out_shape=jax.ShapeDtypeStruct(got.shape, jnp.float32),
        compiler_params=pltpu.CompilerParams(vmem_limit_bytes=32 * 1024 * 1024),
        cost_estimate=pl.CostEstimate(flops=4 * got.size, bytes_accessed=16 * got.size, transcendentals=0),
    )(listed, tend, even, odd, got)


def per_device(u_wind, v_wind, thickness, theta, polar_rows, cutoffs):
    levels, rows, cols = u_wind.shape
    lat_count = lax.axis_size("lat")
    count = lax.axis_size("lon")
    lat_place = lax.axis_index("lat")
    total_rows = rows * lat_count
    total_cols = cols * count
    dlon = 2.0 * math.pi / total_cols
    dlat = math.pi / total_rows
    step_size = 0.25 * dlon
    first_row = lat_place * rows
    fields = (u_wind, v_wind, thickness, theta)
    spread = levels // count
    chunks = [(0, 1), (count, spread - 1)]

    def exchanged(x):
        return lax.all_to_all(x, "lon", 0, 0, tiled=True)

    geo = lax.dynamic_slice_in_dim(jnp.asarray(geometry(total_rows)), first_row, rows, 0)
    own = first_row + jnp.arange(rows)
    listed = jnp.any(polar_rows.reshape(-1)[None, :] == own[:, None], axis=1)[:, None].astype(jnp.int32)
    limit = lax.dynamic_slice_in_dim(cutoffs, first_row, rows, 0)
    ends = jnp.stack([lat_place == 0, lat_place == lat_count - 1]).astype(jnp.int32)
    tables = [jnp.asarray(t) for t in fourier_tables(total_cols)]
    weights = []
    for odd in (0, 1):
        wave = 2 * jnp.arange(KHALF) + odd
        w = jnp.where(wave[None, :] == 0, 1.0, jnp.where(wave[None, :] <= limit[:, None], 2.0, 0.0)) / total_cols
        weights.append(jnp.concatenate([w, w], axis=1))

    circles = [exchanged(pack(count, first, per, fields)) for first, per in chunks]
    high = lax.Precision.HIGH
    done = ()
    for got, (first, per) in zip(circles, chunks):
        split = got.reshape(count, per, 4, rows, cols)
        south = lax.ppermute(split[:, :, :, rows - 1], "lat", [(i, i + 1) for i in range(lat_count - 1)])
        north = lax.ppermute(split[:, :, :, 0], "lat", [(i + 1, i) for i in range(lat_count - 1)])
        tend, *sides = tendencies(rows, dlon, dlat, ends, geo, got, south, north)
        smooth = []
        for x, table, weight in zip(sides, tables, weights):
            spectrum = jnp.dot(x, table, precision=high, preferred_element_type=jnp.float32)
            spectrum = spectrum * jnp.tile(weight, (4 * per, 1))
            smooth.append(jnp.dot(spectrum, table.T, precision=high, preferred_element_type=jnp.float32))
        fresh = exchanged(updated(rows, step_size, listed, tend, *smooth, got))
        done = place(first, per, fresh, done, (levels, rows, cols))
    return tuple(done)


def solution(mesh):
    field = P(None, "lat", "lon")
    return jax.shard_map(
        per_device,
        mesh=mesh,
        in_specs=(field, field, field, field, P(), P()),
        out_specs=(field, field, field, field),
        check_vma=False,
    )
```

time: 483 us -> 187 us (0.39)
  the two profiles are of different devices: /device:TPU:16 before, /device:TPU:102 now
where the time goes in v3:
time: 187 us; the launch traced here: 185 us
  waiting for transfers between devices  68.8 us (37%)
  starting transfers between devices  40.7 us (22%)
  local copies, waits for them, and re-layouts  29 us (16%)
  matrix products  26.5 us (14%)
  Pallas kernels  18.7 us (10%)
    all_to_all x4, waiting for transfers between devices, exchanged(): return lax.all_to_all(x, 'lon', 0, 0, tiled=True)  68.8 us
    all_to_all x4, starting transfers between devices, exchanged(): return lax.all_to_all(x, 'lon', 0, 0, tiled=True)  24.6 us
    unnamed x47, local copies, waits for them, and re-layouts  15.4 us
    dot_general x4, matrix products, per_device(): jnp.dot(x, table, precision=high, preferred_element_type=jnp.float32)  14.6 us
    ppermute x2, starting transfers between devices, per_device(): lax.ppermute(split[:, :, :, 0], 'lat', [(i + 1, i) for i in range(lat_cou...  12.1 us
    dot_general x4, matrix products, per_device(): jnp.dot(spectrum, table.T, precision=high, preferred_element_type=jnp.flo...  11.9 us
    another operation x8, local copies, waits for them, and re-layouts, per_device(): spectrum = spectrum * jnp.tile(weight, (4 * per, 1))  10.7 us
    pallas_call x2, Pallas kernels, tendencies(): pl.pallas_call(functools.partial(tend_body, count, rows, cols, dlon, dlat...  7.73 us
  transfers between devices with their start and end apart: 8, of which 4 were waited for; matrix products, arithmetic and copies ran while one was open for 22% of the time, Pallas kernels for 7%

profile of v3, /device:TPU:102, one launch (start us, length us, event | category | flops | bytes accessed | tf_op | source)
XLA Modules:
  0.0 185.3 jit_solution(7669421874609598035)
XLA Ops:
  7.1 5.8 %all-to-all-start.2 = ((f32[8,128,384]{2,1,0:T(8,128)}), f32[8,128,384]{2,1,0:T(8,128)}, u32[]{:S(2)}, u32[]{:S(2)}) async-start(f32[8,128,384]{2,1,0:T(8,128)} %shard_map.123), calls=%async_computation.2 | async-start | bytes 3145728 | tf_op jit(solution)/shard_map/all_to_all | solution.py:266
  20.1 11.8 %all-to-all-done.2.got_ref = f32[8,128,384]{2,1,0:T(8,128)} async-done(((f32[8,128,384]{2,1,0:T(8,128)}), f32[8,128,384]{2,1,0:T(8,128)}, u32[]{:S(2)}, u32[]{:S(2)}) %all-to-all-start.2) | async-done | bytes 1572896 | tf_op jit(solution)/shard_map/all_to_all | solution.py:266
  31.8 6.1 %all-to-all-start = ((f32[8,256,384]{2,1,0:T(8,128)}), f32[8,256,384]{2,1,0:T(8,128)S(1)}, u32[]{:S(2)}, u32[]{:S(2)}) async-start(f32[8,256,384]{2,1,0:T(8,128)} %copy-done), calls=%async_computation | async-start | bytes 6291456 | tf_op jit(solution)/shard_map/all_to_all | solution.py:266
  43.2 6.0 %collective-permute-start.3 = (f32[8,1,4,384]{3,2,1,0:T(4,128)S(1)}, f32[8,1,4,384]{3,2,1,0:T(4,128)S(1)}, u32[]{:S(2)}, u32[]{:S(2)}) collective-permute-start(f32[8,1,4,384]{3,2,1,0:T(4,128)S(1)} %bitcast.45), channel_id=1, source_target_pairs={{8,0},{16,8},{24,16},{32,24},{40,32},{48,40},{56,48},{64,56},{72,6... | collective-permute-start | bytes 147464 | tf_op jit(solution)/shard_map/ppermute | solution.py:286
  50.2 2.0 %copy.40 = f32[256,416]{0,1:T(8,128)} copy(f32[256,416]{1,0:T(8,128)} %bitcast.39) | data formatting | bytes 851968 | tf_op jit(solution)/shard_map/tile | solution.py:291
  60.0 3.4 %shard_map.124 = (f32[128,3072]{1,0:T(8,128)S(1)}, f32[128,1536]{1,0:T(8,128)S(1)}, f32[128,1536]{1,0:T(8,128)S(1)}) custom-call(s32[2]{0:T(128)S(1)} %add_convert_fusion.where_ref, f32[32,8]{1,0:T(8,128)S(1)} %constant_dynamic-slice_fusion.geo_ref, f32[8,128,384]{2,1,0:T(8,128)} %all-to-all-done.2.got_ref, ...), custom_call_target="tpu_custom_call" | custom-call | flops 15728640 | bytes 4718592 | tf_op jit(solution)/shard_map/pallas_call | solution.py:185
  63.4 5.1 %convolution_multiply_fusion.3 = f32[128,416]{0,1:T(8,128)S(1)} fusion(f32[128,416]{0,1:T(8,128)} %copy.45, f32[128,1536]{1,0:T(8,128)S(1)} %get-tuple-element.18, f32[1536,416]{1,0:T(8,128)} %constant.38.clone), kind=kOutput, calls=%fused_computation.3 | convolution fusion | flops 490786816 | bytes 3768320 | tf_op jit(solution)/shard_map/dot_general | solution.py:290
  68.6 2.6 %fusion.6.even_ref = f32[128,1536]{1,0:T(8,128)} fusion(f32[128,416]{0,1:T(8,128)S(1)} %convolution_multiply_fusion.3, f32[1536,416]{1,0:T(8,128)S(1)} %copy-done.16), kind=kOutput, calls=%fused_computation.25 | convolution fusion | flops 490733568 | bytes 3555328 | tf_op jit(solution)/shard_map/dot_general | solution.py:292
  71.2 3.3 %convolution_multiply_fusion.2 = f32[128,416]{0,1:T(8,128)} fusion(f32[128,416]{0,1:T(8,128)S(1)} %copy-done.19, f32[128,1536]{1,0:T(8,128)S(1)} %get-tuple-element.19, f32[1536,416]{1,0:T(8,128)S(1)} %copy-done.14), kind=kOutput, calls=%fused_computation.2 | convolution fusion | flops 490786816 | bytes 3768320 | tf_op jit(solution)/shard_map/dot_general | solution.py:290
  74.5 9.3 %all-to-all-done.got_ref = f32[8,256,384]{2,1,0:T(8,128)S(1)} async-done(((f32[8,256,384]{2,1,0:T(8,128)}), f32[8,256,384]{2,1,0:T(8,128)S(1)}, u32[]{:S(2)}, u32[]{:S(2)}) %all-to-all-start) | async-done | bytes 3145760 | tf_op jit(solution)/shard_map/all_to_all | solution.py:266
  84.0 2.1 %collective-permute-start = (f32[8,2,4,384]{3,2,1,0:T(4,128)S(1)}, f32[8,2,4,384]{3,2,1,0:T(4,128)S(1)}, u32[]{:S(2)}, u32[]{:S(2)}) collective-permute-start(f32[8,2,4,384]{3,2,1,0:T(4,128)S(1)} %bitcast.43), channel_id=1, source_target_pairs={{0,8},{8,16},{16,24},{24,32},{32,40},{40,48},{48,56},{56,64},{64,7... | collective-permute-start | bytes 294920 | tf_op jit(solution)/shard_map/ppermute | solution.py:285
  86.8 6.0 %collective-permute-start.1 = (f32[8,2,4,384]{3,2,1,0:T(4,128)}, f32[8,2,4,384]{3,2,1,0:T(4,128)S(1)}, u32[]{:S(2)}, u32[]{:S(2)}) collective-permute-start(f32[8,2,4,384]{3,2,1,0:T(4,128)} %bitcast.34), channel_id=1, source_target_pairs={{8,0},{16,8},{24,16},{32,24},{40,32},{48,40},{56,48},{64,56},{72,6... | collective-permute-start | bytes 294920 | tf_op jit(solution)/shard_map/ppermute | solution.py:286
  92.8 3.8 %fusion.7.odd_ref = f32[128,1536]{1,0:T(8,128)S(1)} fusion(f32[128,416]{0,1:T(8,128)} %convolution_multiply_fusion.2, f32[1536,416]{1,0:T(8,128)} %constant.39.clone), kind=kOutput, calls=%fused_computation.26 | convolution fusion | flops 490733568 | bytes 3555328 | tf_op jit(solution)/shard_map/dot_general | solution.py:292
  99.5 7.3 %all-to-all-start.3 = ((f32[8,128,384]{2,1,0:T(8,128)}), f32[8,128,384]{2,1,0:T(8,128)}, u32[]{:S(2)}, u32[]{:S(2)}) async-start(f32[8,128,384]{2,1,0:T(8,128)} %copy-done.2), calls=%async_computation.3 | async-start | bytes 3145728 | tf_op jit(solution)/shard_map/all_to_all | solution.py:266
  106.8 4.3 %shard_map.121 = (f32[256,3072]{1,0:T(8,128)S(1)}, f32[256,1536]{1,0:T(8,128)S(1)}, f32[256,1536]{1,0:T(8,128)S(1)}) custom-call(s32[2]{0:T(128)S(1)} %add_convert_fusion.where_ref, f32[32,8]{1,0:T(8,128)S(1)} %constant_dynamic-slice_fusion.geo_ref, f32[8,256,384]{2,1,0:T(8,128)S(1)} %all-to-all-done.got_ref, ...), custom_call_target="tpu_custom_call" | custom-call | flops 31457280 | bytes 9437184 | tf_op jit(solution)/shard_map/pallas_call | solution.py:185
  111.2 3.6 %convolution_multiply_fusion.1 = f32[256,416]{0,1:T(8,128)S(1)} fusion(f32[256,416]{0,1:T(8,128)} %copy.40, f32[256,1536]{1,0:T(8,128)S(1)} %get-tuple-element.15, f32[1536,416]{1,0:T(8,128)S(1)} %copy-done.17), kind=kOutput, calls=%fused_computation.1 | convolution fusion | flops 981573632 | bytes 4980736 | tf_op jit(solution)/shard_map/dot_general | solution.py:290
  114.9 2.8 %fusion.4.even_ref = f32[256,1536]{1,0:T(8,128)S(1)} fusion(f32[256,416]{0,1:T(8,128)S(1)} %convolution_multiply_fusion.1, f32[1536,416]{1,0:T(8,128)S(1)} %copy-done.17), kind=kOutput, calls=%fused_computation.23 | convolution fusion | flops 981467136 | bytes 4554752 | tf_op jit(solution)/shard_map/dot_general | solution.py:292
  117.7 2.6 %convolution_multiply_fusion = f32[256,416]{0,1:T(8,128)S(1)} fusion(f32[256,416]{0,1:T(8,128)S(1)} %copy-done.18, f32[256,1536]{1,0:T(8,128)S(1)} %get-tuple-element.16, f32[1536,416]{1,0:T(8,128)S(1)} %copy-done.15), kind=kOutput, calls=%fused_computation | convolution fusion | flops 981573632 | bytes 4980736 | tf_op jit(solution)/shard_map/dot_general | solution.py:290
  120.3 2.7 %fusion.5.odd_ref = f32[256,1536]{1,0:T(8,128)S(1)} fusion(f32[256,416]{0,1:T(8,128)S(1)} %convolution_multiply_fusion, f32[1536,416]{1,0:T(8,128)S(1)} %copy-done.15), kind=kOutput, calls=%fused_computation.24 | convolution fusion | flops 981467136 | bytes 4554752 | tf_op jit(solution)/shard_map/dot_general | solution.py:292
  125.8 4.2 %all-to-all-done.3.refs_0_ = f32[8,128,384]{2,1,0:T(8,128)} async-done(((f32[8,128,384]{2,1,0:T(8,128)}), f32[8,128,384]{2,1,0:T(8,128)}, u32[]{:S(2)}, u32[]{:S(2)}) %all-to-all-start.3) | async-done | bytes 1572896 | tf_op jit(solution)/shard_map/all_to_all | solution.py:266
  130.0 5.4 %all-to-all-start.1 = ((f32[8,256,384]{2,1,0:T(8,128)}), f32[8,256,384]{2,1,0:T(8,128)}, u32[]{:S(2)}, u32[]{:S(2)}) async-start(f32[8,256,384]{2,1,0:T(8,128)} %copy-done.1), calls=%async_computation.1 | async-start | bytes 6291456 | tf_op jit(solution)/shard_map/all_to_all | solution.py:266
  135.4 2.6 %shard_map.126 = (f32[24,32,384]{2,1,0:T(8,128)}, f32[24,32,384]{2,1,0:T(8,128)}, f32[24,32,384]{2,1,0:T(8,128)}, f32[24,32,384]{2,1,0:T(8,128)}) custom-call(f32[8,128,384]{2,1,0:T(8,128)} %all-to-all-done.3.refs_0_), custom_call_target="tpu_custom_call" | custom-call | bytes 3145728 | tf_op jit(solution)/shard_map/pallas_call | solution.py:90
  138.0 43.5 %all-to-all-done.1.refs_0_ = f32[8,256,384]{2,1,0:T(8,128)} async-done(((f32[8,256,384]{2,1,0:T(8,128)}), f32[8,256,384]{2,1,0:T(8,128)}, u32[]{:S(2)}, u32[]{:S(2)}) %all-to-all-start.1) | async-done | bytes 3145760 | tf_op jit(solution)/shard_map/all_to_all | solution.py:266
  181.5 3.6 %shard_map.127 = (f32[24,32,384]{2,1,0:T(8,128)}, f32[24,32,384]{2,1,0:T(8,128)}, f32[24,32,384]{2,1,0:T(8,128)}, f32[24,32,384]{2,1,0:T(8,128)}) custom-call(f32[8,256,384]{2,1,0:T(8,128)} %all-to-all-done.1.refs_0_, f32[24,32,384]{2,1,0:T(8,128)} %get-tuple-element.20.refs_1_, ...), custom_call_target="tpu_custom_call", output_to_operand_aliasing={{0}: (1, {}), {1}: (2, {}), {2}: (3, {}), {3}: (4, {})} | custom-call | bytes 6291456 | tf_op jit(solution)/shard_map/pallas_call | solution.py:90
  (79 shorter events, 34.2 us)
Async XLA Ops:
  0.6 1.3 copy-start.3
  1.9 1.3 copy-start.5
  3.2 1.3 copy-start.7
  7.1 24.7 %all-to-all-start.2 = ((f32[8,128,384]{2,1,0:T(8,128)}), f32[8,128,384]{2,1,0:T(8,128)}, u32[]{:S(2)}, u32[]{:S(2)}) async-start(f32[8,128,384]{2,1,0:T(8,128)} %shard_map.123), calls=%async_computation.2 | async-start | bytes 3145728 | tf_op jit(solution)/shard_map/all_to_all | solution.py:266
  12.9 1.3 copy-start.4
  18.4 1.6 copy-start
  20.1 17.9 %copy-start.20 = (s32[32,16]{0,1:T(8,128)S(1)}, s32[32,16]{0,1:T(8,128)}, u32[]{:S(2)}) copy-start(s32[32,16]{0,1:T(8,128)} %param.13) | copy-start | bytes 6148
  31.8 52.0 %all-to-all-start = ((f32[8,256,384]{2,1,0:T(8,128)}), f32[8,256,384]{2,1,0:T(8,128)S(1)}, u32[]{:S(2)}, u32[]{:S(2)}) async-start(f32[8,256,384]{2,1,0:T(8,128)} %copy-done), calls=%async_computation | async-start | bytes 6291456 | tf_op jit(solution)/shard_map/all_to_all | solution.py:266
  41.2 18.8 %collective-permute-start.2 = (f32[8,1,4,384]{3,2,1,0:T(4,128)S(1)}, f32[8,1,4,384]{3,2,1,0:T(4,128)S(1)}, u32[]{:S(2)}, u32[]{:S(2)}) collective-permute-start(f32[8,1,4,384]{3,2,1,0:T(4,128)S(1)} %bitcast.44), channel_id=1, source_target_pairs={{0,8},{8,16},{16,24},{24,32},{32,40},{40,48},{48,56},{56,64},{64,7... | collective-permute-start | bytes 147464 | tf_op jit(solution)/shard_map/ppermute | solution.py:285
  43.2 16.9 %collective-permute-start.3 = (f32[8,1,4,384]{3,2,1,0:T(4,128)S(1)}, f32[8,1,4,384]{3,2,1,0:T(4,128)S(1)}, u32[]{:S(2)}, u32[]{:S(2)}) collective-permute-start(f32[8,1,4,384]{3,2,1,0:T(4,128)S(1)} %bitcast.45), channel_id=1, source_target_pairs={{8,0},{16,8},{24,16},{32,24},{40,32},{48,40},{56,48},{64,56},{72,6... | collective-permute-start | bytes 147464 | tf_op jit(solution)/shard_map/ppermute | solution.py:286
  60.0 8.5 %copy-start.16 = (f32[1536,416]{1,0:T(8,128)S(1)}, f32[1536,416]{1,0:T(8,128)}, u32[]{:S(2)}) copy-start(f32[1536,416]{1,0:T(8,128)} %constant.38.clone) | copy-start | bytes 7667716
  63.4 7.8 %copy-start.12 = (f32[128,3072]{1,0:T(8,128)}, f32[128,3072]{1,0:T(8,128)S(1)}, u32[]{:S(2)}) copy-start(f32[128,3072]{1,0:T(8,128)S(1)} %get-tuple-element.17.tend_ref) | copy-start | bytes 4718596
  68.5 2.7 %copy-start.14 = (f32[1536,416]{1,0:T(8,128)S(1)}, f32[1536,416]{1,0:T(8,128)}, u32[]{:S(2)}) copy-start(f32[1536,416]{1,0:T(8,128)} %constant.39.clone) | copy-start | bytes 7667716
  68.5 2.7 %copy-start.19 = (f32[128,416]{0,1:T(8,128)S(1)}, f32[128,416]{0,1:T(8,128)}, u32[]{:S(2)}) copy-start(f32[128,416]{0,1:T(8,128)} %copy.46) | copy-start | bytes 638980
  83.9 12.7 %copy-start.11 = (f32[128,1536]{1,0:T(8,128)S(1)}, f32[128,1536]{1,0:T(8,128)}, u32[]{:S(2)}) copy-start(f32[128,1536]{1,0:T(8,128)} %fusion.6.even_ref) | copy-start | bytes 2359300
  83.9 12.7 %copy-start.13 = (f32[128,3072]{1,0:T(8,128)S(1)}, f32[128,3072]{1,0:T(8,128)}, u32[]{:S(2)}) copy-start(f32[128,3072]{1,0:T(8,128)} %copy-done.12) | copy-start | bytes 4718596
  84.0 22.8 %collective-permute-start = (f32[8,2,4,384]{3,2,1,0:T(4,128)S(1)}, f32[8,2,4,384]{3,2,1,0:T(4,128)S(1)}, u32[]{:S(2)}, u32[]{:S(2)}) collective-permute-start(f32[8,2,4,384]{3,2,1,0:T(4,128)S(1)} %bitcast.43), channel_id=1, source_target_pairs={{0,8},{8,16},{16,24},{24,32},{32,40},{40,48},{48,56},{56,64},{64,7... | collective-permute-start | bytes 294920 | tf_op jit(solution)/shard_map/ppermute | solution.py:285
  86.8 20.1 %collective-permute-start.1 = (f32[8,2,4,384]{3,2,1,0:T(4,128)}, f32[8,2,4,384]{3,2,1,0:T(4,128)S(1)}, u32[]{:S(2)}, u32[]{:S(2)}) collective-permute-start(f32[8,2,4,384]{3,2,1,0:T(4,128)} %bitcast.34), channel_id=1, source_target_pairs={{8,0},{16,8},{24,16},{32,24},{40,32},{48,40},{56,48},{64,56},{72,6... | collective-permute-start | bytes 294920 | tf_op jit(solution)/shard_map/ppermute | solution.py:286
  99.5 30.5 %all-to-all-start.3 = ((f32[8,128,384]{2,1,0:T(8,128)}), f32[8,128,384]{2,1,0:T(8,128)}, u32[]{:S(2)}, u32[]{:S(2)}) async-start(f32[8,128,384]{2,1,0:T(8,128)} %copy-done.2), calls=%async_computation.3 | async-start | bytes 3145728 | tf_op jit(solution)/shard_map/all_to_all | solution.py:266
  106.8 4.4 %copy-start.17 = (f32[1536,416]{1,0:T(8,128)S(1)}, f32[1536,416]{1,0:T(8,128)}, u32[]{:S(2)}) copy-start(f32[1536,416]{1,0:T(8,128)} %constant.38.clone) | copy-start | bytes 7667716
  114.8 2.8 %copy-start.15 = (f32[1536,416]{1,0:T(8,128)S(1)}, f32[1536,416]{1,0:T(8,128)}, u32[]{:S(2)}) copy-start(f32[1536,416]{1,0:T(8,128)} %constant.39.clone) | copy-start | bytes 7667716
  114.9 2.8 %copy-start.18 = (f32[256,416]{0,1:T(8,128)S(1)}, f32[256,416]{0,1:T(8,128)}, u32[]{:S(2)}) copy-start(f32[256,416]{0,1:T(8,128)} %copy.41) | copy-start | bytes 1277956
  124.2 1.6 copy-start.1
  130.0 51.5 %all-to-all-start.1 = ((f32[8,256,384]{2,1,0:T(8,128)}), f32[8,256,384]{2,1,0:T(8,128)}, u32[]{:S(2)}, u32[]{:S(2)}) async-start(f32[8,256,384]{2,1,0:T(8,128)} %copy-done.1), calls=%async_computation.1 | async-start | bytes 6291456 | tf_op jit(solution)/shard_map/all_to_all | solution.py:266
  (5 other events, 6.2 us)

commit v4 on v3

v4 whole, which is shorter than its diff:
```python
import functools
import math

import jax
import jax.numpy as jnp
import numpy as np
from jax import lax
from jax.experimental import pallas as pl
from jax.experimental.pallas import tpu as pltpu
from jax.sharding import PartitionSpec as P

OMEGA = 30.0
SECTORS = 8
REAL_Q = 64
FULL_Q = 128
SHIFT_Q = 52
LANES = 128


def geometry(total_rows):
    row = np.arange(-1, total_rows + 1)
    dist = np.maximum(np.minimum(row, total_rows - 1 - row), 0)
    cos_row = np.sin(np.pi * (dist + 0.5) / total_rows)
    face = np.arange(total_rows + 1)
    cos_face = np.sin(np.pi * np.minimum(face, total_rows - face) / total_rows)
    spin = -2.0 * OMEGA * np.cos(np.pi * (np.arange(total_rows) + 0.5) / total_rows)
    table = np.zeros((total_rows, 8))
    table[:, 0] = cos_row[1:-1]
    table[:, 1] = cos_row[:-2]
    table[:, 2] = cos_row[2:]
    table[:, 3] = cos_face[:-1]
    table[:, 4] = cos_face[1:]
    table[:, 5] = spin
    table[:, 6] = 1.0 / cos_row[1:-1]
    return table.astype(np.float32)


def split(x):
    high = x.astype(jnp.bfloat16)
    return high, (x - high.astype(jnp.float32)).astype(jnp.bfloat16)


def fourier_tables(total):
    column = np.arange(total // SECTORS)

    def angle(wave):
        return (column[:, None] * wave[None, :] % total) * (2.0 * np.pi / total)

    real, full = [], []
    for r in (0, 4):
        theta = angle(SECTORS * np.arange(REAL_Q) + r)
        real.append(np.concatenate([np.cos(theta), -np.sin(theta)], axis=1))
    for r in (1, 2, 3):
        theta = angle(SECTORS * (np.arange(FULL_Q) - SHIFT_Q) + r)
        cos, sin = np.cos(theta), np.sin(theta)
        full.append(np.block([[cos, -sin], [sin, cos]]))

    def halves(table):
        table = table.astype(np.float32)
        high = table.astype(jnp.bfloat16)
        return np.stack([high, (table - high.astype(np.float32)).astype(jnp.bfloat16)], axis=1)

    real, full = np.stack(real), np.stack(full)
    tables = (real, full, real.transpose(0, 2, 1), full.transpose(0, 2, 1))
    return [jnp.asarray(halves(t)) for t in tables]


def copy_all(pairs, sems):
    copies = [pltpu.make_async_copy(src, dst, sems.at[i]) for i, (src, dst) in enumerate(pairs)]
    for copy in copies:
        copy.start()
    for copy in copies:
        copy.wait()


def pack_body(count, per, rows, *refs):
    fields, out, sems = refs[:4], refs[4], refs[5]
    pairs = []
    for d in range(count):
        for k in range(per):
            for f in range(4):
                pairs.append((fields[f].at[d * per + k], out.at[d, pl.ds((4 * k + f) * rows, rows), :]))
    copy_all(pairs, sems)


def pack(count, fields):
    levels, rows, cols = fields[0].shape
    shape = (count, 4 * (levels // count) * rows, cols)
    return pl.pallas_call(
        functools.partial(pack_body, count, levels // count, rows),
        in_specs=[pl.BlockSpec(memory_space=pl.ANY)] * 4,
        out_specs=pl.BlockSpec(memory_space=pltpu.VMEM),
        out_shape=jax.ShapeDtypeStruct(shape, jnp.float32),
        scratch_shapes=[pltpu.SemaphoreType.DMA((4 * levels,))],
        compiler_params=pltpu.CompilerParams(vmem_limit_bytes=56 * 1024 * 1024),
        cost_estimate=pl.CostEstimate(flops=0, bytes_accessed=8 * math.prod(shape), transcendentals=0),
    )(*fields)


def place_body(count, per, rows, *refs):
    got, outs, sems = refs[0], refs[1:5], refs[5]
    pairs = []
    for d in range(count):
        for k in range(per):
            for f in range(4):
                pairs.append((got.at[d, pl.ds((4 * k + f) * rows, rows), :], outs[f].at[d * per + k]))
    copy_all(pairs, sems)


def place(got, shape):
    count = got.shape[0]
    return pl.pallas_call(
        functools.partial(place_body, count, shape[0] // count, shape[1]),
        in_specs=[pl.BlockSpec(memory_space=pltpu.VMEM)],
        out_specs=[pl.BlockSpec(memory_space=pl.ANY)] * 4,
        out_shape=[jax.ShapeDtypeStruct(shape, jnp.float32)] * 4,
        scratch_shapes=[pltpu.SemaphoreType.DMA((4 * shape[0],))],
        compiler_params=pltpu.CompilerParams(vmem_limit_bytes=32 * 1024 * 1024),
        cost_estimate=pl.CostEstimate(flops=0, bytes_accessed=8 * got.size, transcendentals=0),
    )(got)


def lat_shift(x, amount, edge):
    size = x.shape[0]
    place = lax.broadcasted_iota(jnp.int32, x.shape, 0)
    at = size - 1 if amount < 0 else 0
    return jnp.where(place == at, edge, pltpu.roll(x, amount % size, 0))


def level_tendencies(level, count, rows, cols, dlon, dlat, where_ref, geo_ref, got_ref, halo_ref, tend_ref):
    high = 4 * rows
    start = pl.multiple_of(level * high, high)
    halo_start = pl.multiple_of(level * 8, 8)
    blocks = [got_ref.at[r, pl.ds(start, high), :] for r in range(count)]
    halos = [halo_ref[r, pl.ds(halo_start, 8), :] for r in range(count)]
    is_first, is_last = where_ref[0] == 1, where_ref[1] == 1
    geo = geo_ref[...]
    cs, cn = geo[:, 1:2], geo[:, 2:3]
    fs, fn, spin0, inv = geo[0:1, 3:4], geo[:, 4:5], geo[:, 5:6], geo[:, 6:7]
    wide = cols + 2 * LANES
    signs = (-1.0, -1.0, 1.0, 1.0)

    def mid(x):
        return x[:, LANES : LANES + cols]

    def east_of(x):
        return pltpu.roll(x, wide - 1, 1)

    def west_of(x):
        return pltpu.roll(x, 1, 1)

    for r in range(count):
        prev, here, nxt = blocks[r - 1], blocks[r], blocks[(r + 1) % count]
        across = blocks[(r + count // 2) % count]
        ext = []
        south, north = [], []
        for f in range(4):
            part = slice(f * rows, (f + 1) * rows)
            ext.append(jnp.concatenate([prev[part, cols - LANES :], here[part, :], nxt[part, :LANES]], axis=1))
            low, top = f * rows, (f + 1) * rows - 1
            south.append(jnp.where(is_first, signs[f] * across[low : low + 1, :], halos[r][f : f + 1, :]))
            north.append(jnp.where(is_last, signs[f] * across[top : top + 1, :], halos[r][4 + f : 5 + f, :]))
        ux, vx, px, hx = ext
        heat_x = px * hx
        energy_x = 0.5 * (ux * ux + vx * vx) + heat_x
        u, v, p, heat, energy = mid(ux), mid(vx), mid(px), mid(heat_x), mid(energy_x)
        out = tend_ref.at[r, pl.ds(start, high), :]

        zeta = (mid(east_of(vx)) - mid(west_of(vx))) * (0.5 / dlon)
        zeta -= (cn * lat_shift(u, -1, north[0]) - cs * lat_shift(u, 1, south[0])) * (0.5 / dlat)
        absolute = spin0 + zeta * inv
        edges = [0.5 * (q[0] * q[0] + q[1] * q[1]) + q[2] * q[3] for q in (south, north)]
        de_x = mid(east_of(energy_x)) - mid(west_of(energy_x))
        de_y = lat_shift(energy, -1, edges[1]) - lat_shift(energy, 1, edges[0])
        out[0:rows, :] = absolute * v - de_x * ((0.5 / dlon) * inv)
        out[rows : 2 * rows, :] = -absolute * u - de_y * (0.5 / dlat)

        a = 0.5 * (ux + east_of(ux))
        ap, am = jnp.maximum(a, 0.0), jnp.minimum(a, 0.0)
        flow_x = ap * px + am * east_of(px)
        hot_x = ap * heat_x + am * east_of(heat_x)
        b = 0.5 * (v + lat_shift(v, -1, north[1]))
        bp, bm = fn * jnp.maximum(b, 0.0), fn * jnp.minimum(b, 0.0)
        flow_y = bp * p + bm * lat_shift(p, -1, north[2])
        hot_y = bp * heat + bm * lat_shift(heat, -1, north[2] * north[3])
        b0 = 0.5 * (south[1] + v[0:1, :])
        bp0, bm0 = fs * jnp.maximum(b0, 0.0), fs * jnp.minimum(b0, 0.0)
        flow_y0 = bp0 * south[2] + bm0 * p[0:1, :]
        hot_y0 = bp0 * (south[2] * south[3]) + bm0 * heat[0:1, :]
        out[2 * rows : 3 * rows, :] = -inv * (
            (mid(flow_x) - mid(west_of(flow_x))) * (1.0 / dlon) + (flow_y - lat_shift(flow_y, 1, flow_y0)) * (1.0 / dlat)
        )
        out[3 * rows : 4 * rows, :] = -inv * (
            (mid(hot_x) - mid(west_of(hot_x))) * (1.0 / dlon) + (hot_y - lat_shift(hot_y, 1, hot_y0)) * (1.0 / dlat)
        )


def butterfly(rows_at, cols, tend_ref, high_ref, low_ref):
    x = [tend_ref[b, rows_at, :] for b in range(SECTORS)]
    s = [x[b] + x[b + 4] for b in range(4)]
    d = [x[b] - x[b + 4] for b in range(4)]
    c = math.sqrt(0.5)
    even, odd = s[0] + s[2], s[1] + s[3]
    plus, minus = c * (d[1] + d[3]), c * (d[1] - d[3])
    parts = (even + odd, even - odd, d[0] + minus, -d[2] - plus, s[0] - s[2], s[3] - s[1], d[0] - minus, d[2] - plus)
    for i, part in enumerate(parts):
        at = slice(i * cols, (i + 1) * cols)
        high_ref[rows_at, at], low_ref[rows_at, at] = split(part)


def product(high, low, table_ref, *index):
    big, small = table_ref[(*index, 0)], table_ref[(*index, 1)]
    total = jnp.dot(high, big, preferred_element_type=jnp.float32)
    total += jnp.dot(low, big, preferred_element_type=jnp.float32)
    return total + jnp.dot(high, small, preferred_element_type=jnp.float32)


def truncate(total, cols, limit_ref, tables, high_ref, low_ref, wave_ref):
    real_ref, full_ref, real_back_ref, full_back_ref = tables
    limit = limit_ref[...]
    for i, r in enumerate((0, 4, 1, 2, 3)):
        if i < 2:
            at, half = slice(i * cols, (i + 1) * cols), REAL_Q
            ahead, back, place = real_ref, real_back_ref, i
        else:
            at, half = slice((2 * i - 2) * cols, 2 * i * cols), FULL_Q
            ahead, back, place = full_ref, full_back_ref, i - 2
        spectrum = product(high_ref[:, at], low_ref[:, at], ahead, place)
        lane = lax.broadcasted_iota(jnp.int32, (1, 2 * half), 1)
        q = jnp.where(lane >= half, lane - half, lane) - (0 if i < 2 else SHIFT_Q)
        k = jnp.abs(SECTORS * q + r)
        factor = jnp.where(k <= limit, jnp.where(k == 0, 1.0 / total, 2.0 / total), 0.0)
        wave_ref[:, at] = product(*split(spectrum * factor), back, place)


def update(level, rows, cols, step_size, listed_ref, got_ref, tend_ref, wave_ref, out_ref):
    c = math.sqrt(0.5)
    high = 4 * rows
    for f in range(4):
        for j in range(0, rows, 8):
            at = pl.ds(pl.multiple_of(level * high + f * rows + j, 8), 8)
            w0, w4, a1, b1, a2, b2, a3, b3 = [wave_ref[at, i * cols : (i + 1) * cols] for i in range(SECTORS)]
            near, far = w0 + w4, w0 - w4
            even = (near + a2, far - b2, near - a2, far + b2)
            odd = (a1 + a3, c * ((a1 - b1) - (a3 + b3)), b3 - b1, c * ((a3 - b3) - (a1 + b1)))
            listed = listed_ref[j : j + 8, :] > 0
            for b in range(SECTORS):
                smooth = even[b % 4] + odd[b % 4] if b < 4 else even[b % 4] - odd[b % 4]
                base = got_ref[b, at, :]
                if f == 3:
                    base = base * got_ref[b, pl.ds(pl.multiple_of(level * high + 2 * rows + j, 8), 8), :]
                out_ref[b, at, :] = base + step_size * jnp.where(listed, smooth, tend_ref[b, at, :])


def step_body(per, rows, cols, dlon, dlat, step_size, where_ref, geo_ref, limit_ref, listed_ref, got_ref, *refs):
    tables, halos = refs[:4], refs[4 : 4 + SECTORS]
    out_ref, tend_ref, high_ref, low_ref, wave_ref, halo_ref = refs[4 + SECTORS :]
    high = 4 * rows
    for r in range(SECTORS):
        halo_ref[lax.rem(where_ref[2] + r, SECTORS)] = halos[r][0]

    @pl.loop(0, per)
    def _(level):
        level_tendencies(level, SECTORS, rows, cols, dlon, dlat, where_ref, geo_ref, got_ref, halo_ref, tend_ref)

    @pl.loop(0, per * high // 16)
    def _(group):
        butterfly(pl.ds(pl.multiple_of(group * 16, 16), 16), cols, tend_ref, high_ref, low_ref)

    truncate(SECTORS * cols, cols, limit_ref, tables, high_ref, low_ref, wave_ref)

    @pl.loop(0, per)
    def _(level):
        update(level, rows, cols, step_size, listed_ref, got_ref, tend_ref, wave_ref, out_ref)


def stepped(rows, dlon, dlat, step_size, where, geo, limit, listed, got, halos, tables):
    count, height, cols = got.shape
    inside = pl.BlockSpec(memory_space=pltpu.VMEM)
    full = count * cols
    return pl.pallas_call(
        functools.partial(step_body, height // (4 * rows), rows, cols, dlon, dlat, step_size),
        in_specs=[pl.BlockSpec(memory_space=pltpu.SMEM)] + [inside] * (8 + count),
        out_specs=inside,
        out_shape=jax.ShapeDtypeStruct(got.shape, jnp.float32),
        scratch_shapes=[
            pltpu.VMEM(got.shape, jnp.float32),
            pltpu.VMEM((height, full), jnp.bfloat16),
            pltpu.VMEM((height, full), jnp.bfloat16),
            pltpu.VMEM((height, full), jnp.float32),
            pltpu.VMEM((count, height // (4 * rows) * 8, cols), jnp.float32),
        ],
        compiler_params=pltpu.CompilerParams(vmem_limit_bytes=48 * 1024 * 1024),
        cost_estimate=pl.CostEstimate(flops=8 * 1024 * 1024 * height, bytes_accessed=24 * height * full, transcendentals=0),
    )(where, geo, limit, listed, got, *tables, *halos)


def per_device(u_wind, v_wind, thickness, theta, polar_rows, cutoffs):
    levels, rows, cols = u_wind.shape
    lat_count = lax.axis_size("lat")
    count = lax.axis_size("lon")
    lat_place = lax.axis_index("lat")
    me = lax.axis_index("lon")
    total_rows = rows * lat_count
    total_cols = cols * count
    dlon = 2.0 * math.pi / total_cols
    dlat = math.pi / total_rows
    step_size = 0.25 * dlon
    first_row = lat_place * rows
    fields = (u_wind, v_wind, thickness, theta)
    per = levels // count

    got = lax.all_to_all(pack(count, fields), "lon", 0, 0, tiled=True)

    low_rows = jnp.stack([f[:, 0, :] for f in fields], axis=1)
    high_rows = jnp.stack([f[:, rows - 1, :] for f in fields], axis=1)
    south = lax.ppermute(high_rows, "lat", [(i, i + 1) for i in range(lat_count - 1)])
    north = lax.ppermute(low_rows, "lat", [(i + 1, i) for i in range(lat_count - 1)])
    halo = jnp.concatenate([south, north], axis=1).reshape(count, 8 * per, cols)
    turned = [lax.dynamic_slice_in_dim(halo, lax.rem(me + step, count), 1, 0) for step in range(count)]
    for step in range(1, count):
        turned[step] = lax.ppermute(turned[step], "lon", [(i, (i + step) % count) for i in range(count)])
    halos = [turned[(count - r) % count] for r in range(count)]

    geo = lax.dynamic_slice_in_dim(jnp.asarray(geometry(total_rows)), first_row, rows, 0)
    own = first_row + jnp.arange(rows)
    listed = jnp.any(polar_rows.reshape(-1)[None, :] == own[:, None], axis=1)[:, None].astype(jnp.int32)
    limit = jnp.tile(lax.dynamic_slice_in_dim(cutoffs, first_row, rows, 0), 4 * per)[:, None]
    where = jnp.stack([lat_place == 0, lat_place == lat_count - 1, me]).astype(jnp.int32)
    tables = fourier_tables(total_cols)
    fresh = stepped(rows, dlon, dlat, step_size, where, geo, limit, listed, got, halos, tables)
    return tuple(place(lax.all_to_all(fresh, "lon", 0, 0, tiled=True), u_wind.shape))


def solution(mesh):
    field = P(None, "lat", "lon")
    return jax.shard_map(
        per_device,
        mesh=mesh,
        in_specs=(field, field, field, field, P(), P()),
        out_specs=(field, field, field, field),
        check_vma=False,
    )
```

time: 187 us -> 168 us (0.90)
  the two profiles are of different devices: /device:TPU:102 before, /device:TPU:16 now
where the time goes in v4:
time: 168 us; the launch traced here: 167 us
  waiting for transfers between devices  55.6 us (33%)
  blocking collectives  55.4 us (33%)
  Pallas kernels  25.6 us (15%)
  starting transfers between devices  20.7 us (12%)
  local copies, waits for them, and re-layouts  7.17 us (4%)
    all_to_all x1, blocking collectives, per_device(): lax.all_to_all(fresh, 'lon', 0, 0, tiled=True)  55.4 us
    ppermute x1, waiting for transfers between devices, per_device(): lax.ppermute(low_rows, 'lat', [(i + 1, i) for i in range(lat_count - 1)])  31.9 us
    pallas_call x1, Pallas kernels, stepped(): pl.pallas_call(functools.partial(step_body, height // (4 * rows), rows, c...  17.3 us
    ppermute x1, waiting for transfers between devices, per_device(): lax.ppermute(high_rows, 'lat', [(i, i + 1) for i in range(lat_count - 1)])  14.6 us
    ppermute x7, starting transfers between devices, per_device(): lax.ppermute(turned[step], 'lon', [(i, (i + step) % count) for i in range...  11.2 us
    ppermute x7, waiting for transfers between devices, per_device(): lax.ppermute(turned[step], 'lon', [(i, (i + step) % count) for i in range...  9.11 us
    pallas_call x1, Pallas kernels, pack(): pl.pallas_call(functools.partial(pack_body, count, levels // count, rows)...  5.36 us
    all_to_all x1, starting transfers between devices, per_device(): got = lax.all_to_all(pack(count, fields), 'lon', 0, 0, tiled=True)  5.16 us
  transfers between devices with their start and end apart: 10, of which 4 were waited for; matrix products, arithmetic and copies ran while one was open for 4% of the time, Pallas kernels for 0%

profile of v4, /device:TPU:16, one launch (start us, length us, event | category | flops | bytes accessed | tf_op | source)
XLA Modules:
  0.0 167.0 jit_solution(11690844691782990742)
XLA Ops:
  0.6 5.4 %shard_map.138 = f32[8,384,384]{2,1,0:T(8,128)} custom-call(f32[24,32,384]{2,1,0:T(8,128)} %refs_0_.2, f32[24,32,384]{2,1,0:T(8,128)} %refs_1_.2, f32[24,32,384]{2,1,0:T(8,128)} %refs_2_.2, f32[24,32,384]{2,1,0:T(8,128)} %refs_3_.2), custom_call_target="tpu_custom_call" | custom-call | bytes 9437184 | tf_op jit(solution)/shard_map/pallas_call | solution.py:89
  6.0 5.2 %all-to-all-start = ((f32[8,384,384]{2,1,0:T(8,128)}), f32[8,384,384]{2,1,0:T(8,128)}, u32[]{:S(2)}, u32[]{:S(2)}) async-start(f32[8,384,384]{2,1,0:T(8,128)} %shard_map.138), calls=%async_computation | async-start | bytes 9437184 | tf_op jit(solution)/shard_map/all_to_all | solution.py:313
  11.2 1.4 fusion.2
  12.6 1.5 fusion
  14.2 1.9 %collective-permute-start.1 = (f32[24,4,384]{2,1,0:T(4,128)S(1)}, f32[24,4,384]{2,1,0:T(4,128)}, u32[]{:S(2)}, u32[]{:S(2)}) collective-permute-start(f32[24,4,384]{2,1,0:T(4,128)S(1)} %pad_maximum_fusion.2), channel_id=1, source_target_pairs={{8,0},{16,8},{24,16},{32,24},{40,32},{48,40},{56,48},{64,56},{72,6... | collective-permute-start | bytes 442376 | tf_op jit(solution)/shard_map/ppermute | solution.py:318
  16.3 2.4 %collective-permute-start = (f32[24,4,384]{2,1,0:T(4,128)S(1)}, f32[24,4,384]{2,1,0:T(4,128)}, u32[]{:S(2)}, u32[]{:S(2)}) collective-permute-start(f32[24,4,384]{2,1,0:T(4,128)S(1)} %pad_maximum_fusion.1), channel_id=1, source_target_pairs={{0,8},{8,16},{16,24},{24,32},{32,40},{40,48},{48,56},{56,64},{64,7... | collective-permute-start | bytes 442376 | tf_op jit(solution)/shard_map/ppermute | solution.py:317
  19.2 31.9 %collective-permute-done.1 = f32[24,4,384]{2,1,0:T(4,128)} collective-permute-done((f32[24,4,384]{2,1,0:T(4,128)S(1)}, f32[24,4,384]{2,1,0:T(4,128)}, u32[]{:S(2)}, u32[]{:S(2)}) %collective-permute-start.1) | collective-permute-done | bytes 147488 | tf_op jit(solution)/shard_map/ppermute | solution.py:318
  51.0 14.6 %collective-permute-done = f32[24,4,384]{2,1,0:T(4,128)} collective-permute-done((f32[24,4,384]{2,1,0:T(4,128)S(1)}, f32[24,4,384]{2,1,0:T(4,128)}, u32[]{:S(2)}, u32[]{:S(2)}) %collective-permute-start) | collective-permute-done | bytes 147488 | tf_op jit(solution)/shard_map/ppermute | solution.py:317
  65.6 1.0 pad_maximum_fusion
  66.6 0.7 constant_dynamic-slice_fusion
  67.3 4.8 %collective-permute-start.2 = (f32[1,24,384]{2,1,0:T(8,128)S(1)}, f32[1,24,384]{2,1,0:T(8,128)S(1)}, u32[]{:S(2)}, u32[]{:S(2)}) collective-permute-start(f32[1,24,384]{2,1,0:T(8,128)S(1)} %get-tuple-element.18), channel_id=1, source_target_pairs={{0,7},{1,0},{2,1},{3,2},{4,3},{5,4},{6,5},{7,6},{8,15},{9,8},{10,9... | collective-permute-start | bytes 110600 | tf_op jit(solution)/shard_map/ppermute | solution.py:322
  72.2 1.4 collective-permute-start.3
  73.5 0.7 constant_dynamic-slice_fusion.8.geo_ref
  74.2 0.9 collective-permute-start.4
  75.2 2.0 %collective-permute-start.5 = (f32[1,24,384]{2,1,0:T(8,128)}, f32[1,24,384]{2,1,0:T(8,128)}, u32[]{:S(2)}, u32[]{:S(2)}) collective-permute-start(f32[1,24,384]{2,1,0:T(8,128)} %get-tuple-element.15), channel_id=1, source_target_pairs={{0,4},{1,5},{2,6},{3,7},{4,0},{5,1},{6,2},{7,3},{8,12},{9,13},{10,... | collective-permute-start | bytes 110600 | tf_op jit(solution)/shard_map/ppermute | solution.py:322
  77.1 0.4 collective-permute-start.6
  77.5 5.1 %collective-permute-done.2.refs_5_ = f32[1,24,384]{2,1,0:T(8,128)S(1)} collective-permute-done((f32[1,24,384]{2,1,0:T(8,128)S(1)}, f32[1,24,384]{2,1,0:T(8,128)S(1)}, u32[]{:S(2)}, u32[]{:S(2)}) %collective-permute-start.2) | collective-permute-done | bytes 36896 | tf_op jit(solution)/shard_map/ppermute | solution.py:322
  82.7 1.7 %collective-permute-start.8 = (f32[1,24,384]{2,1,0:T(8,128)}, f32[1,24,384]{2,1,0:T(8,128)}, u32[]{:S(2)}, u32[]{:S(2)}) collective-permute-start(f32[1,24,384]{2,1,0:T(8,128)} %get-tuple-element.12), channel_id=1, source_target_pairs={{0,1},{1,2},{2,3},{3,4},{4,5},{5,6},{6,7},{7,0},{8,9},{9,10},{10,1... | collective-permute-start | bytes 110600 | tf_op jit(solution)/shard_map/ppermute | solution.py:322
  84.4 0.8 dynamic_slice.31
  85.5 3.9 %collective-permute-done.7.refs_10_ = f32[1,24,384]{2,1,0:T(8,128)} collective-permute-done((f32[1,24,384]{2,1,0:T(8,128)}, f32[1,24,384]{2,1,0:T(8,128)}, u32[]{:S(2)}, u32[]{:S(2)}) %collective-permute-start.7) | collective-permute-done | bytes 36896 | tf_op jit(solution)/shard_map/ppermute | solution.py:322
  89.5 1.7 copy-done.1
  91.2 17.3 %shard_map.139 = f32[8,384,384]{2,1,0:T(8,128)} custom-call(s32[3]{0:T(128)S(1)} %pad_add_fusion.where_ref, f32[32,8]{1,0:T(8,128)S(1)} %constant_dynamic-slice_fusion.8.geo_ref, s32[384,1]{1,0:T(8,128)S(1)} %broadcast_in_dim_tile.4.limit_ref, s32[32,1]{1,0:T(8,128)S(1)} %copy.21.listed_ref, f32[8,384,384]{2,1,0:T(8,128)} %all-to-all-done.got_ref, ...), custom_call_target="tpu_custom_call" | custom-call | flops 3221225472 | bytes 28311552 | tf_op jit(solution)/shard_map/pallas_call | solution.py:281
  108.5 55.4 %all_to_all.10.refs_0_ = f32[8,384,384]{2,1,0:T(8,128)S(1)} all-to-all(f32[8,384,384]{2,1,0:T(8,128)} %shard_map.139), channel_id=1, replica_groups=mesh['lat'=32,'lon'=8] {'lon'}, dimensions={0} | all-to-all | bytes 9437184 | tf_op jit(solution)/shard_map/all_to_all | solution.py:332
  163.9 3.0 %shard_map.140 = (f32[24,32,384]{2,1,0:T(8,128)}, f32[24,32,384]{2,1,0:T(8,128)}, f32[24,32,384]{2,1,0:T(8,128)}, f32[24,32,384]{2,1,0:T(8,128)}) custom-call(f32[8,384,384]{2,1,0:T(8,128)S(1)} %all_to_all.10.refs_0_), custom_call_target="tpu_custom_call" | custom-call | bytes 9437184 | tf_op jit(solution)/shard_map/pallas_call | solution.py:112
  (27 shorter events, 1.1 us)
Async XLA Ops:
  6.0 83.5 %copy-start.3 = (bf16[2,2,128,384]{3,2,1,0:T(8,128)(2,1)S(1)}, bf16[2,2,128,384]{3,2,1,0:T(8,128)(2,1)}, u32[]{:S(2)}) copy-start(bf16[2,2,128,384]{3,2,1,0:T(8,128)(2,1)} %constant.64.clone.refs_2_) | copy-start | bytes 1179652
  6.0 83.5 %all-to-all-start = ((f32[8,384,384]{2,1,0:T(8,128)}), f32[8,384,384]{2,1,0:T(8,128)}, u32[]{:S(2)}, u32[]{:S(2)}) async-start(f32[8,384,384]{2,1,0:T(8,128)} %shard_map.138), calls=%async_computation | async-start | bytes 9437184 | tf_op jit(solution)/shard_map/all_to_all | solution.py:313
  11.2 7.6 %copy-start.4 = (s32[32,16]{0,1:T(8,128)S(1)}, s32[32,16]{0,1:T(8,128)}, u32[]{:S(2)}) copy-start(s32[32,16]{0,1:T(8,128)} %param.15) | copy-start | bytes 6148
  11.2 78.3 %copy-start.2 = (bf16[2,2,384,128]{3,2,1,0:T(8,128)(2,1)S(1)}, bf16[2,2,384,128]{3,2,1,0:T(8,128)(2,1)}, u32[]{:S(2)}) copy-start(bf16[2,2,384,128]{3,2,1,0:T(8,128)(2,1)} %constant.62.clone.refs_0_) | copy-start | bytes 1179652
  12.6 76.9 %copy-start = (bf16[3,2,768,256]{3,2,1,0:T(8,128)(2,1)S(1)}, bf16[3,2,768,256]{3,2,1,0:T(8,128)(2,1)}, u32[]{:S(2)}) copy-start(bf16[3,2,768,256]{3,2,1,0:T(8,128)(2,1)} %constant.63.clone.refs_1_) | copy-start | bytes 7077892
  14.2 36.8 %collective-permute-start.1 = (f32[24,4,384]{2,1,0:T(4,128)S(1)}, f32[24,4,384]{2,1,0:T(4,128)}, u32[]{:S(2)}, u32[]{:S(2)}) collective-permute-start(f32[24,4,384]{2,1,0:T(4,128)S(1)} %pad_maximum_fusion.2), channel_id=1, source_target_pairs={{8,0},{16,8},{24,16},{32,24},{40,32},{48,40},{56,48},{64,56},{72,6... | collective-permute-start | bytes 442376 | tf_op jit(solution)/shard_map/ppermute | solution.py:318
  16.3 49.3 %collective-permute-start = (f32[24,4,384]{2,1,0:T(4,128)S(1)}, f32[24,4,384]{2,1,0:T(4,128)}, u32[]{:S(2)}, u32[]{:S(2)}) collective-permute-start(f32[24,4,384]{2,1,0:T(4,128)S(1)} %pad_maximum_fusion.1), channel_id=1, source_target_pairs={{0,8},{8,16},{16,24},{24,32},{32,40},{40,48},{48,56},{56,64},{64,7... | collective-permute-start | bytes 442376 | tf_op jit(solution)/shard_map/ppermute | solution.py:317
  67.3 15.4 %collective-permute-start.2 = (f32[1,24,384]{2,1,0:T(8,128)S(1)}, f32[1,24,384]{2,1,0:T(8,128)S(1)}, u32[]{:S(2)}, u32[]{:S(2)}) collective-permute-start(f32[1,24,384]{2,1,0:T(8,128)S(1)} %get-tuple-element.18), channel_id=1, source_target_pairs={{0,7},{1,0},{2,1},{3,2},{4,3},{5,4},{6,5},{7,6},{8,15},{9,8},{10,9... | collective-permute-start | bytes 110600 | tf_op jit(solution)/shard_map/ppermute | solution.py:322
  72.2 10.5 %collective-permute-start.3 = (f32[1,24,384]{2,1,0:T(8,128)S(1)}, f32[1,24,384]{2,1,0:T(8,128)S(1)}, u32[]{:S(2)}, u32[]{:S(2)}) collective-permute-start(f32[1,24,384]{2,1,0:T(8,128)S(1)} %get-tuple-element.17), channel_id=1, source_target_pairs={{0,6},{1,7},{2,0},{3,1},{4,2},{5,3},{6,4},{7,5},{8,14},{9,15},{10,... | collective-permute-start | bytes 110600 | tf_op jit(solution)/shard_map/ppermute | solution.py:322
  74.2 11.3 %collective-permute-start.4 = (f32[1,24,384]{2,1,0:T(8,128)}, f32[1,24,384]{2,1,0:T(8,128)S(1)}, u32[]{:S(2)}, u32[]{:S(2)}) collective-permute-start(f32[1,24,384]{2,1,0:T(8,128)} %get-tuple-element.16), channel_id=1, source_target_pairs={{0,5},{1,6},{2,7},{3,0},{4,1},{5,2},{6,3},{7,4},{8,13},{9,14},{10,... | collective-permute-start | bytes 110600 | tf_op jit(solution)/shard_map/ppermute | solution.py:322
  75.2 10.3 %collective-permute-start.5 = (f32[1,24,384]{2,1,0:T(8,128)}, f32[1,24,384]{2,1,0:T(8,128)}, u32[]{:S(2)}, u32[]{:S(2)}) collective-permute-start(f32[1,24,384]{2,1,0:T(8,128)} %get-tuple-element.15), channel_id=1, source_target_pairs={{0,4},{1,5},{2,6},{3,7},{4,0},{5,1},{6,2},{7,3},{8,12},{9,13},{10,... | collective-permute-start | bytes 110600 | tf_op jit(solution)/shard_map/ppermute | solution.py:322
  77.1 8.4 %collective-permute-start.6 = (f32[1,24,384]{2,1,0:T(8,128)}, f32[1,24,384]{2,1,0:T(8,128)}, u32[]{:S(2)}, u32[]{:S(2)}) collective-permute-start(f32[1,24,384]{2,1,0:T(8,128)} %get-tuple-element.14), channel_id=1, source_target_pairs={{0,3},{1,4},{2,5},{3,6},{4,7},{5,0},{6,1},{7,2},{8,11},{9,12},{10,... | collective-permute-start | bytes 110600 | tf_op jit(solution)/shard_map/ppermute | solution.py:322
  82.7 6.8 %collective-permute-start.7 = (f32[1,24,384]{2,1,0:T(8,128)}, f32[1,24,384]{2,1,0:T(8,128)}, u32[]{:S(2)}, u32[]{:S(2)}) collective-permute-start(f32[1,24,384]{2,1,0:T(8,128)} %get-tuple-element.13), channel_id=1, source_target_pairs={{0,2},{1,3},{2,4},{3,5},{4,6},{5,7},{6,0},{7,1},{8,10},{9,11},{10,... | collective-permute-start | bytes 110600 | tf_op jit(solution)/shard_map/ppermute | solution.py:322
  82.7 6.8 %collective-permute-start.8 = (f32[1,24,384]{2,1,0:T(8,128)}, f32[1,24,384]{2,1,0:T(8,128)}, u32[]{:S(2)}, u32[]{:S(2)}) collective-permute-start(f32[1,24,384]{2,1,0:T(8,128)} %get-tuple-element.12), channel_id=1, source_target_pairs={{0,1},{1,2},{2,3},{3,4},{4,5},{5,6},{6,7},{7,0},{8,9},{9,10},{10,1... | collective-permute-start | bytes 110600 | tf_op jit(solution)/shard_map/ppermute | solution.py:322
  89.5 1.7 copy-start.1

commit v5 on v4

v5 whole, which is shorter than its diff:
```python
import functools
import math

import jax
import jax.numpy as jnp
import numpy as np
from jax import lax
from jax.experimental import pallas as pl
from jax.experimental.pallas import tpu as pltpu
from jax.sharding import PartitionSpec as P

OMEGA = 30.0
SECTORS = 8
REAL_Q = 64
FULL_Q = 128
SHIFT_Q = 52
LANES = 128


def geometry(total_rows):
    row = np.arange(-1, total_rows + 1)
    dist = np.maximum(np.minimum(row, total_rows - 1 - row), 0)
    cos_row = np.sin(np.pi * (dist + 0.5) / total_rows)
    face = np.arange(total_rows + 1)
    cos_face = np.sin(np.pi * np.minimum(face, total_rows - face) / total_rows)
    spin = -2.0 * OMEGA * np.cos(np.pi * (np.arange(total_rows) + 0.5) / total_rows)
    table = np.zeros((total_rows, 8))
    table[:, 0] = cos_row[1:-1]
    table[:, 1] = cos_row[:-2]
    table[:, 2] = cos_row[2:]
    table[:, 3] = cos_face[:-1]
    table[:, 4] = cos_face[1:]
    table[:, 5] = spin
    table[:, 6] = 1.0 / cos_row[1:-1]
    return table.astype(np.float32)


def split(x):
    high = x.astype(jnp.bfloat16)
    return high, (x - high.astype(jnp.float32)).astype(jnp.bfloat16)


def fourier_tables(total):
    column = np.arange(total // SECTORS)

    def angle(wave):
        return (column[:, None] * wave[None, :] % total) * (2.0 * np.pi / total)

    real, full = [], []
    for r in (0, 4):
        theta = angle(SECTORS * np.arange(REAL_Q) + r)
        real.append(np.concatenate([np.cos(theta), -np.sin(theta)], axis=1))
    for r in (1, 2, 3):
        theta = angle(SECTORS * (np.arange(FULL_Q) - SHIFT_Q) + r)
        cos, sin = np.cos(theta), np.sin(theta)
        full.append(np.block([[cos, -sin], [sin, cos]]))

    def halves(table):
        table = table.astype(np.float32)
        high = table.astype(jnp.bfloat16)
        return np.stack([high, (table - high.astype(np.float32)).astype(jnp.bfloat16)], axis=1)

    real, full = np.stack(real), np.stack(full)
    tables = (real, full, real.transpose(0, 2, 1), full.transpose(0, 2, 1))
    return [jnp.asarray(halves(t)) for t in tables]


def copy_all(pairs, sems):
    copies = [pltpu.make_async_copy(src, dst, sems.at[i]) for i, (src, dst) in enumerate(pairs)]
    for copy in copies:
        copy.start()
    for copy in copies:
        copy.wait()


def pack_body(count, per, rows, *refs):
    fields, out, held, arrive, leave = refs[:4], *refs[4:]
    comes, goes = [], []
    for d in range(count):
        for k in range(per):
            for f in range(4):
                at = pl.ds((4 * k + f) * rows, rows)
                i = len(comes)
                comes.append(pltpu.make_async_copy(fields[f].at[d * per + k], held.at[d, at, :], arrive.at[i]))
        goes.append(pltpu.make_async_copy(held.at[d], out.at[d], leave.at[d]))
    for copy in comes:
        copy.start()
    for d in range(count):
        for copy in comes[4 * per * d : 4 * per * (d + 1)]:
            copy.wait()
        goes[d].start()
    for copy in goes:
        copy.wait()


def pack(count, fields):
    levels, rows, cols = fields[0].shape
    shape = (count, 4 * (levels // count) * rows, cols)
    return pl.pallas_call(
        functools.partial(pack_body, count, levels // count, rows),
        in_specs=[pl.BlockSpec(memory_space=pl.ANY)] * 4,
        out_specs=pl.BlockSpec(memory_space=pl.ANY),
        out_shape=jax.ShapeDtypeStruct(shape, jnp.float32),
        scratch_shapes=[
            pltpu.VMEM(shape, jnp.float32),
            pltpu.SemaphoreType.DMA((4 * levels,)),
            pltpu.SemaphoreType.DMA((count,)),
        ],
        compiler_params=pltpu.CompilerParams(vmem_limit_bytes=56 * 1024 * 1024),
        cost_estimate=pl.CostEstimate(flops=0, bytes_accessed=8 * math.prod(shape), transcendentals=0),
    )(*fields)


def place_body(count, per, rows, *refs):
    got, outs, sems = refs[0], refs[1:5], refs[5]
    pairs = []
    for d in range(count):
        for k in range(per):
            for f in range(4):
                pairs.append((got.at[d, pl.ds((4 * k + f) * rows, rows), :], outs[f].at[d * per + k]))
    copy_all(pairs, sems)


def place(got, shape):
    count = got.shape[0]
    return pl.pallas_call(
        functools.partial(place_body, count, shape[0] // count, shape[1]),
        in_specs=[pl.BlockSpec(memory_space=pltpu.VMEM)],
        out_specs=[pl.BlockSpec(memory_space=pl.ANY)] * 4,
        out_shape=[jax.ShapeDtypeStruct(shape, jnp.float32)] * 4,
        scratch_shapes=[pltpu.SemaphoreType.DMA((4 * shape[0],))],
        compiler_params=pltpu.CompilerParams(vmem_limit_bytes=32 * 1024 * 1024),
        cost_estimate=pl.CostEstimate(flops=0, bytes_accessed=8 * got.size, transcendentals=0),
    )(got)


def lat_shift(x, amount, edge):
    size = x.shape[0]
    place = lax.broadcasted_iota(jnp.int32, x.shape, 0)
    at = size - 1 if amount < 0 else 0
    return jnp.where(place == at, edge, pltpu.roll(x, amount % size, 0))


def group_tendencies(level, first, size, span, rows, cols, dlon, dlat, place, geo_ref, got_ref, halo_refs, tend_ref, skip=0):
    start = pl.multiple_of(level * 4 * rows, 4 * rows)
    geo = geo_ref[pl.ds(pl.multiple_of(place * rows + first, 8), size), :]
    fs, fn, spin0, inv = geo[0:1, 3:4], geo[:, 4:5], geo[:, 5:6], geo[:, 6:7]
    to_east = (0.5 / dlon) * inv
    to_south, to_north = (0.5 / dlat) * (geo[:, 1:2] * inv), (0.5 / dlat) * (geo[:, 2:3] * inv)
    out_x, out_y = (-1.0 / dlon) * inv, (-1.0 / dlat) * inv
    wide = span * cols + 2 * LANES
    signs = (-1.0, -1.0, 1.0, 1.0)

    def mid(x):
        return x[:, LANES : LANES + span * cols]

    def east_of(x):
        return pltpu.roll(x, wide - 1, 1)

    def west_of(x):
        return pltpu.roll(x, 1, 1)

    def joined(parts):
        return parts[0] if len(parts) == 1 else jnp.concatenate(parts, axis=1)

    def edge_row(f, r, row, side, at_pole):
        if 0 <= row < rows:
            return got_ref[r, pl.ds(start + f * rows + row, 1), :]
        near = 0 if row < 0 else rows - 1
        across = got_ref[(r + SECTORS // 2) % SECTORS, pl.ds(start + f * rows + near, 1), :]
        return jnp.where(at_pole, signs[f] * across, halo_refs[side][r, level, f : f + 1, :])

    for base in range(0, SECTORS, span):
        sectors = range(base, base + span)
        ext, south, north = [], [], []
        for f in range(4):
            part = pl.ds(pl.multiple_of(start + f * rows + first, 8), size)
            ext.append(
                jnp.concatenate(
                    [got_ref[(base - 1) % SECTORS, part, cols - LANES :]]
                    + [got_ref[r, part, :] for r in sectors]
                    + [got_ref[(base + span) % SECTORS, part, :LANES]],
                    axis=1,
                )
            )
            south.append(joined([edge_row(f, r, first - 1, 0, place == 0) for r in sectors]))
            north.append(joined([edge_row(f, r, first + size, 1, place == lax.axis_size("lat") - 1) for r in sectors]))
        ux, vx, px, hx = ext
        heat_x = px * hx
        energy_x = 0.5 * (ux * ux + vx * vx) + heat_x
        u, v, p, heat, energy = mid(ux), mid(vx), mid(px), mid(heat_x), mid(energy_x)

        spin = spin0 + (mid(east_of(vx)) - mid(west_of(vx))) * to_east
        spin -= to_north * lat_shift(u, -1, north[0]) - to_south * lat_shift(u, 1, south[0])
        edges = [0.5 * (q[0] * q[0] + q[1] * q[1]) + q[2] * q[3] for q in (south, north)]
        de_x = mid(east_of(energy_x)) - mid(west_of(energy_x))
        de_y = lat_shift(energy, -1, edges[1]) - lat_shift(energy, 1, edges[0])
        u_t = spin * v - de_x * to_east
        v_t = de_y * (-0.5 / dlat) - spin * u

        a = 0.5 * (ux + east_of(ux))
        ap, am = jnp.maximum(a, 0.0), jnp.minimum(a, 0.0)
        flow_x = ap * px + am * east_of(px)
        hot_x = ap * heat_x + am * east_of(heat_x)
        b = (0.5 * fn) * (v + lat_shift(v, -1, north[1]))
        bp, bm = jnp.maximum(b, 0.0), jnp.minimum(b, 0.0)
        flow_y = bp * p + bm * lat_shift(p, -1, north[2])
        hot_y = bp * heat + bm * lat_shift(heat, -1, north[2] * north[3])
        b0 = (0.5 * fs) * (south[1] + v[0:1, :])
        bp0, bm0 = jnp.maximum(b0, 0.0), jnp.minimum(b0, 0.0)
        flow_y0 = bp0 * south[2] + bm0 * p[0:1, :]
        hot_y0 = bp0 * (south[2] * south[3]) + bm0 * heat[0:1, :]
        p_t = (mid(flow_x) - mid(west_of(flow_x))) * out_x + (flow_y - lat_shift(flow_y, 1, flow_y0)) * out_y
        h_t = (mid(hot_x) - mid(west_of(hot_x))) * out_x + (hot_y - lat_shift(hot_y, 1, hot_y0)) * out_y
        for f, value in enumerate((u_t, v_t, p_t, h_t)):
            kept = rows - 2 * skip
            part = pl.ds(pl.multiple_of(level * 4 * kept + f * kept + first - skip, 8), size)
            for i, r in enumerate(sectors):
                tend_ref[r, part, :] = value[:, i * cols : (i + 1) * cols]


def butterfly(rows_at, cols, tend_ref, high_ref, low_ref):
    x = [tend_ref[b, rows_at, :] for b in range(SECTORS)]
    s = [x[b] + x[b + 4] for b in range(4)]
    d = [x[b] - x[b + 4] for b in range(4)]
    c = math.sqrt(0.5)
    even, odd = s[0] + s[2], s[1] + s[3]
    plus, minus = c * (d[1] + d[3]), c * (d[1] - d[3])
    parts = (even + odd, even - odd, d[0] + minus, -d[2] - plus, s[0] - s[2], s[3] - s[1], d[0] - minus, d[2] - plus)
    for i, part in enumerate(parts):
        at = slice(i * cols, (i + 1) * cols)
        high_ref[rows_at, at], low_ref[rows_at, at] = split(part)


def product(high, low, table_ref, *index):
    big, small = table_ref[(*index, 0)], table_ref[(*index, 1)]
    total = jnp.dot(high, big, preferred_element_type=jnp.float32)
    total += jnp.dot(low, big, preferred_element_type=jnp.float32)
    return total + jnp.dot(high, small, preferred_element_type=jnp.float32)


def truncate(total, cols, limit, tables, high_ref, low_ref, wave_ref):
    real_ref, full_ref, real_back_ref, full_back_ref = tables
    for i, r in enumerate((0, 4, 1, 2, 3)):
        if i < 2:
            at, half = slice(i * cols, (i + 1) * cols), REAL_Q
            ahead, back, place = real_ref, real_back_ref, i
        else:
            at, half = slice((2 * i - 2) * cols, 2 * i * cols), FULL_Q
            ahead, back, place = full_ref, full_back_ref, i - 2
        spectrum = product(high_ref[:, at], low_ref[:, at], ahead, place)
        lane = lax.broadcasted_iota(jnp.int32, (1, 2 * half), 1)
        q = jnp.where(lane >= half, lane - half, lane) - (0 if i < 2 else SHIFT_Q)
        k = jnp.abs(SECTORS * q + r)
        factor = jnp.where(k <= limit, jnp.where(k == 0, 1.0 / total, 2.0 / total), 0.0)
        wave_ref[:, at] = product(*split(spectrum * factor), back, place)


def update(level, rows, cols, step_size, listed, got_ref, tend_ref, wave_ref, out_ref):
    c = math.sqrt(0.5)
    high = 4 * rows
    for f in range(4):
        for j in range(0, rows, 8):
            at = pl.ds(pl.multiple_of(level * high + f * rows + j, 8), 8)
            w0, w4, a1, b1, a2, b2, a3, b3 = [wave_ref[at, i * cols : (i + 1) * cols] for i in range(SECTORS)]
            near, far = w0 + w4, w0 - w4
            even = (near + a2, far - b2, near - a2, far + b2)
            odd = (a1 + a3, c * ((a1 - b1) - (a3 + b3)), b3 - b1, c * ((a3 - b3) - (a1 + b1)))
            chosen = listed[j : j + 8, :]
            for b in range(SECTORS):
                smooth = even[b % 4] + odd[b % 4] if b < 4 else even[b % 4] - odd[b % 4]
                base = got_ref[b, at, :]
                if f == 3:
                    base = base * got_ref[b, pl.ds(pl.multiple_of(level * high + 2 * rows + j, 8), 8), :]
                out_ref[b, at, :] = base + step_size * jnp.where(chosen, smooth, tend_ref[b, at, :])


def inner_body(per, rows, cols, dlon, dlat, geo_ref, got_ref, tend_ref):
    place = lax.axis_index("lat")

    @pl.loop(0, per)
    def _(level):
        for first in range(8, rows - 8, 8):
            group_tendencies(level, first, 8, 2, rows, cols, dlon, dlat, place, geo_ref, got_ref, None, tend_ref, 8)


def inner_tendencies(rows, dlon, dlat, geo, got):
    inside = pl.BlockSpec(memory_space=pltpu.VMEM)
    return pl.pallas_call(
        functools.partial(inner_body, got.shape[1] // (4 * rows), rows, got.shape[2], dlon, dlat),
        in_specs=[inside, inside],
        out_specs=inside,
        out_shape=jax.ShapeDtypeStruct((got.shape[0], got.shape[1] // rows * (rows - 16), got.shape[2]), jnp.float32),
        compiler_params=pltpu.CompilerParams(vmem_limit_bytes=12 * 1024 * 1024),
        cost_estimate=pl.CostEstimate(flops=40 * got.size, bytes_accessed=6 * got.size, transcendentals=0),
    )(geo, got)


def step_body(per, rows, cols, dlon, dlat, step_size, geo_ref, polar_ref, cutoff_ref, got_ref, tend_ref, south_ref, north_ref, *refs):
    tables = refs[:4]
    out_ref, edge_ref, high_ref, low_ref, wave_ref = refs[4:]
    high = 4 * rows
    halos = (south_ref, north_ref)
    place = lax.axis_index("lat")
    total = rows * lax.axis_size("lat")
    edge = jnp.sum((polar_ref[...] < total // 2).astype(jnp.int32))
    own = place * rows + lax.broadcasted_iota(jnp.int32, (rows, 1), 0)
    listed = (own < edge) | (own >= total // 2 + edge)
    bands = LANES // rows
    cut = cutoff_ref[pl.ds(place // bands, 1), :]
    lane = lax.broadcasted_iota(jnp.int32, (rows, LANES), 1)
    mine = lane == lax.rem(place, bands) * rows + lax.broadcasted_iota(jnp.int32, (rows, LANES), 0)
    limit = jnp.sum(jnp.where(mine, cut, 0), axis=1, keepdims=True)
    limit = jnp.concatenate([limit] * (4 * per), axis=0)

    @pl.loop(0, per)
    def _(level):
        for first in (0, rows - 8):
            group_tendencies(level, first, 8, 2, rows, cols, dlon, dlat, place, geo_ref, got_ref, halos, edge_ref)
        for f in range(4):
            part = pl.ds(pl.multiple_of(level * high + f * rows + 8, 8), rows - 16)
            kept = pl.ds(pl.multiple_of((level * 4 + f) * (rows - 16), 8), rows - 16)
            for r in range(SECTORS):
                edge_ref[r, part, :] = tend_ref[r, kept, :]

    @pl.loop(0, per * high // 16)
    def _(group):
        butterfly(pl.ds(pl.multiple_of(group * 16, 16), 16), cols, edge_ref, high_ref, low_ref)

    truncate(SECTORS * cols, cols, limit, tables, high_ref, low_ref, wave_ref)

    @pl.loop(0, per)
    def _(level):
        update(level, rows, cols, step_size, listed, got_ref, edge_ref, wave_ref, out_ref)


def stepped(rows, dlon, dlat, step_size, geo, polar_rows, cutoffs, got, tend, south, north, tables):
    count, height, cols = got.shape
    inside = pl.BlockSpec(memory_space=pltpu.VMEM)
    full = count * cols
    return pl.pallas_call(
        functools.partial(step_body, height // (4 * rows), rows, cols, dlon, dlat, step_size),
        in_specs=[inside] * 11,
        out_specs=inside,
        out_shape=jax.ShapeDtypeStruct(got.shape, jnp.float32),
        scratch_shapes=[
            pltpu.VMEM(got.shape, jnp.float32),
            pltpu.VMEM((height, full), jnp.bfloat16),
            pltpu.VMEM((height, full), jnp.bfloat16),
            pltpu.VMEM((height, full), jnp.float32),
        ],
        compiler_params=pltpu.CompilerParams(vmem_limit_bytes=26 * 1024 * 1024),
        cost_estimate=pl.CostEstimate(flops=8 * 1024 * 1024 * height, bytes_accessed=24 * height * full, transcendentals=0),
    )(geo, polar_rows, cutoffs, got, tend, south, north, *tables)


def per_device(u_wind, v_wind, thickness, theta, polar_rows, cutoffs):
    levels, rows, cols = u_wind.shape
    lat_count = lax.axis_size("lat")
    count = lax.axis_size("lon")
    total_rows = rows * lat_count
    total_cols = cols * count
    dlon = 2.0 * math.pi / total_cols
    dlat = math.pi / total_rows
    step_size = 0.25 * dlon
    fields = (u_wind, v_wind, thickness, theta)
    per = levels // count

    got = lax.all_to_all(pack(count, fields), "lon", 0, 0, tiled=True)

    split_rows = got.reshape(count, per, 4, rows, cols)
    south = lax.ppermute(split_rows[:, :, :, rows - 1], "lat", [(i, i + 1) for i in range(lat_count - 1)])
    north = lax.ppermute(split_rows[:, :, :, 0], "lat", [(i + 1, i) for i in range(lat_count - 1)])

    geo = jnp.asarray(geometry(total_rows))
    cutoffs = cutoffs.reshape(total_rows // LANES, LANES)
    tables = fourier_tables(total_cols)
    tend = inner_tendencies(rows, dlon, dlat, geo, got)
    fresh = stepped(rows, dlon, dlat, step_size, geo, polar_rows, cutoffs, got, tend, south, north, tables)
    return tuple(place(lax.all_to_all(fresh, "lon", 0, 0, tiled=True), u_wind.shape))


def solution(mesh):
    field = P(None, "lat", "lon")
    return jax.shard_map(
        per_device,
        mesh=mesh,
        in_specs=(field, field, field, field, P(), P()),
        out_specs=(field, field, field, field),
        check_vma=False,
    )
```

time: 168 us -> 159 us (0.946)
  blocking collectives: 55.4 us -> 119 us
  waiting for transfers between devices: 55.6 us -> 0.01 us
  starting transfers between devices: 20.7 us -> 7.06 us
    all_to_all x0 -> x1, blocking collectives: none -> 60.6 us  [per_device(): got = lax.all_to_all(pack(count, fields), 'lon', 0, 0, tiled=True)]
    ppermute x9 -> x2, waiting for transfers between devices: 55.6 us -> 0.01 us  [the longest x1 0.01 us: per_device(): lax.ppermute(split_rows[:, :, :, rows - 1], 'lat', [(i, i + 1) for i in r...]
    ppermute x9 -> x2, starting transfers between devices: 15.5 us -> 7.06 us  [the longest x1 5.15 us: per_device(): lax.ppermute(split_rows[:, :, :, 0], 'lat', [(i + 1, i) for i in range(la...]
    all_to_all x1 -> x0, starting transfers between devices: 5.16 us -> none  [per_device(): got = lax.all_to_all(pack(count, fields), 'lon', 0, 0, tiled=True)]
    pallas_call x1, Pallas kernels: 17.3 us -> 12.5 us  [stepped(): pl.pallas_call(functools.partial(step_body, height // (4 * rows), rows, c...]
    unnamed x11 -> x23, local copies, waits for them, and re-layouts: 1.76 us -> 5.98 us
    pallas_call x0 -> x1, Pallas kernels: none -> 3.72 us  [inner_tendencies(): pl.pallas_call(functools.partial(inner_body, got.shape[1] // (4 * rows),...]
    all_to_all x1, blocking collectives: 55.4 us -> 58.6 us  [per_device(): lax.all_to_all(fresh, 'lon', 0, 0, tiled=True)]
  transfers between devices with their start and end apart: 10 -> 2, of which waited for: 4 -> 0; matrix products, arithmetic and copies ran while one was open for 4% -> 0% of each run, Pallas kernels for 0% -> 2%
where the time goes in v5:
time: 159 us; the launch traced here: 158 us
  blocking collectives  119 us (75%)
  Pallas kernels  24.4 us (15%)
  starting transfers between devices  7.06 us (4%)
  local copies, waits for them, and re-layouts  6.18 us (4%)
    all_to_all x1, blocking collectives, per_device(): got = lax.all_to_all(pack(count, fields), 'lon', 0, 0, tiled=True)  60.6 us
    all_to_all x1, blocking collectives, per_device(): lax.all_to_all(fresh, 'lon', 0, 0, tiled=True)  58.6 us
    pallas_call x1, Pallas kernels, stepped(): pl.pallas_call(functools.partial(step_body, height // (4 * rows), rows, c...  12.5 us
    unnamed x23, local copies, waits for them, and re-layouts  5.98 us
    pallas_call x1, Pallas kernels, pack(): pl.pallas_call(functools.partial(pack_body, count, levels // count, rows)...  5.16 us
    ppermute x1, starting transfers between devices, per_device(): lax.ppermute(split_rows[:, :, :, 0], 'lat', [(i + 1, i) for i in range(la...  5.15 us
    pallas_call x1, Pallas kernels, inner_tendencies(): pl.pallas_call(functools.partial(inner_body, got.shape[1] // (4 * rows),...  3.72 us
  transfers between devices with their start and end apart: 2, of which 0 were waited for; matrix products, arithmetic and copies ran while one was open for 0% of the time, Pallas kernels for 2%

profile of v5, /device:TPU:16, one launch (start us, length us, event | category | flops | bytes accessed | tf_op | source)
XLA Modules:
  0.0 157.6 jit_solution(8945420955284957781)
XLA Ops:
  0.6 5.2 %shard_map.138 = f32[8,384,384]{2,1,0:T(8,128)} custom-call(f32[24,32,384]{2,1,0:T(8,128)} %refs_0_.2, f32[24,32,384]{2,1,0:T(8,128)} %refs_1_.2, f32[24,32,384]{2,1,0:T(8,128)} %refs_2_.2, f32[24,32,384]{2,1,0:T(8,128)} %refs_3_.2), custom_call_target="tpu_custom_call" | custom-call | bytes 9437184 | tf_op jit(solution)/shard_map/pallas_call | solution.py:99
  5.8 0.0 copy-start.9
  5.8 0.0 copy-start.5
  5.8 0.0 copy-start.4
  5.8 60.6 %all_to_all.10.got_ref = f32[8,384,384]{2,1,0:T(8,128)S(1)} all-to-all(f32[8,384,384]{2,1,0:T(8,128)} %shard_map.138), channel_id=1, replica_groups=mesh['lat'=32,'lon'=8] {'lon'}, dimensions={0} | all-to-all | bytes 9437184 | tf_op jit(solution)/shard_map/all_to_all | solution.py:369
  66.4 0.2 fusion
  66.6 0.0 copy-start
  66.7 2.1 %copy-done = f32[8,384,384]{2,1,0:T(8,128)} copy-done((f32[8,384,384]{2,1,0:T(8,128)}, f32[8,384,384]{2,1,0:T(8,128)S(1)}, u32[]{:S(2)}) %copy-start) | copy-done | bytes 4718616
  68.8 0.7 copy.23
  69.5 0.7 copy.24
  70.2 1.9 %collective-permute-start = (f32[8,3,4,384]{3,2,1,0:T(4,128)}, f32[8,3,4,384]{3,2,1,0:T(4,128)S(1)}, u32[]{:S(2)}, u32[]{:S(2)}) collective-permute-start(f32[8,3,4,384]{3,2,1,0:T(4,128)} %bitcast.7), channel_id=1, source_target_pairs={{0,8},{8,16},{16,24},{24,32},{32,40},{40,48},{48,56},{56,64},{64,7... | collective-permute-start | bytes 442376 | tf_op jit(solution)/shard_map/ppermute | solution.py:372
  72.1 5.1 %collective-permute-start.1 = (f32[8,3,4,384]{3,2,1,0:T(4,128)}, f32[8,3,4,384]{3,2,1,0:T(4,128)}, u32[]{:S(2)}, u32[]{:S(2)}) collective-permute-start(f32[8,3,4,384]{3,2,1,0:T(4,128)} %bitcast.6), channel_id=1, source_target_pairs={{8,0},{16,8},{24,16},{32,24},{40,32},{48,40},{56,48},{64,56},{72,6... | collective-permute-start | bytes 442376 | tf_op jit(solution)/shard_map/ppermute | solution.py:373
  77.3 0.0 copy-done.9
  77.3 0.1 copy.18.polar_ref
  77.3 0.0 copy-done.5
  77.3 2.3 %copy-done.1 = f32[8,384,384]{2,1,0:T(8,128)S(1)} copy-done((f32[8,384,384]{2,1,0:T(8,128)S(1)}, f32[8,384,384]{2,1,0:T(8,128)}, u32[]{:S(2)}) %copy-start.1) | copy-done | bytes 4718616
  79.7 3.7 %shard_map.139.tend_ref = f32[8,192,384]{2,1,0:T(8,128)S(1)} custom-call(f32[1024,8]{1,0:T(8,128)S(1)} %copy-done.5, f32[8,384,384]{2,1,0:T(8,128)S(1)} %copy-done.1), custom_call_target="tpu_custom_call" | custom-call | flops 47185920 | bytes 7077888 | tf_op jit(solution)/shard_map/pallas_call | solution.py:289
  83.4 0.0 collective-permute-done.south_ref
  83.4 0.0 collective-permute-done.1.north_ref
  83.4 0.0 copy-done.4
  83.5 0.0 copy-done.7
  83.5 12.5 %shard_map.140 = f32[8,384,384]{2,1,0:T(8,128)S(1)} custom-call(f32[1024,8]{1,0:T(8,128)S(1)} %copy-done.5, s32[32,16]{1,0:T(8,128)S(1)} %copy.18.polar_ref, s32[8,128]{1,0:T(8,128)S(1)} %bitcast.9, f32[8,384,384]{2,1,0:T(8,128)S(1)} %copy-done.2, f32[8,192,384]{2,1,0:T(8,128)S(1)} %shard_map.139.tend_ref, ...), custom_call_target="tpu_custom_call" | custom-call | flops 3221225472 | bytes 28311552 | tf_op jit(solution)/shard_map/pallas_call | solution.py:341
  96.0 58.6 %all_to_all.11.refs_0_ = f32[8,384,384]{2,1,0:T(8,128)S(1)} all-to-all(f32[8,384,384]{2,1,0:T(8,128)S(1)} %shard_map.140), channel_id=1, replica_groups=mesh['lat'=32,'lon'=8] {'lon'}, dimensions={0} | all-to-all | bytes 9437184 | tf_op jit(solution)/shard_map/all_to_all | solution.py:380
  154.7 3.0 %shard_map.141 = (f32[24,32,384]{2,1,0:T(8,128)}, f32[24,32,384]{2,1,0:T(8,128)}, f32[24,32,384]{2,1,0:T(8,128)}, f32[24,32,384]{2,1,0:T(8,128)}) custom-call(f32[8,384,384]{2,1,0:T(8,128)S(1)} %all_to_all.11.refs_0_), custom_call_target="tpu_custom_call" | custom-call | bytes 9437184 | tf_op jit(solution)/shard_map/pallas_call | solution.py:126
  (10 shorter events, 0.0 us)
Async XLA Ops:
  5.8 71.5 %copy-start.9 = (s32[32,16]{0,1:T(8,128)S(1)}, s32[32,16]{0,1:T(8,128)}, u32[]{:S(2)}) copy-start(s32[32,16]{0,1:T(8,128)} %param.15) | copy-start | bytes 6148
  5.8 71.5 %copy-start.5 = (f32[1024,8]{1,0:T(8,128)S(1)}, f32[1024,8]{1,0:T(8,128)}, u32[]{:S(2)}) copy-start(f32[1024,8]{1,0:T(8,128)} %constant.10.clone.geo_ref) | copy-start | bytes 98308
  5.8 77.6 %copy-start.4 = (bf16[3,2,768,256]{3,2,1,0:T(8,128)(2,1)S(1)}, bf16[3,2,768,256]{3,2,1,0:T(8,128)(2,1)}, u32[]{:S(2)}) copy-start(bf16[3,2,768,256]{3,2,1,0:T(8,128)(2,1)} %constant.12.clone.refs_1_) | copy-start | bytes 7077892
  66.6 2.1 %copy-start = (f32[8,384,384]{2,1,0:T(8,128)}, f32[8,384,384]{2,1,0:T(8,128)S(1)}, u32[]{:S(2)}) copy-start(f32[8,384,384]{2,1,0:T(8,128)S(1)} %all_to_all.10.got_ref) | copy-start | bytes 14155780
  68.8 14.7 %copy-start.7 = (bf16[2,2,384,128]{3,2,1,0:T(8,128)(2,1)S(1)}, bf16[2,2,384,128]{3,2,1,0:T(8,128)(2,1)}, u32[]{:S(2)}) copy-start(bf16[2,2,384,128]{3,2,1,0:T(8,128)(2,1)} %constant.11.clone.refs_0_) | copy-start | bytes 1179652
  70.2 13.2 %collective-permute-start = (f32[8,3,4,384]{3,2,1,0:T(4,128)}, f32[8,3,4,384]{3,2,1,0:T(4,128)S(1)}, u32[]{:S(2)}, u32[]{:S(2)}) collective-permute-start(f32[8,3,4,384]{3,2,1,0:T(4,128)} %bitcast.7), channel_id=1, source_target_pairs={{0,8},{8,16},{16,24},{24,32},{32,40},{40,48},{48,56},{56,64},{64,7... | collective-permute-start | bytes 442376 | tf_op jit(solution)/shard_map/ppermute | solution.py:372
  72.1 11.3 %collective-permute-start.1 = (f32[8,3,4,384]{3,2,1,0:T(4,128)}, f32[8,3,4,384]{3,2,1,0:T(4,128)}, u32[]{:S(2)}, u32[]{:S(2)}) collective-permute-start(f32[8,3,4,384]{3,2,1,0:T(4,128)} %bitcast.6), channel_id=1, source_target_pairs={{8,0},{16,8},{24,16},{32,24},{40,32},{48,40},{56,48},{64,56},{72,6... | collective-permute-start | bytes 442376 | tf_op jit(solution)/shard_map/ppermute | solution.py:373
  77.3 2.3 %copy-start.1 = (f32[8,384,384]{2,1,0:T(8,128)S(1)}, f32[8,384,384]{2,1,0:T(8,128)}, u32[]{:S(2)}) copy-start(f32[8,384,384]{2,1,0:T(8,128)} %copy-done) | copy-start | bytes 14155780
  79.7 3.8 %copy-start.2 = (f32[8,384,384]{2,1,0:T(8,128)S(1)}, f32[8,384,384]{2,1,0:T(8,128)}, u32[]{:S(2)}) copy-start(f32[8,384,384]{2,1,0:T(8,128)} %copy-done) | copy-start | bytes 14155780
  79.7 3.8 %copy-start.3 = (bf16[3,2,256,768]{3,2,1,0:T(8,128)(2,1)S(1)}, bf16[3,2,256,768]{3,2,1,0:T(8,128)(2,1)}, u32[]{:S(2)}) copy-start(bf16[3,2,256,768]{3,2,1,0:T(8,128)(2,1)} %constant.14.clone.refs_3_) | copy-start | bytes 7077892
  79.7 3.8 %copy-start.6 = (bf16[2,2,128,384]{3,2,1,0:T(8,128)(2,1)S(1)}, bf16[2,2,128,384]{3,2,1,0:T(8,128)(2,1)}, u32[]{:S(2)}) copy-start(bf16[2,2,128,384]{3,2,1,0:T(8,128)(2,1)} %constant.13.clone.refs_2_) | copy-start | bytes 1179652
  79.7 3.8 %copy-start.8 = (s32[1024]{0:T(1024)S(1)}, s32[1024]{0:T(1024)}, u32[]{:S(2)}) copy-start(s32[1024]{0:T(1024)} %param.16) | copy-start | bytes 12292

commit v6 on v5

--- a/solution.py
+++ b/solution.py
@@ -74,23 +74,13 @@
 
 
 def pack_body(count, per, rows, *refs):
-    fields, out, held, arrive, leave = refs[:4], *refs[4:]
-    comes, goes = [], []
+    fields, out, sems = refs[:4], refs[4], refs[5]
+    pairs = []
     for d in range(count):
         for k in range(per):
             for f in range(4):
-                at = pl.ds((4 * k + f) * rows, rows)
-                i = len(comes)
-                comes.append(pltpu.make_async_copy(fields[f].at[d * per + k], held.at[d, at, :], arrive.at[i]))
-        goes.append(pltpu.make_async_copy(held.at[d], out.at[d], leave.at[d]))
-    for copy in comes:
-        copy.start()
-    for d in range(count):
-        for copy in comes[4 * per * d : 4 * per * (d + 1)]:
-            copy.wait()
-        goes[d].start()
-    for copy in goes:
-        copy.wait()
+                pairs.append((fields[f].at[d * per + k], out.at[d, pl.ds((4 * k + f) * rows, rows), :]))
+    copy_all(pairs, sems)
 
 
 def pack(count, fields):
@@ -99,16 +89,12 @@
     return pl.pallas_call(
         functools.partial(pack_body, count, levels // count, rows),
         in_specs=[pl.BlockSpec(memory_space=pl.ANY)] * 4,
-        out_specs=pl.BlockSpec(memory_space=pl.ANY),
-        out_shape=jax.ShapeDtypeStruct(shape, jnp.float32),
-        scratch_shapes=[
-            pltpu.VMEM(shape, jnp.float32),
-            pltpu.SemaphoreType.DMA((4 * levels,)),
-            pltpu.SemaphoreType.DMA((count,)),
-        ],
-        compiler_params=pltpu.CompilerParams(vmem_limit_bytes=56 * 1024 * 1024),
+        out_specs=pl.BlockSpec(memory_space=pltpu.VMEM),
+        out_shape=pltpu.VMEM(shape, jnp.float32),
+        scratch_shapes=[pltpu.SemaphoreType.DMA((4 * levels,))],
+        compiler_params=pltpu.CompilerParams(vmem_limit_bytes=8 * 1024 * 1024),
         cost_estimate=pl.CostEstimate(flops=0, bytes_accessed=8 * math.prod(shape), transcendentals=0),
-    )(*fields)
+    )(*[pltpu.with_memory_space_constraint(f, pltpu.HBM) for f in fields])
 
 
 def place_body(count, per, rows, *refs):
@@ -168,7 +154,9 @@
             return got_ref[r, pl.ds(start + f * rows + row, 1), :]
         near = 0 if row < 0 else rows - 1
         across = got_ref[(r + SECTORS // 2) % SECTORS, pl.ds(start + f * rows + near, 1), :]
-        return jnp.where(at_pole, signs[f] * across, halo_refs[side][r, level, f : f + 1, :])
+        per = got_ref.shape[1] // (4 * rows)
+        halo = halo_refs[side][pl.ds((r * per + level) * 4 + f, 1), :]
+        return jnp.where(at_pole, signs[f] * across, halo)
 
     for base in range(0, SECTORS, span):
         sectors = range(base, base + span)
@@ -275,11 +263,52 @@
                 out_ref[b, at, :] = base + step_size * jnp.where(chosen, smooth, tend_ref[b, at, :])
 
 
-def inner_body(per, rows, cols, dlon, dlat, geo_ref, got_ref, tend_ref):
+def edges_body(per, rows, got_ref, low_ref, high_ref, held_ref, sems):
+    parts = range(4 * per)
+    pairs = [(got_ref.at[:, pl.ds(q * rows, 8), :], held_ref.at[0, q]) for q in parts]
+    pairs += [(got_ref.at[:, pl.ds((q + 1) * rows - 8, 8), :], held_ref.at[1, q]) for q in parts]
+    copy_all(pairs, sems)
+    for r in range(SECTORS):
+        for q in parts:
+            at = r * 4 * per + q
+            low_ref[at : at + 1, :] = held_ref[0, q, r, 0:1, :]
+            high_ref[at : at + 1, :] = held_ref[1, q, r, 7:8, :]
+
+
+def edge_rows(rows, got):
+    count, height, cols = got.shape
+    inside = pl.BlockSpec(memory_space=pltpu.VMEM)
+    return pl.pallas_call(
+        functools.partial(edges_body, height // (4 * rows), rows),
+        in_specs=[pl.BlockSpec(memory_space=pltpu.HBM)],
+        out_specs=[inside] * 2,
+        out_shape=[jax.ShapeDtypeStruct((count * height // rows, cols), jnp.float32)] * 2,
+        scratch_shapes=[
+            pltpu.VMEM((2, height // rows, count, 8, cols), jnp.float32),
+            pltpu.SemaphoreType.DMA((2 * height // rows,)),
+        ],
+        compiler_params=pltpu.CompilerParams(vmem_limit_bytes=8 * 1024 * 1024),
+        cost_estimate=pl.CostEstimate(flops=0, bytes_accessed=16 * count * height // rows * cols, transcendentals=0),
+    )(got)
+
+
+def arrivals(per, high, far_ref, near_ref, sems):
+    def one(level):
+        at = pl.ds(pl.multiple_of(level * high, high), high)
+        return pltpu.make_async_copy(far_ref.at[:, at, :], near_ref.at[:, at, :], sems.at[level])
+
+    for level in range(per):
+        one(level).start()
+    return one
+
+
+def inner_body(per, rows, cols, dlon, dlat, geo_ref, far_ref, tend_ref, got_ref, sems):
     place = lax.axis_index("lat")
+    arrival = arrivals(per, 4 * rows, far_ref, got_ref, sems)
 
     @pl.loop(0, per)
     def _(level):
+        arrival(level).wait()
         for first in range(8, rows - 8, 8):
             group_tendencies(level, first, 8, 2, rows, cols, dlon, dlat, place, geo_ref, got_ref, None, tend_ref, 8)
 
@@ -288,18 +317,20 @@
     inside = pl.BlockSpec(memory_space=pltpu.VMEM)
     return pl.pallas_call(
         functools.partial(inner_body, got.shape[1] // (4 * rows), rows, got.shape[2], dlon, dlat),
-        in_specs=[inside, inside],
+        in_specs=[inside, pl.BlockSpec(memory_space=pltpu.HBM)],
         out_specs=inside,
+        scratch_shapes=[pltpu.VMEM(got.shape, jnp.float32), pltpu.SemaphoreType.DMA((got.shape[1] // (4 * rows),))],
         out_shape=jax.ShapeDtypeStruct((got.shape[0], got.shape[1] // rows * (rows - 16), got.shape[2]), jnp.float32),
         compiler_params=pltpu.CompilerParams(vmem_limit_bytes=12 * 1024 * 1024),
         cost_estimate=pl.CostEstimate(flops=40 * got.size, bytes_accessed=6 * got.size, transcendentals=0),
     )(geo, got)
 
 
-def step_body(per, rows, cols, dlon, dlat, step_size, geo_ref, polar_ref, cutoff_ref, got_ref, tend_ref, south_ref, north_ref, *refs):
+def step_body(per, rows, cols, dlon, dlat, step_size, geo_ref, polar_ref, cutoff_ref, far_ref, tend_ref, south_ref, north_ref, *refs):
     tables = refs[:4]
-    out_ref, edge_ref, high_ref, low_ref, wave_ref = refs[4:]
+    out_ref, edge_ref, high_ref, low_ref, wave_ref, got_ref, sems = refs[4:]
     high = 4 * rows
+    arrival = arrivals(per, high, far_ref, got_ref, sems)
     halos = (south_ref, north_ref)
     place = lax.axis_index("lat")
     total = rows * lax.axis_size("lat")
@@ -315,6 +346,7 @@
 
     @pl.loop(0, per)
     def _(level):
+        arrival(level).wait()
         for first in (0, rows - 8):
             group_tendencies(level, first, 8, 2, rows, cols, dlon, dlat, place, geo_ref, got_ref, halos, edge_ref)
         for f in range(4):
@@ -340,7 +372,7 @@
     full = count * cols
     return pl.pallas_call(
         functools.partial(step_body, height // (4 * rows), rows, cols, dlon, dlat, step_size),
-        in_specs=[inside] * 11,
+        in_specs=[inside] * 3 + [pl.BlockSpec(memory_space=pltpu.HBM)] + [inside] * 7,
         out_specs=inside,
         out_shape=jax.ShapeDtypeStruct(got.shape, jnp.float32),
         scratch_shapes=[
@@ -348,8 +380,10 @@
             pltpu.VMEM((height, full), jnp.bfloat16),
             pltpu.VMEM((height, full), jnp.bfloat16),
             pltpu.VMEM((height, full), jnp.float32),
+            pltpu.VMEM(got.shape, jnp.float32),
+            pltpu.SemaphoreType.DMA((height // (4 * rows),)),
         ],
-        compiler_params=pltpu.CompilerParams(vmem_limit_bytes=26 * 1024 * 1024),
+        compiler_params=pltpu.CompilerParams(vmem_limit_bytes=32 * 1024 * 1024),
         cost_estimate=pl.CostEstimate(flops=8 * 1024 * 1024 * height, bytes_accessed=24 * height * full, transcendentals=0),
     )(geo, polar_rows, cutoffs, got, tend, south, north, *tables)
 
@@ -368,9 +402,10 @@
 
     got = lax.all_to_all(pack(count, fields), "lon", 0, 0, tiled=True)
 
-    split_rows = got.reshape(count, per, 4, rows, cols)
-    south = lax.ppermute(split_rows[:, :, :, rows - 1], "lat", [(i, i + 1) for i in range(lat_count - 1)])
-    north = lax.ppermute(split_rows[:, :, :, 0], "lat", [(i + 1, i) for i in range(lat_count - 1)])
+    got = pltpu.with_memory_space_constraint(got, pltpu.HBM)
+    low_rows, high_rows = edge_rows(rows, got)
+    south = lax.ppermute(high_rows, "lat", [(i, i + 1) for i in range(lat_count - 1)])
+    north = lax.ppermute(low_rows, "lat", [(i + 1, i) for i in range(lat_count - 1)])
 
     geo = jnp.asarray(geometry(total_rows))
     cutoffs = cutoffs.reshape(total_rows // LANES, LANES)

time: 159 us -> 154 us (0.969)
  local copies, waits for them, and re-layouts: 6.18 us -> 0.11 us
  Pallas kernels: 24.4 us -> 26.4 us
    unnamed x23 -> x15, local copies, waits for them, and re-layouts: 5.98 us -> 0.11 us
    pallas_call x0 -> x1, Pallas kernels: none -> 2.06 us  [edge_rows(): pl.pallas_call(functools.partial(edges_body, height // (4 * rows), rows),...]
    pallas_call x1, Pallas kernels: 5.16 us -> 3.18 us  [pack(): pl.pallas_call(functools.partial(pack_body, count, levels // count, rows)...]
  transfers between devices with their start and end apart: 2 -> 2, of which waited for: 0 -> 0; matrix products, arithmetic and copies ran while one was open for 0% -> 0% of each run, Pallas kernels for 2% -> 3%
where the time goes in v6:
time: 154 us
  blocking collectives  119 us (77%)
  Pallas kernels  26.4 us (17%)
  starting transfers between devices  7.07 us (5%)
    all_to_all x1, blocking collectives, per_device(): got = lax.all_to_all(pack(count, fields), 'lon', 0, 0, tiled=True)  60.2 us
    all_to_all x1, blocking collectives, per_device(): lax.all_to_all(fresh, 'lon', 0, 0, tiled=True)  59.1 us
    pallas_call x1, Pallas kernels, stepped(): pl.pallas_call(functools.partial(step_body, height // (4 * rows), rows, c...  13 us
    pallas_call x1, Pallas kernels, inner_tendencies(): pl.pallas_call(functools.partial(inner_body, got.shape[1] // (4 * rows),...  5.26 us
    ppermute x1, starting transfers between devices, per_device(): lax.ppermute(low_rows, 'lat', [(i + 1, i) for i in range(lat_count - 1)])  5.15 us
    pallas_call x1, Pallas kernels, pack(): pl.pallas_call(functools.partial(pack_body, count, levels // count, rows)...  3.18 us
  transfers between devices with their start and end apart: 2, of which 0 were waited for; matrix products, arithmetic and copies ran while one was open for 0% of the time, Pallas kernels for 3%

profile of v6, /device:TPU:16, one launch (start us, length us, event | category | flops | bytes accessed | tf_op | source)
XLA Modules:
  0.0 153.7 jit_solution(9104913204344525512)
XLA Ops:
  0.6 3.2 %shard_map.138 = f32[8,384,384]{2,1,0:T(8,128)S(1)} custom-call(f32[24,32,384]{2,1,0:T(8,128)} %refs_0_.2, f32[24,32,384]{2,1,0:T(8,128)} %refs_1_.2, f32[24,32,384]{2,1,0:T(8,128)} %refs_2_.2, f32[24,32,384]{2,1,0:T(8,128)} %refs_3_.2), custom_call_target="tpu_custom_call" | custom-call | bytes 9437184 | tf_op jit(solution)/shard_map/pallas_call | solution.py:89
  3.8 60.2 %all_to_all.10.far_ref.got_ref = f32[8,384,384]{2,1,0:T(8,128)} all-to-all(f32[8,384,384]{2,1,0:T(8,128)S(1)} %shard_map.138), channel_id=1, replica_groups=mesh['lat'=32,'lon'=8] {'lon'}, dimensions={0} | all-to-all | bytes 9437184 | tf_op jit(solution)/shard_map/all_to_all | solution.py:403
  64.1 0.0 copy-start.6
  64.1 0.0 copy-start.2
  64.1 2.1 %shard_map.140 = (f32[96,384]{1,0:T(8,128)S(1)}, f32[96,384]{1,0:T(8,128)S(1)}) custom-call(f32[8,384,384]{2,1,0:T(8,128)} %all_to_all.10.far_ref.got_ref), custom_call_target="tpu_custom_call" | custom-call | bytes 589824 | tf_op jit(solution)/shard_map/pallas_call | solution.py:281
  66.1 1.9 %collective-permute-start = (f32[96,384]{1,0:T(8,128)S(1)}, f32[96,384]{1,0:T(8,128)S(1)}, u32[]{:S(2)}, u32[]{:S(2)}) collective-permute-start(f32[96,384]{1,0:T(8,128)S(1)} %get-tuple-element.6), channel_id=1, source_target_pairs={{0,8},{8,16},{16,24},{24,32},{32,40},{40,48},{48,56},{56,64},{64,7... | collective-permute-start | bytes 442376 | tf_op jit(solution)/shard_map/ppermute | solution.py:407
  68.1 5.1 %collective-permute-start.1 = (f32[96,384]{1,0:T(8,128)S(1)}, f32[96,384]{1,0:T(8,128)S(1)}, u32[]{:S(2)}, u32[]{:S(2)}) collective-permute-start(f32[96,384]{1,0:T(8,128)S(1)} %get-tuple-element.7), channel_id=1, source_target_pairs={{8,0},{16,8},{24,16},{32,24},{40,32},{48,40},{56,48},{64,56},{72,6... | collective-permute-start | bytes 442376 | tf_op jit(solution)/shard_map/ppermute | solution.py:408
  73.2 0.0 copy-done.6
  73.2 0.1 copy.15.polar_ref
  73.3 0.0 copy-done.2
  73.3 0.0 copy-start.3
  73.3 0.0 copy-start.4
  73.3 0.0 copy-start.5
  73.4 5.3 %shard_map.139.tend_ref = f32[8,192,384]{2,1,0:T(8,128)S(1)} custom-call(f32[1024,8]{1,0:T(8,128)S(1)} %copy-done.2, f32[8,384,384]{2,1,0:T(8,128)} %all_to_all.10.far_ref.got_ref), custom_call_target="tpu_custom_call" | custom-call | flops 47185920 | bytes 7077888 | tf_op jit(solution)/shard_map/pallas_call | solution.py:318
  78.6 0.0 collective-permute-done.south_ref
  78.6 0.0 collective-permute-done.1.north_ref
  78.6 0.0 copy-done
  78.7 0.0 copy-done.1
  78.7 0.0 copy-done.3
  78.7 0.0 copy-done.4
  78.7 0.0 copy-done.5
  78.7 13.0 %shard_map.141 = f32[8,384,384]{2,1,0:T(8,128)S(1)} custom-call(f32[1024,8]{1,0:T(8,128)S(1)} %copy-done.2, s32[32,16]{1,0:T(8,128)S(1)} %copy.15.polar_ref, s32[8,128]{1,0:T(8,128)S(1)} %bitcast.1, f32[8,384,384]{2,1,0:T(8,128)} %all_to_all.10.far_ref.got_ref, f32[8,192,384]{2,1,0:T(8,128)S(1)} %shard_map.139.tend_ref, ...), custom_call_target="tpu_custom_call" | custom-call | flops 3221225472 | bytes 28311552 | tf_op jit(solution)/shard_map/pallas_call | solution.py:373
  91.7 59.1 %all_to_all.11.refs_0_ = f32[8,384,384]{2,1,0:T(8,128)S(1)} all-to-all(f32[8,384,384]{2,1,0:T(8,128)S(1)} %shard_map.141), channel_id=1, replica_groups=mesh['lat'=32,'lon'=8] {'lon'}, dimensions={0} | all-to-all | bytes 9437184 | tf_op jit(solution)/shard_map/all_to_all | solution.py:415
  150.8 3.0 %shard_map.142 = (f32[24,32,384]{2,1,0:T(8,128)}, f32[24,32,384]{2,1,0:T(8,128)}, f32[24,32,384]{2,1,0:T(8,128)}, f32[24,32,384]{2,1,0:T(8,128)}) custom-call(f32[8,384,384]{2,1,0:T(8,128)S(1)} %all_to_all.11.refs_0_), custom_call_target="tpu_custom_call" | custom-call | bytes 9437184 | tf_op jit(solution)/shard_map/pallas_call | solution.py:112
  (2 shorter events, 0.0 us)
Async XLA Ops:
  64.1 9.2 %copy-start.6 = (s32[32,16]{0,1:T(8,128)S(1)}, s32[32,16]{0,1:T(8,128)}, u32[]{:S(2)}) copy-start(s32[32,16]{0,1:T(8,128)} %param.15) | copy-start | bytes 6148
  64.1 9.2 %copy-start.2 = (f32[1024,8]{1,0:T(8,128)S(1)}, f32[1024,8]{1,0:T(8,128)}, u32[]{:S(2)}) copy-start(f32[1024,8]{1,0:T(8,128)} %constant.10.clone.geo_ref) | copy-start | bytes 98308
  66.1 12.5 %collective-permute-start = (f32[96,384]{1,0:T(8,128)S(1)}, f32[96,384]{1,0:T(8,128)S(1)}, u32[]{:S(2)}, u32[]{:S(2)}) collective-permute-start(f32[96,384]{1,0:T(8,128)S(1)} %get-tuple-element.6), channel_id=1, source_target_pairs={{0,8},{8,16},{16,24},{24,32},{32,40},{40,48},{48,56},{56,64},{64,7... | collective-permute-start | bytes 442376 | tf_op jit(solution)/shard_map/ppermute | solution.py:407
  68.1 10.6 %collective-permute-start.1 = (f32[96,384]{1,0:T(8,128)S(1)}, f32[96,384]{1,0:T(8,128)S(1)}, u32[]{:S(2)}, u32[]{:S(2)}) collective-permute-start(f32[96,384]{1,0:T(8,128)S(1)} %get-tuple-element.7), channel_id=1, source_target_pairs={{8,0},{16,8},{24,16},{32,24},{40,32},{48,40},{56,48},{64,56},{72,6... | collective-permute-start | bytes 442376 | tf_op jit(solution)/shard_map/ppermute | solution.py:408
  73.3 5.3 %copy-start = (bf16[3,2,256,768]{3,2,1,0:T(8,128)(2,1)S(1)}, bf16[3,2,256,768]{3,2,1,0:T(8,128)(2,1)}, u32[]{:S(2)}) copy-start(bf16[3,2,256,768]{3,2,1,0:T(8,128)(2,1)} %constant.14.clone.refs_3_) | copy-start | bytes 7077892
  73.3 5.3 %copy-start.1 = (bf16[3,2,768,256]{3,2,1,0:T(8,128)(2,1)S(1)}, bf16[3,2,768,256]{3,2,1,0:T(8,128)(2,1)}, u32[]{:S(2)}) copy-start(bf16[3,2,768,256]{3,2,1,0:T(8,128)(2,1)} %constant.12.clone.refs_1_) | copy-start | bytes 7077892
  73.3 5.4 %copy-start.3 = (bf16[2,2,128,384]{3,2,1,0:T(8,128)(2,1)S(1)}, bf16[2,2,128,384]{3,2,1,0:T(8,128)(2,1)}, u32[]{:S(2)}) copy-start(bf16[2,2,128,384]{3,2,1,0:T(8,128)(2,1)} %constant.13.clone.refs_2_) | copy-start | bytes 1179652
  73.3 5.3 %copy-start.4 = (bf16[2,2,384,128]{3,2,1,0:T(8,128)(2,1)S(1)}, bf16[2,2,384,128]{3,2,1,0:T(8,128)(2,1)}, u32[]{:S(2)}) copy-start(bf16[2,2,384,128]{3,2,1,0:T(8,128)(2,1)} %constant.11.clone.refs_0_) | copy-start | bytes 1179652
  73.3 5.3 %copy-start.5 = (s32[1024]{0:T(1024)S(1)}, s32[1024]{0:T(1024)}, u32[]{:S(2)}) copy-start(s32[1024]{0:T(1024)} %param.16) | copy-start | bytes 12292

commit v7 on v6

--- a/solution.py
+++ b/solution.py
@@ -41,28 +41,30 @@
 
 
 def fourier_tables(total):
-    column = np.arange(total // SECTORS)
+    cols = total // SECTORS
+    column = np.arange(cols)
 
     def angle(wave):
         return (column[:, None] * wave[None, :] % total) * (2.0 * np.pi / total)
 
-    real, full = [], []
+    real = []
     for r in (0, 4):
         theta = angle(SECTORS * np.arange(REAL_Q) + r)
         real.append(np.concatenate([np.cos(theta), -np.sin(theta)], axis=1))
+    gap = np.zeros_like(real[0])
+    tables = [np.block([[real[0], gap], [gap, real[1]]])]
     for r in (1, 2, 3):
         theta = angle(SECTORS * (np.arange(FULL_Q) - SHIFT_Q) + r)
         cos, sin = np.cos(theta), np.sin(theta)
-        full.append(np.block([[cos, -sin], [sin, cos]]))
+        tables.append(np.block([[cos, -sin], [sin, cos]]))
 
     def halves(table):
         table = table.astype(np.float32)
         high = table.astype(jnp.bfloat16)
         return np.stack([high, (table - high.astype(np.float32)).astype(jnp.bfloat16)], axis=1)
 
-    real, full = np.stack(real), np.stack(full)
-    tables = (real, full, real.transpose(0, 2, 1), full.transpose(0, 2, 1))
-    return [jnp.asarray(halves(t)) for t in tables]
+    tables = np.stack(tables)
+    return [jnp.asarray(halves(t)) for t in (tables, tables.transpose(0, 2, 1))]
 
 
 def copy_all(pairs, sems):
@@ -155,7 +157,8 @@
         near = 0 if row < 0 else rows - 1
         across = got_ref[(r + SECTORS // 2) % SECTORS, pl.ds(start + f * rows + near, 1), :]
         per = got_ref.shape[1] // (4 * rows)
-        halo = halo_refs[side][pl.ds((r * per + level) * 4 + f, 1), :]
+        at = pl.ds((r * per + level) * 4 + f, 1)
+        halo = jnp.where(lax.rem(place, 2) == 1, halo_refs[side][at, :], halo_refs[1 - side][at, :])
         return jnp.where(at_pole, signs[f] * across, halo)
 
     for base in range(0, SECTORS, span):
@@ -207,7 +210,10 @@
                 tend_ref[r, part, :] = value[:, i * cols : (i + 1) * cols]
 
 
-def butterfly(rows_at, cols, tend_ref, high_ref, low_ref):
+def butterfly(group, cols, tend_ref, parts_ref):
+    half = parts_ref.shape[0] // 2
+    rows_at = pl.ds(pl.multiple_of(group * 16, 16), 16)
+    low_at = pl.ds(pl.multiple_of(half + group * 16, 16), 16)
     x = [tend_ref[b, rows_at, :] for b in range(SECTORS)]
     s = [x[b] + x[b + 4] for b in range(4)]
     d = [x[b] - x[b + 4] for b in range(4)]
@@ -217,31 +223,27 @@
     parts = (even + odd, even - odd, d[0] + minus, -d[2] - plus, s[0] - s[2], s[3] - s[1], d[0] - minus, d[2] - plus)
     for i, part in enumerate(parts):
         at = slice(i * cols, (i + 1) * cols)
-        high_ref[rows_at, at], low_ref[rows_at, at] = split(part)
-
-
-def product(high, low, table_ref, *index):
-    big, small = table_ref[(*index, 0)], table_ref[(*index, 1)]
-    total = jnp.dot(high, big, preferred_element_type=jnp.float32)
-    total += jnp.dot(low, big, preferred_element_type=jnp.float32)
-    return total + jnp.dot(high, small, preferred_element_type=jnp.float32)
-
-
-def truncate(total, cols, limit, tables, high_ref, low_ref, wave_ref):
-    real_ref, full_ref, real_back_ref, full_back_ref = tables
-    for i, r in enumerate((0, 4, 1, 2, 3)):
-        if i < 2:
-            at, half = slice(i * cols, (i + 1) * cols), REAL_Q
-            ahead, back, place = real_ref, real_back_ref, i
+        parts_ref[rows_at, at], parts_ref[low_at, at] = split(part)
+
+
+def product(parts, table_ref, place):
+    half = parts.shape[0] // 2
+    total = jnp.dot(parts, table_ref[place, 0], preferred_element_type=jnp.float32)
+    small = jnp.dot(parts[:half], table_ref[place, 1], preferred_element_type=jnp.float32)
+    return total[:half] + (total[half:] + small)
+
+
+def truncate(total, cols, limit, ahead_ref, back_ref, parts_ref, wave_ref):
+    lane = lax.broadcasted_iota(jnp.int32, (1, 2 * FULL_Q), 1)
+    for r in range(4):
+        at = slice(2 * r * cols, (2 * r + 2) * cols)
+        spectrum = product(parts_ref[:, at], ahead_ref, r)
+        if r == 0:
+            k = SECTORS * lax.rem(lane, REAL_Q) + jnp.where(lane >= FULL_Q, 4, 0)
         else:
-            at, half = slice((2 * i - 2) * cols, 2 * i * cols), FULL_Q
-            ahead, back, place = full_ref, full_back_ref, i - 2
-        spectrum = product(high_ref[:, at], low_ref[:, at], ahead, place)
-        lane = lax.broadcasted_iota(jnp.int32, (1, 2 * half), 1)
-        q = jnp.where(lane >= half, lane - half, lane) - (0 if i < 2 else SHIFT_Q)
-        k = jnp.abs(SECTORS * q + r)
+            k = jnp.abs(SECTORS * (lax.rem(lane, FULL_Q) - SHIFT_Q) + r)
         factor = jnp.where(k <= limit, jnp.where(k == 0, 1.0 / total, 2.0 / total), 0.0)
-        wave_ref[:, at] = product(*split(spectrum * factor), back, place)
+        wave_ref[:, at] = product(jnp.concatenate(split(spectrum * factor), axis=0), back_ref, r)
 
 
 def update(level, rows, cols, step_size, listed, got_ref, tend_ref, wave_ref, out_ref):
@@ -263,16 +265,18 @@
                 out_ref[b, at, :] = base + step_size * jnp.where(chosen, smooth, tend_ref[b, at, :])
 
 
-def edges_body(per, rows, got_ref, low_ref, high_ref, held_ref, sems):
+def edges_body(per, rows, got_ref, inner_ref, outer_ref, held_ref, sems):
     parts = range(4 * per)
     pairs = [(got_ref.at[:, pl.ds(q * rows, 8), :], held_ref.at[0, q]) for q in parts]
     pairs += [(got_ref.at[:, pl.ds((q + 1) * rows - 8, 8), :], held_ref.at[1, q]) for q in parts]
     copy_all(pairs, sems)
+    odd = lax.rem(lax.axis_index("lat"), 2) == 1
     for r in range(SECTORS):
         for q in parts:
             at = r * 4 * per + q
-            low_ref[at : at + 1, :] = held_ref[0, q, r, 0:1, :]
-            high_ref[at : at + 1, :] = held_ref[1, q, r, 7:8, :]
+            low, high = held_ref[0, q, r, 0:1, :], held_ref[1, q, r, 7:8, :]
+            inner_ref[at : at + 1, :] = jnp.where(odd, low, high)
+            outer_ref[at : at + 1, :] = jnp.where(odd, high, low)
 
 
 def edge_rows(rows, got):
@@ -326,12 +330,11 @@
     )(geo, got)
 
 
-def step_body(per, rows, cols, dlon, dlat, step_size, geo_ref, polar_ref, cutoff_ref, far_ref, tend_ref, south_ref, north_ref, *refs):
-    tables = refs[:4]
-    out_ref, edge_ref, high_ref, low_ref, wave_ref, got_ref, sems = refs[4:]
+def step_body(per, rows, cols, dlon, dlat, step_size, geo_ref, polar_ref, cutoff_ref, far_ref, tend_ref, inner_ref, outer_ref, *refs):
+    ahead_ref, back_ref, out_ref, edge_ref, parts_ref, wave_ref, got_ref, sems = refs
     high = 4 * rows
     arrival = arrivals(per, high, far_ref, got_ref, sems)
-    halos = (south_ref, north_ref)
+    halos = (inner_ref, outer_ref)
     place = lax.axis_index("lat")
     total = rows * lax.axis_size("lat")
     edge = jnp.sum((polar_ref[...] < total // 2).astype(jnp.int32))
@@ -357,35 +360,34 @@
 
     @pl.loop(0, per * high // 16)
     def _(group):
-        butterfly(pl.ds(pl.multiple_of(group * 16, 16), 16), cols, edge_ref, high_ref, low_ref)
-
-    truncate(SECTORS * cols, cols, limit, tables, high_ref, low_ref, wave_ref)
+        butterfly(group, cols, edge_ref, parts_ref)
+
+    truncate(SECTORS * cols, cols, limit, ahead_ref, back_ref, parts_ref, wave_ref)
 
     @pl.loop(0, per)
     def _(level):
         update(level, rows, cols, step_size, listed, got_ref, edge_ref, wave_ref, out_ref)
 
 
-def stepped(rows, dlon, dlat, step_size, geo, polar_rows, cutoffs, got, tend, south, north, tables):
+def stepped(rows, dlon, dlat, step_size, geo, polar_rows, cutoffs, got, tend, inner, outer, tables):
     count, height, cols = got.shape
     inside = pl.BlockSpec(memory_space=pltpu.VMEM)
     full = count * cols
     return pl.pallas_call(
         functools.partial(step_body, height // (4 * rows), rows, cols, dlon, dlat, step_size),
-        in_specs=[inside] * 3 + [pl.BlockSpec(memory_space=pltpu.HBM)] + [inside] * 7,
+        in_specs=[inside] * 3 + [pl.BlockSpec(memory_space=pltpu.HBM)] + [inside] * 5,
         out_specs=inside,
         out_shape=jax.ShapeDtypeStruct(got.shape, jnp.float32),
         scratch_shapes=[
             pltpu.VMEM(got.shape, jnp.float32),
-            pltpu.VMEM((height, full), jnp.bfloat16),
-            pltpu.VMEM((height, full), jnp.bfloat16),
+            pltpu.VMEM((2 * height, full), jnp.bfloat16),
             pltpu.VMEM((height, full), jnp.float32),
             pltpu.VMEM(got.shape, jnp.float32),
             pltpu.SemaphoreType.DMA((height // (4 * rows),)),
         ],
         compiler_params=pltpu.CompilerParams(vmem_limit_bytes=32 * 1024 * 1024),
         cost_estimate=pl.CostEstimate(flops=8 * 1024 * 1024 * height, bytes_accessed=24 * height * full, transcendentals=0),
-    )(geo, polar_rows, cutoffs, got, tend, south, north, *tables)
+    )(geo, polar_rows, cutoffs, got, tend, inner, outer, *tables)
 
 
 def per_device(u_wind, v_wind, thickness, theta, polar_rows, cutoffs):
@@ -403,15 +405,17 @@
     got = lax.all_to_all(pack(count, fields), "lon", 0, 0, tiled=True)
 
     got = pltpu.with_memory_space_constraint(got, pltpu.HBM)
-    low_rows, high_rows = edge_rows(rows, got)
-    south = lax.ppermute(high_rows, "lat", [(i, i + 1) for i in range(lat_count - 1)])
-    north = lax.ppermute(low_rows, "lat", [(i + 1, i) for i in range(lat_count - 1)])
+    inner, outer = edge_rows(rows, got)
+    across = [(i, i + 1) for i in range(1, lat_count - 1, 2)]
+    within = [(i, i + 1) for i in range(0, lat_count, 2)]
+    outer = lax.ppermute(outer, "lat", across + [(j, i) for i, j in across])
+    inner = lax.ppermute(inner, "lat", within + [(j, i) for i, j in within])
 
     geo = jnp.asarray(geometry(total_rows))
     cutoffs = cutoffs.reshape(total_rows // LANES, LANES)
     tables = fourier_tables(total_cols)
     tend = inner_tendencies(rows, dlon, dlat, geo, got)
-    fresh = stepped(rows, dlon, dlat, step_size, geo, polar_rows, cutoffs, got, tend, south, north, tables)
+    fresh = stepped(rows, dlon, dlat, step_size, geo, polar_rows.T, cutoffs, got, tend, inner, outer, tables)
     return tuple(place(lax.all_to_all(fresh, "lon", 0, 0, tiled=True), u_wind.shape))
 
 

time: 154 us -> 151 us (0.981)
  starting transfers between devices: 7.07 us -> 2.83 us
    ppermute x2, starting transfers between devices: 7.07 us -> 2.83 us  [the longest x1 2.74 us: per_device(): outer = lax.ppermute(outer, 'lat', across + [(j, i) for i, j in across])]
  transfers between devices with their start and end apart: 2 -> 2, of which waited for: 0 -> 0; matrix products, arithmetic and copies ran while one was open for 0% -> 0% of each run, Pallas kernels for 3% -> 4%
where the time goes in v7:
time: 151 us; the launch traced here: 150 us
  blocking collectives  120 us (79%)
  Pallas kernels  26.4 us (17%)
  starting transfers between devices  2.83 us (2%)
    all_to_all x1, blocking collectives, per_device(): got = lax.all_to_all(pack(count, fields), 'lon', 0, 0, tiled=True)  60.2 us
    all_to_all x1, blocking collectives, per_device(): lax.all_to_all(fresh, 'lon', 0, 0, tiled=True)  60 us
    pallas_call x1, Pallas kernels, stepped(): pl.pallas_call(functools.partial(step_body, height // (4 * rows), rows, c...  12.9 us
    pallas_call x1, Pallas kernels, inner_tendencies(): pl.pallas_call(functools.partial(inner_body, got.shape[1] // (4 * rows),...  5.26 us
    pallas_call x1, Pallas kernels, pack(): pl.pallas_call(functools.partial(pack_body, count, levels // count, rows)...  3.18 us
  transfers between devices with their start and end apart: 2, of which 0 were waited for; matrix products, arithmetic and copies ran while one was open for 0% of the time, Pallas kernels for 4%

profile of v7, /device:TPU:16, one launch (start us, length us, event | category | flops | bytes accessed | tf_op | source)
XLA Modules:
  0.0 150.2 jit_solution(2724638256524320235)
XLA Ops:
  0.6 3.2 %shard_map.120 = f32[8,384,384]{2,1,0:T(8,128)S(1)} custom-call(f32[24,32,384]{2,1,0:T(8,128)} %refs_0_.2, f32[24,32,384]{2,1,0:T(8,128)} %refs_1_.2, f32[24,32,384]{2,1,0:T(8,128)} %refs_2_.1, f32[24,32,384]{2,1,0:T(8,128)} %refs_3_.1), custom_call_target="tpu_custom_call" | custom-call | bytes 9437184 | tf_op jit(solution)/shard_map/pallas_call | solution.py:91
  3.8 60.2 %all_to_all.10.far_ref.got_ref = f32[8,384,384]{2,1,0:T(8,128)} all-to-all(f32[8,384,384]{2,1,0:T(8,128)S(1)} %shard_map.120), channel_id=1, replica_groups=mesh['lat'=32,'lon'=8] {'lon'}, dimensions={0} | all-to-all | bytes 9437184 | tf_op jit(solution)/shard_map/all_to_all | solution.py:405
  64.1 0.0 copy-start.2
  64.1 2.1 %shard_map.122 = (f32[96,384]{1,0:T(8,128)S(1)}, f32[96,384]{1,0:T(8,128)S(1)}) custom-call(f32[8,384,384]{2,1,0:T(8,128)} %all_to_all.10.far_ref.got_ref), custom_call_target="tpu_custom_call" | custom-call | bytes 589824 | tf_op jit(solution)/shard_map/pallas_call | solution.py:285
  66.1 0.1 collective-permute-start
  66.2 0.0 copy-start.3
  66.3 0.0 copy-start.4
  66.3 2.7 %collective-permute-start.1 = (f32[96,384]{1,0:T(8,128)S(1)}, f32[96,384]{1,0:T(8,128)S(1)}, u32[]{:S(2)}, u32[]{:S(2)}) collective-permute-start(f32[96,384]{1,0:T(8,128)S(1)} %get-tuple-element.7), channel_id=1, source_target_pairs={{8,16},{24,32},{40,48},{56,64},{72,80},{88,96},{104,112},{120,128}... | collective-permute-start | bytes 442376 | tf_op jit(solution)/shard_map/ppermute | solution.py:411
  69.0 0.0 copy-done.2
  69.0 0.0 copy-start
  69.0 0.0 copy-start.1
  69.0 5.3 %shard_map.121.tend_ref = f32[8,192,384]{2,1,0:T(8,128)S(1)} custom-call(f32[1024,8]{1,0:T(8,128)S(1)} %copy-done.2, f32[8,384,384]{2,1,0:T(8,128)} %all_to_all.10.far_ref.got_ref), custom_call_target="tpu_custom_call" | custom-call | flops 47185920 | bytes 7077888 | tf_op jit(solution)/shard_map/pallas_call | solution.py:322
  74.3 0.0 collective-permute-done.inner_ref
  74.3 0.0 collective-permute-done.1.outer_ref
  74.3 0.0 copy-done.3
  74.3 0.0 copy-done.4
  74.4 0.0 copy-done
  74.4 0.0 copy-done.1
  74.4 12.9 %shard_map.123 = f32[8,384,384]{2,1,0:T(8,128)S(1)} custom-call(f32[1024,8]{1,0:T(8,128)S(1)} %copy-done.2, s32[16,32]{1,0:T(8,128)S(1)} %bitcast.2, s32[8,128]{1,0:T(8,128)S(1)} %bitcast.3, f32[8,384,384]{2,1,0:T(8,128)} %all_to_all.10.far_ref.got_ref, f32[8,192,384]{2,1,0:T(8,128)S(1)} %shard_map.121.tend_ref, ...), custom_call_target="tpu_custom_call" | custom-call | flops 3221225472 | bytes 28311552 | tf_op jit(solution)/shard_map/pallas_call | solution.py:376
  87.3 60.0 %all_to_all.11.refs_0_ = f32[8,384,384]{2,1,0:T(8,128)S(1)} all-to-all(f32[8,384,384]{2,1,0:T(8,128)S(1)} %shard_map.123), channel_id=1, replica_groups=mesh['lat'=32,'lon'=8] {'lon'}, dimensions={0} | all-to-all | bytes 9437184 | tf_op jit(solution)/shard_map/all_to_all | solution.py:419
  147.2 3.0 %shard_map.124 = (f32[24,32,384]{2,1,0:T(8,128)}, f32[24,32,384]{2,1,0:T(8,128)}, f32[24,32,384]{2,1,0:T(8,128)}, f32[24,32,384]{2,1,0:T(8,128)}) custom-call(f32[8,384,384]{2,1,0:T(8,128)S(1)} %all_to_all.11.refs_0_), custom_call_target="tpu_custom_call" | custom-call | bytes 9437184 | tf_op jit(solution)/shard_map/pallas_call | solution.py:114
Async XLA Ops:
  64.1 4.9 %copy-start.2 = (f32[1024,8]{1,0:T(8,128)S(1)}, f32[1024,8]{1,0:T(8,128)}, u32[]{:S(2)}) copy-start(f32[1024,8]{1,0:T(8,128)} %constant.6.clone.geo_ref) | copy-start | bytes 98308
  66.1 8.2 %collective-permute-start = (f32[96,384]{1,0:T(8,128)S(1)}, f32[96,384]{1,0:T(8,128)S(1)}, u32[]{:S(2)}, u32[]{:S(2)}) collective-permute-start(f32[96,384]{1,0:T(8,128)S(1)} %get-tuple-element.6), channel_id=1, source_target_pairs={{0,8},{16,24},{32,40},{48,56},{64,72},{80,88},{96,104},{112,120},{... | collective-permute-start | bytes 442376 | tf_op jit(solution)/shard_map/ppermute | solution.py:412
  66.2 8.1 %copy-start.3 = (s32[32,16]{0,1:T(8,128)S(1)}, s32[32,16]{0,1:T(8,128)}, u32[]{:S(2)}) copy-start(s32[32,16]{0,1:T(8,128)} %param.13) | copy-start | bytes 6148
  66.3 8.1 %copy-start.4 = (s32[1024]{0:T(1024)S(1)}, s32[1024]{0:T(1024)}, u32[]{:S(2)}) copy-start(s32[1024]{0:T(1024)} %param.14) | copy-start | bytes 12292
  66.3 8.1 %collective-permute-start.1 = (f32[96,384]{1,0:T(8,128)S(1)}, f32[96,384]{1,0:T(8,128)S(1)}, u32[]{:S(2)}, u32[]{:S(2)}) collective-permute-start(f32[96,384]{1,0:T(8,128)S(1)} %get-tuple-element.7), channel_id=1, source_target_pairs={{8,16},{24,32},{40,48},{56,64},{72,80},{88,96},{104,112},{120,128}... | collective-permute-start | bytes 442376 | tf_op jit(solution)/shard_map/ppermute | solution.py:411
  69.0 5.3 %copy-start = (bf16[4,2,256,768]{3,2,1,0:T(8,128)(2,1)S(1)}, bf16[4,2,256,768]{3,2,1,0:T(8,128)(2,1)}, u32[]{:S(2)}) copy-start(bf16[4,2,256,768]{3,2,1,0:T(8,128)(2,1)} %constant.8.clone.refs_1_) | copy-start | bytes 9437188
  69.0 5.3 %copy-start.1 = (bf16[4,2,768,256]{3,2,1,0:T(8,128)(2,1)S(1)}, bf16[4,2,768,256]{3,2,1,0:T(8,128)(2,1)}, u32[]{:S(2)}) copy-start(bf16[4,2,768,256]{3,2,1,0:T(8,128)(2,1)} %constant.7.clone.refs_0_) | copy-start | bytes 9437188

commit v8 on v7

--- a/solution.py
+++ b/solution.py
@@ -61,7 +61,7 @@
     def halves(table):
         table = table.astype(np.float32)
         high = table.astype(jnp.bfloat16)
-        return np.stack([high, (table - high.astype(np.float32)).astype(jnp.bfloat16)], axis=1)
+        return np.concatenate([high, high, (table - high.astype(np.float32)).astype(jnp.bfloat16)], axis=1)
 
     tables = np.stack(tables)
     return [jnp.asarray(halves(t)) for t in (tables, tables.transpose(0, 2, 1))]
@@ -75,51 +75,43 @@
         copy.wait()
 
 
-def pack_body(count, per, rows, *refs):
+def pack_body(count, per, *refs):
     fields, out, sems = refs[:4], refs[4], refs[5]
-    pairs = []
-    for d in range(count):
-        for k in range(per):
-            for f in range(4):
-                pairs.append((fields[f].at[d * per + k], out.at[d, pl.ds((4 * k + f) * rows, rows), :]))
-    copy_all(pairs, sems)
+    copy_all([(fields[f].at[pl.ds(d * per, per)], out.at[d, :, f]) for d in range(count) for f in range(4)], sems)
 
 
 def pack(count, fields):
     levels, rows, cols = fields[0].shape
-    shape = (count, 4 * (levels // count) * rows, cols)
-    return pl.pallas_call(
-        functools.partial(pack_body, count, levels // count, rows),
+    shape = (count, levels // count, 4, rows, cols)
+    packed = pl.pallas_call(
+        functools.partial(pack_body, count, levels // count),
         in_specs=[pl.BlockSpec(memory_space=pl.ANY)] * 4,
         out_specs=pl.BlockSpec(memory_space=pltpu.VMEM),
         out_shape=pltpu.VMEM(shape, jnp.float32),
-        scratch_shapes=[pltpu.SemaphoreType.DMA((4 * levels,))],
+        scratch_shapes=[pltpu.SemaphoreType.DMA((4 * count,))],
         compiler_params=pltpu.CompilerParams(vmem_limit_bytes=8 * 1024 * 1024),
         cost_estimate=pl.CostEstimate(flops=0, bytes_accessed=8 * math.prod(shape), transcendentals=0),
     )(*[pltpu.with_memory_space_constraint(f, pltpu.HBM) for f in fields])
-
-
-def place_body(count, per, rows, *refs):
+    return packed.reshape(count, 4 * (levels // count) * rows, cols)
+
+
+def place_body(count, per, *refs):
     got, outs, sems = refs[0], refs[1:5], refs[5]
-    pairs = []
-    for d in range(count):
-        for k in range(per):
-            for f in range(4):
-                pairs.append((got.at[d, pl.ds((4 * k + f) * rows, rows), :], outs[f].at[d * per + k]))
-    copy_all(pairs, sems)
+    copy_all([(got.at[d, :, f], outs[f].at[pl.ds(d * per, per)]) for d in range(count) for f in range(4)], sems)
 
 
 def place(got, shape):
     count = got.shape[0]
+    per = shape[0] // count
     return pl.pallas_call(
-        functools.partial(place_body, count, shape[0] // count, shape[1]),
+        functools.partial(place_body, count, per),
         in_specs=[pl.BlockSpec(memory_space=pltpu.VMEM)],
         out_specs=[pl.BlockSpec(memory_space=pl.ANY)] * 4,
         out_shape=[jax.ShapeDtypeStruct(shape, jnp.float32)] * 4,
-        scratch_shapes=[pltpu.SemaphoreType.DMA((4 * shape[0],))],
+        scratch_shapes=[pltpu.SemaphoreType.DMA((4 * count,))],
         compiler_params=pltpu.CompilerParams(vmem_limit_bytes=32 * 1024 * 1024),
         cost_estimate=pl.CostEstimate(flops=0, bytes_accessed=8 * got.size, transcendentals=0),
-    )(got)
+    )(got.reshape(count, per, 4, shape[1], shape[2]))
 
 
 def lat_shift(x, amount, edge):
@@ -211,9 +203,7 @@
 
 
 def butterfly(group, cols, tend_ref, parts_ref):
-    half = parts_ref.shape[0] // 2
     rows_at = pl.ds(pl.multiple_of(group * 16, 16), 16)
-    low_at = pl.ds(pl.multiple_of(half + group * 16, 16), 16)
     x = [tend_ref[b, rows_at, :] for b in range(SECTORS)]
     s = [x[b] + x[b + 4] for b in range(4)]
     d = [x[b] - x[b + 4] for b in range(4)]
@@ -222,28 +212,28 @@
     plus, minus = c * (d[1] + d[3]), c * (d[1] - d[3])
     parts = (even + odd, even - odd, d[0] + minus, -d[2] - plus, s[0] - s[2], s[3] - s[1], d[0] - minus, d[2] - plus)
     for i, part in enumerate(parts):
-        at = slice(i * cols, (i + 1) * cols)
-        parts_ref[rows_at, at], parts_ref[low_at, at] = split(part)
-
-
-def product(parts, table_ref, place):
-    half = parts.shape[0] // 2
-    total = jnp.dot(parts, table_ref[place, 0], preferred_element_type=jnp.float32)
-    small = jnp.dot(parts[:half], table_ref[place, 1], preferred_element_type=jnp.float32)
-    return total[:half] + (total[half:] + small)
+        start = (i // 2 * 4 + i % 2) * cols
+        high, low = split(part)
+        parts_ref[rows_at, start : start + cols] = high
+        parts_ref[rows_at, start + 2 * cols : start + 3 * cols] = low
 
 
 def truncate(total, cols, limit, ahead_ref, back_ref, parts_ref, wave_ref):
     lane = lax.broadcasted_iota(jnp.int32, (1, 2 * FULL_Q), 1)
     for r in range(4):
         at = slice(2 * r * cols, (2 * r + 2) * cols)
-        spectrum = product(parts_ref[:, at], ahead_ref, r)
+        both = slice(4 * r * cols, (4 * r + 4) * cols)
+        high = slice(4 * r * cols, (4 * r + 2) * cols)
+        spectrum = jnp.dot(parts_ref[:, both], ahead_ref[r, : 4 * cols], preferred_element_type=jnp.float32)
+        spectrum += jnp.dot(parts_ref[:, high], ahead_ref[r, 4 * cols :], preferred_element_type=jnp.float32)
         if r == 0:
             k = SECTORS * lax.rem(lane, REAL_Q) + jnp.where(lane >= FULL_Q, 4, 0)
         else:
             k = jnp.abs(SECTORS * (lax.rem(lane, FULL_Q) - SHIFT_Q) + r)
         factor = jnp.where(k <= limit, jnp.where(k == 0, 1.0 / total, 2.0 / total), 0.0)
-        wave_ref[:, at] = product(jnp.concatenate(split(spectrum * factor), axis=0), back_ref, r)
+        high, low = split(spectrum * factor)
+        both = jnp.concatenate([high, low, high], axis=1)
+        wave_ref[:, at] = jnp.dot(both, back_ref[r], preferred_element_type=jnp.float32)
 
 
 def update(level, rows, cols, step_size, listed, got_ref, tend_ref, wave_ref, out_ref):
@@ -380,7 +370,7 @@
         out_shape=jax.ShapeDtypeStruct(got.shape, jnp.float32),
         scratch_shapes=[
             pltpu.VMEM(got.shape, jnp.float32),
-            pltpu.VMEM((2 * height, full), jnp.bfloat16),
+            pltpu.VMEM((height, 2 * full), jnp.bfloat16),
             pltpu.VMEM((height, full), jnp.float32),
             pltpu.VMEM(got.shape, jnp.float32),
             pltpu.SemaphoreType.DMA((height // (4 * rows),)),

time: 151 us -> 151 us (level)
  transfers between devices with their start and end apart: 2 -> 2, of which waited for: 0 -> 1; matrix products, arithmetic and copies ran while one was open for 0% -> 0% of each run, Pallas kernels for 4% -> 3%
where the time goes in v8:
time: 151 us; the launch traced here: 149 us
  blocking collectives  120 us (79%)
  Pallas kernels  25.2 us (17%)
  starting transfers between devices  2.82 us (2%)
    all_to_all x1, blocking collectives, per_device(): got = lax.all_to_all(pack(count, fields), 'lon', 0, 0, tiled=True)  60.5 us
    all_to_all x1, blocking collectives, per_device(): lax.all_to_all(fresh, 'lon', 0, 0, tiled=True)  59.6 us
    pallas_call x1, Pallas kernels, stepped(): pl.pallas_call(functools.partial(step_body, height // (4 * rows), rows, c...  12.8 us
    pallas_call x1, Pallas kernels, inner_tendencies(): pl.pallas_call(functools.partial(inner_body, got.shape[1] // (4 * rows),...  5.11 us
  transfers between devices with their start and end apart: 2, of which 1 were waited for; matrix products, arithmetic and copies ran while one was open for 0% of the time, Pallas kernels for 3%

profile of v8, /device:TPU:16, one launch (start us, length us, event | category | flops | bytes accessed | tf_op | source)
XLA Modules:
  0.0 149.2 jit_solution(4592340625187501454)
XLA Ops:
  0.6 2.7 %shard_map.120 = f32[8,3,4,32,384]{4,3,2,1,0:T(8,128)S(1)} custom-call(f32[24,32,384]{2,1,0:T(8,128)} %refs_0_.2, f32[24,32,384]{2,1,0:T(8,128)} %refs_1_.2, f32[24,32,384]{2,1,0:T(8,128)} %refs_2_.1, f32[24,32,384]{2,1,0:T(8,128)} %refs_3_.1), custom_call_target="tpu_custom_call" | custom-call | bytes 9437184 | tf_op jit(solution)/shard_map/pallas_call | solution.py:86
  3.3 0.0 copy-start
  3.3 0.0 slice-start.2
  3.4 60.5 %all_to_all.10.far_ref.got_ref = f32[8,384,384]{2,1,0:T(8,128)} all-to-all(f32[8,384,384]{2,1,0:T(8,128)S(1)} %bitcast.5), channel_id=1, replica_groups=mesh['lat'=32,'lon'=8] {'lon'}, dimensions={0} | all-to-all | bytes 9437184 | tf_op jit(solution)/shard_map/all_to_all | solution.py:395
  63.9 0.0 slice-start
  63.9 2.2 %shard_map.122 = (f32[96,384]{1,0:T(8,128)S(1)}, f32[96,384]{1,0:T(8,128)S(1)}) custom-call(f32[8,384,384]{2,1,0:T(8,128)} %all_to_all.10.far_ref.got_ref), custom_call_target="tpu_custom_call" | custom-call | bytes 589824 | tf_op jit(solution)/shard_map/pallas_call | solution.py:275
  66.0 0.1 collective-permute-start
  66.1 0.0 slice-start.1
  66.1 0.0 copy-start.1
  66.2 0.0 copy-start.2
  66.2 2.7 %collective-permute-start.1 = (f32[96,384]{1,0:T(8,128)S(1)}, f32[96,384]{1,0:T(8,128)S(1)}, u32[]{:S(2)}, u32[]{:S(2)}) collective-permute-start(f32[96,384]{1,0:T(8,128)S(1)} %get-tuple-element.7), channel_id=1, source_target_pairs={{8,16},{24,32},{40,48},{56,64},{72,80},{88,96},{104,112},{120,128}... | collective-permute-start | bytes 442376 | tf_op jit(solution)/shard_map/ppermute | solution.py:401
  68.9 0.0 copy-done
  68.9 5.1 %shard_map.121.tend_ref = f32[8,192,384]{2,1,0:T(8,128)S(1)} custom-call(f32[1024,8]{1,0:T(8,128)S(1)} %copy-done, f32[8,384,384]{2,1,0:T(8,128)} %all_to_all.10.far_ref.got_ref), custom_call_target="tpu_custom_call" | custom-call | flops 47185920 | bytes 7077888 | tf_op jit(solution)/shard_map/pallas_call | solution.py:312
  74.0 0.0 collective-permute-done.inner_ref
  74.0 0.2 collective-permute-done.1.outer_ref
  74.3 0.0 slice-done.2
  74.3 0.0 slice-done
  74.3 0.0 slice-done.3
  74.3 0.0 slice-done.1
  74.3 0.0 copy-done.1
  74.3 0.0 copy-done.2
  74.3 12.8 %shard_map.123 = f32[8,384,384]{2,1,0:T(8,128)S(1)} custom-call(f32[1024,8]{1,0:T(8,128)S(1)} %copy-done, s32[16,32]{1,0:T(8,128)S(1)} %bitcast.10, s32[8,128]{1,0:T(8,128)S(1)} %bitcast.11, f32[8,384,384]{2,1,0:T(8,128)} %all_to_all.10.far_ref.got_ref, f32[8,192,384]{2,1,0:T(8,128)S(1)} %shard_map.121.tend_ref, ...), custom_call_target="tpu_custom_call" | custom-call | flops 3221225472 | bytes 28311552 | tf_op jit(solution)/shard_map/pallas_call | solution.py:366
  87.2 59.6 %all_to_all.11 = f32[8,384,384]{2,1,0:T(8,128)S(1)} all-to-all(f32[8,384,384]{2,1,0:T(8,128)S(1)} %shard_map.123), channel_id=1, replica_groups=mesh['lat'=32,'lon'=8] {'lon'}, dimensions={0} | all-to-all | bytes 9437184 | tf_op jit(solution)/shard_map/all_to_all | solution.py:409
  146.8 2.4 %shard_map.124 = (f32[24,32,384]{2,1,0:T(8,128)}, f32[24,32,384]{2,1,0:T(8,128)}, f32[24,32,384]{2,1,0:T(8,128)}, f32[24,32,384]{2,1,0:T(8,128)}) custom-call(f32[8,3,4,32,384]{4,3,2,1,0:T(8,128)S(1)} %bitcast.4), custom_call_target="tpu_custom_call" | custom-call | bytes 9437184 | tf_op jit(solution)/shard_map/pallas_call | solution.py:106
  (3 shorter events, 0.0 us)
Async XLA Ops:
  3.3 65.6 %copy-start = (f32[1024,8]{1,0:T(8,128)S(1)}, f32[1024,8]{1,0:T(8,128)}, u32[]{:S(2)}) copy-start(f32[1024,8]{1,0:T(8,128)} %constant.6.clone.geo_ref) | copy-start | bytes 98308
  3.3 70.9 %slice-start.2 = ((s8[4718592]{0:T(1024)(128)(4,1)}), s8[4194304]{0:T(1024)(128)(4,1)S(1)}, s32[]{:S(2)}) async-start(s8[4718592]{0:T(1024)(128)(4,1)} %bitcast.8), calls=%async_computation.4 | async-start | bytes 8388608
  63.9 10.4 %slice-start = ((s8[4718592]{0:T(1024)(128)(4,1)}), s8[4194304]{0:T(1024)(128)(4,1)S(1)}, s32[]{:S(2)}) async-start(s8[4718592]{0:T(1024)(128)(4,1)} %bitcast.6), calls=%async_computation.2 | async-start | bytes 8388608
  63.9 10.4 %slice-start.3 = ((s8[4718592]{0:T(1024)(128)(4,1)}), s8[524288]{0:T(1024)(128)(4,1)S(1)}, s32[]{:S(2)}) async-start(s8[4718592]{0:T(1024)(128)(4,1)} %bitcast.8), calls=%async_computation.5 | async-start | bytes 1048576
  66.0 8.0 %collective-permute-start = (f32[96,384]{1,0:T(8,128)S(1)}, f32[96,384]{1,0:T(8,128)S(1)}, u32[]{:S(2)}, u32[]{:S(2)}) collective-permute-start(f32[96,384]{1,0:T(8,128)S(1)} %get-tuple-element.6), channel_id=1, source_target_pairs={{0,8},{16,24},{32,40},{48,56},{64,72},{80,88},{96,104},{112,120},{... | collective-permute-start | bytes 442376 | tf_op jit(solution)/shard_map/ppermute | solution.py:402
  66.1 8.2 %slice-start.1 = ((s8[4718592]{0:T(1024)(128)(4,1)}), s8[524288]{0:T(1024)(128)(4,1)S(1)}, s32[]{:S(2)}) async-start(s8[4718592]{0:T(1024)(128)(4,1)} %bitcast.6), calls=%async_computation.3 | async-start | bytes 1048576
  66.1 8.2 %copy-start.1 = (s32[32,16]{0,1:T(8,128)S(1)}, s32[32,16]{0,1:T(8,128)}, u32[]{:S(2)}) copy-start(s32[32,16]{0,1:T(8,128)} %param.13) | copy-start | bytes 6148
  66.2 8.2 %copy-start.2 = (s32[1024]{0:T(1024)S(1)}, s32[1024]{0:T(1024)}, u32[]{:S(2)}) copy-start(s32[1024]{0:T(1024)} %param.14) | copy-start | bytes 12292
  66.2 8.1 %collective-permute-start.1 = (f32[96,384]{1,0:T(8,128)S(1)}, f32[96,384]{1,0:T(8,128)S(1)}, u32[]{:S(2)}, u32[]{:S(2)}) collective-permute-start(f32[96,384]{1,0:T(8,128)S(1)} %get-tuple-element.7), channel_id=1, source_target_pairs={{8,16},{24,32},{40,48},{56,64},{72,80},{88,96},{104,112},{120,128}... | collective-permute-start | bytes 442376 | tf_op jit(solution)/shard_map/ppermute | solution.py:401

commit v9 on v8

--- a/solution.py
+++ b/solution.py
@@ -202,9 +202,14 @@
                 tend_ref[r, part, :] = value[:, i * cols : (i + 1) * cols]
 
 
-def butterfly(group, cols, tend_ref, parts_ref):
-    rows_at = pl.ds(pl.multiple_of(group * 16, 16), 16)
-    x = [tend_ref[b, rows_at, :] for b in range(SECTORS)]
+def butterfly(part, side, rows, cols, edge_ref, inner_ref, parts_ref):
+    rows_at = pl.ds(pl.multiple_of(part * rows + side * 16, 16), 16)
+    edge_at = pl.ds(pl.multiple_of(part * rows + side * (rows - 8), 8), 8)
+    inner_at = pl.ds(pl.multiple_of(part * (rows - 16) + side * 8, 8), 8)
+    x = []
+    for b in range(SECTORS):
+        pair = [edge_ref[b, edge_at, :], inner_ref[b, inner_at, :]]
+        x.append(jnp.concatenate(pair[::-1] if side else pair, axis=0))
     s = [x[b] + x[b + 4] for b in range(4)]
     d = [x[b] - x[b + 4] for b in range(4)]
     c = math.sqrt(0.5)
@@ -236,7 +241,7 @@
         wave_ref[:, at] = jnp.dot(both, back_ref[r], preferred_element_type=jnp.float32)
 
 
-def update(level, rows, cols, step_size, listed, got_ref, tend_ref, wave_ref, out_ref):
+def update(level, rows, cols, step_size, listed, got_ref, edge_ref, inner_ref, wave_ref, out_ref):
     c = math.sqrt(0.5)
     high = 4 * rows
     for f in range(4):
@@ -247,12 +252,17 @@
             even = (near + a2, far - b2, near - a2, far + b2)
             odd = (a1 + a3, c * ((a1 - b1) - (a3 + b3)), b3 - b1, c * ((a3 - b3) - (a1 + b1)))
             chosen = listed[j : j + 8, :]
+            if 0 < j < rows - 8:
+                tend_ref = inner_ref
+                tend_at = pl.ds(pl.multiple_of((level * 4 + f) * (rows - 16) + j - 8, 8), 8)
+            else:
+                tend_ref, tend_at = edge_ref, at
             for b in range(SECTORS):
                 smooth = even[b % 4] + odd[b % 4] if b < 4 else even[b % 4] - odd[b % 4]
                 base = got_ref[b, at, :]
                 if f == 3:
                     base = base * got_ref[b, pl.ds(pl.multiple_of(level * high + 2 * rows + j, 8), 8), :]
-                out_ref[b, at, :] = base + step_size * jnp.where(chosen, smooth, tend_ref[b, at, :])
+                out_ref[b, at, :] = base + step_size * jnp.where(chosen, smooth, tend_ref[b, tend_at, :])
 
 
 def edges_body(per, rows, got_ref, inner_ref, outer_ref, held_ref, sems):
@@ -304,7 +314,7 @@
     def _(level):
         arrival(level).wait()
         for first in range(8, rows - 8, 8):
-            group_tendencies(level, first, 8, 2, rows, cols, dlon, dlat, place, geo_ref, got_ref, None, tend_ref, 8)
+            group_tendencies(level, first, 8, 4, rows, cols, dlon, dlat, place, geo_ref, got_ref, None, tend_ref, 8)
 
 
 def inner_tendencies(rows, dlon, dlat, geo, got):
@@ -341,22 +351,18 @@
     def _(level):
         arrival(level).wait()
         for first in (0, rows - 8):
-            group_tendencies(level, first, 8, 2, rows, cols, dlon, dlat, place, geo_ref, got_ref, halos, edge_ref)
-        for f in range(4):
-            part = pl.ds(pl.multiple_of(level * high + f * rows + 8, 8), rows - 16)
-            kept = pl.ds(pl.multiple_of((level * 4 + f) * (rows - 16), 8), rows - 16)
-            for r in range(SECTORS):
-                edge_ref[r, part, :] = tend_ref[r, kept, :]
-
-    @pl.loop(0, per * high // 16)
-    def _(group):
-        butterfly(group, cols, edge_ref, parts_ref)
+            group_tendencies(level, first, 8, 4, rows, cols, dlon, dlat, place, geo_ref, got_ref, halos, edge_ref)
+
+    @pl.loop(0, 4 * per)
+    def _(part):
+        for side in (0, 1):
+            butterfly(part, side, rows, cols, edge_ref, tend_ref, parts_ref)
 
     truncate(SECTORS * cols, cols, limit, ahead_ref, back_ref, parts_ref, wave_ref)
 
     @pl.loop(0, per)
     def _(level):
-        update(level, rows, cols, step_size, listed, got_ref, edge_ref, wave_ref, out_ref)
+        update(level, rows, cols, step_size, listed, got_ref, edge_ref, tend_ref, wave_ref, out_ref)
 
 
 def stepped(rows, dlon, dlat, step_size, geo, polar_rows, cutoffs, got, tend, inner, outer, tables):

time: 151 us -> 150 us (level)
  no operation moved by 1% of the time
where the time goes in v9:
time: 150 us; the launch traced here: 148 us
  blocking collectives  120 us (80%)
  Pallas kernels  24.5 us (16%)
  starting transfers between devices  2.82 us (2%)
    all_to_all x1, blocking collectives, per_device(): got = lax.all_to_all(pack(count, fields), 'lon', 0, 0, tiled=True)  60.5 us
    all_to_all x1, blocking collectives, per_device(): lax.all_to_all(fresh, 'lon', 0, 0, tiled=True)  59.2 us
    pallas_call x1, Pallas kernels, stepped(): pl.pallas_call(functools.partial(step_body, height // (4 * rows), rows, c...  12.4 us
    pallas_call x1, Pallas kernels, inner_tendencies(): pl.pallas_call(functools.partial(inner_body, got.shape[1] // (4 * rows),...  4.73 us
  transfers between devices with their start and end apart: 2, of which 1 were waited for; matrix products, arithmetic and copies ran while one was open for 0% of the time, Pallas kernels for 3%

profile of v9, /device:TPU:16, one launch (start us, length us, event | category | flops | bytes accessed | tf_op | source)
XLA Modules:
  0.0 148.4 jit_solution(7694564031798217178)
XLA Ops:
  0.6 2.7 %shard_map.120 = f32[8,3,4,32,384]{4,3,2,1,0:T(8,128)S(1)} custom-call(f32[24,32,384]{2,1,0:T(8,128)} %refs_0_.2, f32[24,32,384]{2,1,0:T(8,128)} %refs_1_.2, f32[24,32,384]{2,1,0:T(8,128)} %refs_2_.1, f32[24,32,384]{2,1,0:T(8,128)} %refs_3_.1), custom_call_target="tpu_custom_call" | custom-call | bytes 9437184 | tf_op jit(solution)/shard_map/pallas_call | solution.py:86
  3.3 0.0 copy-start
  3.3 0.0 slice-start.2
  3.4 60.5 %all_to_all.10.far_ref.got_ref = f32[8,384,384]{2,1,0:T(8,128)} all-to-all(f32[8,384,384]{2,1,0:T(8,128)S(1)} %bitcast.5), channel_id=1, replica_groups=mesh['lat'=32,'lon'=8] {'lon'}, dimensions={0} | all-to-all | bytes 9437184 | tf_op jit(solution)/shard_map/all_to_all | solution.py:401
  63.9 0.0 slice-start.3
  63.9 2.2 %shard_map.122 = (f32[96,384]{1,0:T(8,128)S(1)}, f32[96,384]{1,0:T(8,128)S(1)}) custom-call(f32[8,384,384]{2,1,0:T(8,128)} %all_to_all.10.far_ref.got_ref), custom_call_target="tpu_custom_call" | custom-call | bytes 589824 | tf_op jit(solution)/shard_map/pallas_call | solution.py:285
  66.0 0.1 collective-permute-start
  66.1 0.0 slice-start.1
  66.1 0.0 copy-start.1
  66.2 0.0 copy-start.2
  66.2 2.7 %collective-permute-start.1 = (f32[96,384]{1,0:T(8,128)S(1)}, f32[96,384]{1,0:T(8,128)S(1)}, u32[]{:S(2)}, u32[]{:S(2)}) collective-permute-start(f32[96,384]{1,0:T(8,128)S(1)} %get-tuple-element.7), channel_id=1, source_target_pairs={{8,16},{24,32},{40,48},{56,64},{72,80},{88,96},{104,112},{120,128}... | collective-permute-start | bytes 442376 | tf_op jit(solution)/shard_map/ppermute | solution.py:407
  68.9 0.0 copy-done
  68.9 4.7 %shard_map.121.tend_ref = f32[8,192,384]{2,1,0:T(8,128)S(1)} custom-call(f32[1024,8]{1,0:T(8,128)S(1)} %copy-done, f32[8,384,384]{2,1,0:T(8,128)} %all_to_all.10.far_ref.got_ref), custom_call_target="tpu_custom_call" | custom-call | flops 47185920 | bytes 7077888 | tf_op jit(solution)/shard_map/pallas_call | solution.py:322
  73.7 0.0 collective-permute-done.inner_ref
  73.7 0.6 collective-permute-done.1.outer_ref
  74.3 0.0 slice-done.2
  74.3 0.0 slice-done
  74.3 0.0 slice-done.3
  74.3 0.0 slice-done.1
  74.3 0.0 copy-done.1
  74.3 0.0 copy-done.2
  74.3 12.4 %shard_map.123 = f32[8,384,384]{2,1,0:T(8,128)S(1)} custom-call(f32[1024,8]{1,0:T(8,128)S(1)} %copy-done, s32[16,32]{1,0:T(8,128)S(1)} %bitcast.10, s32[8,128]{1,0:T(8,128)S(1)} %bitcast.11, f32[8,384,384]{2,1,0:T(8,128)} %all_to_all.10.far_ref.got_ref, f32[8,192,384]{2,1,0:T(8,128)S(1)} %shard_map.121.tend_ref, ...), custom_call_target="tpu_custom_call" | custom-call | flops 3221225472 | bytes 28311552 | tf_op jit(solution)/shard_map/pallas_call | solution.py:372
  86.8 59.2 %all_to_all.11 = f32[8,384,384]{2,1,0:T(8,128)S(1)} all-to-all(f32[8,384,384]{2,1,0:T(8,128)S(1)} %shard_map.123), channel_id=1, replica_groups=mesh['lat'=32,'lon'=8] {'lon'}, dimensions={0} | all-to-all | bytes 9437184 | tf_op jit(solution)/shard_map/all_to_all | solution.py:415
  146.0 2.4 %shard_map.124 = (f32[24,32,384]{2,1,0:T(8,128)}, f32[24,32,384]{2,1,0:T(8,128)}, f32[24,32,384]{2,1,0:T(8,128)}, f32[24,32,384]{2,1,0:T(8,128)}) custom-call(f32[8,3,4,32,384]{4,3,2,1,0:T(8,128)S(1)} %bitcast.4), custom_call_target="tpu_custom_call" | custom-call | bytes 9437184 | tf_op jit(solution)/shard_map/pallas_call | solution.py:106
  (3 shorter events, 0.0 us)
Async XLA Ops:
  3.3 65.6 %copy-start = (f32[1024,8]{1,0:T(8,128)S(1)}, f32[1024,8]{1,0:T(8,128)}, u32[]{:S(2)}) copy-start(f32[1024,8]{1,0:T(8,128)} %constant.6.clone.geo_ref) | copy-start | bytes 98308
  3.3 70.9 %slice-start.2 = ((s8[4718592]{0:T(1024)(128)(4,1)}), s8[4194304]{0:T(1024)(128)(4,1)S(1)}, s32[]{:S(2)}) async-start(s8[4718592]{0:T(1024)(128)(4,1)} %bitcast.8), calls=%async_computation.4 | async-start | bytes 8388608
  63.9 10.4 %slice-start = ((s8[4718592]{0:T(1024)(128)(4,1)}), s8[4194304]{0:T(1024)(128)(4,1)S(1)}, s32[]{:S(2)}) async-start(s8[4718592]{0:T(1024)(128)(4,1)} %bitcast.6), calls=%async_computation.2 | async-start | bytes 8388608
  63.9 10.4 %slice-start.3 = ((s8[4718592]{0:T(1024)(128)(4,1)}), s8[524288]{0:T(1024)(128)(4,1)S(1)}, s32[]{:S(2)}) async-start(s8[4718592]{0:T(1024)(128)(4,1)} %bitcast.8), calls=%async_computation.5 | async-start | bytes 1048576
  66.0 7.6 %collective-permute-start = (f32[96,384]{1,0:T(8,128)S(1)}, f32[96,384]{1,0:T(8,128)S(1)}, u32[]{:S(2)}, u32[]{:S(2)}) collective-permute-start(f32[96,384]{1,0:T(8,128)S(1)} %get-tuple-element.6), channel_id=1, source_target_pairs={{0,8},{16,24},{32,40},{48,56},{64,72},{80,88},{96,104},{112,120},{... | collective-permute-start | bytes 442376 | tf_op jit(solution)/shard_map/ppermute | solution.py:408
  66.1 8.2 %slice-start.1 = ((s8[4718592]{0:T(1024)(128)(4,1)}), s8[524288]{0:T(1024)(128)(4,1)S(1)}, s32[]{:S(2)}) async-start(s8[4718592]{0:T(1024)(128)(4,1)} %bitcast.6), calls=%async_computation.3 | async-start | bytes 1048576
  66.1 8.2 %copy-start.1 = (s32[32,16]{0,1:T(8,128)S(1)}, s32[32,16]{0,1:T(8,128)}, u32[]{:S(2)}) copy-start(s32[32,16]{0,1:T(8,128)} %param.13) | copy-start | bytes 6148
  66.2 8.2 %copy-start.2 = (s32[1024]{0:T(1024)S(1)}, s32[1024]{0:T(1024)}, u32[]{:S(2)}) copy-start(s32[1024]{0:T(1024)} %param.14) | copy-start | bytes 12292
  66.2 8.1 %collective-permute-start.1 = (f32[96,384]{1,0:T(8,128)S(1)}, f32[96,384]{1,0:T(8,128)S(1)}, u32[]{:S(2)}, u32[]{:S(2)}) collective-permute-start(f32[96,384]{1,0:T(8,128)S(1)} %get-tuple-element.7), channel_id=1, source_target_pairs={{8,16},{24,32},{40,48},{56,64},{72,80},{88,96},{104,112},{120,128}... | collective-permute-start | bytes 442376 | tf_op jit(solution)/shard_map/ppermute | solution.py:407
